TPU v7x, 256 devices: a whole 4x4x8 slice. The times are simulated.
256 devices in a mesh: lsec: 8 (over x, y_hi), rsec: 32 (over z, y_lo, core).
Axes of the slice: x: 4, y: 4 (y_hi: 2, y_lo: 2; y = y_hi * 2 + y_lo), z: 8, core: 2. Of those that a mesh axis runs over, the one named last changes fastest.
Arguments:
- psi: bfloat16 [32, 64, 256, 256], P('lsec', 'rsec'), may hold values from -6 to 6
- left_env: bfloat16 [32, 4, 256, 256], P('lsec'), may hold values from -0.375 to 0.375
- right_env: bfloat16 [64, 4, 256, 256], P('rsec'), may hold values from -0.1875 to 0.1875
- energies: float32 [32, 64], P('lsec', 'rsec'), may hold values from 0.5 to 3
- coef_num: int32 [2], replicated, may hold values from 3 to 9
- coef_den: int32 [2], replicated, may hold values from 4 to 8
Outputs:
- vector_out: bfloat16 [32, 64, 256, 256], P('lsec', 'rsec')
- ritz: float32 [3], replicated
All inputs are finite; a program needn't handle non-finite values.
Results may differ from a plain program's by a relative error of at most 0.015.
Values may be sent and summed in bfloat16 or wider, within the bound.
No kernel may reach another device: no remote copies, remote signals or barrier semaphores. Data moves between devices by JAX's collectives and lax.ppermute only.
A program may use at most 64 MiB of HBM per device.

v0:
```python
import jax
import jax.numpy as jnp
from jax import lax
from jax.sharding import PartitionSpec as P

DIAG = 2
HOPS = 1
ITERS = 3


eps = 1e-06


def padded(block, sides, width):
    for axis, dim in sides:
        count = lax.axis_size(axis)
        forward = [(i, i + 1) for i in range(count - 1)]
        backward = [(target, source) for source, target in forward]
        low = lax.ppermute(
            lax.slice_in_dim(block, block.shape[dim] - width, None, axis=dim), axis, forward
        )
        high = lax.ppermute(lax.slice_in_dim(block, 0, width, axis=dim), axis, backward)
        block = jnp.concatenate([low, block, high], axis=dim)
    return block


def add_terms(left_env, right_env, source, first, number, total):
    for term in range(first, first + number):
        inner = jnp.einsum(
            "aij,abjk->abik", left_env[:, term], source, preferred_element_type=jnp.float32
        ).astype(jnp.bfloat16)
        total = total + jnp.einsum(
            "abik,blk->abil", inner, right_env[:, term], preferred_element_type=jnp.float32
        )
    return total


def with_rims(vec):
    wide = padded(vec, (("rsec", 1),), 1)
    full = padded(wide, (("lsec", 0),), 1)
    return full


def matvec(vec, left_env, right_env, energies):
    vals = vec.astype(jnp.float32)
    total = energies[:, :, None, None] * vals
    total = add_terms(left_env, right_env, vec, 0, DIAG, total)
    full = with_rims(vec)
    plus_blocks = full[:-2, 2:]
    minus_blocks = full[2:, :-2]
    total = add_terms(left_env, right_env, plus_blocks, DIAG, HOPS, total)
    total = add_terms(left_env, right_env, minus_blocks, DIAG + HOPS, HOPS, total)
    return total


def per_device(psi, left_env, right_env, energies, coef_num, coef_den):
    count = 1.0 / float(psi.size * lax.axis_size("lsec") * lax.axis_size("rsec"))
    start_vals = psi.astype(jnp.float32)
    start = lax.psum(jnp.sum(start_vals * start_vals), ("lsec", "rsec")) * count
    vec = (start_vals * lax.rsqrt(start + eps)).astype(jnp.bfloat16)
    previous = jnp.zeros(psi.shape, jnp.float32)
    thetas = []
    for step in range(ITERS):
        sigma = matvec(vec, left_env, right_env, energies)
        vals = vec.astype(jnp.float32)
        if step == 0:
            coef = jnp.float32(0.0)
        else:
            coef = coef_num[step - 1].astype(jnp.float32) / coef_den[step - 1].astype(jnp.float32)
        theta = lax.psum(jnp.sum(vals * sigma), ("lsec", "rsec")) * count
        resid = sigma - theta * vals - coef * previous
        norm_sq = lax.psum(jnp.sum(resid * resid), ("lsec", "rsec")) * count
        thetas.append(theta)
        previous = vals
        vec = (resid * lax.rsqrt(norm_sq + eps)).astype(jnp.bfloat16)
    return (vec, jnp.stack(thetas))


def solution(mesh):
    in_specs = (
        P("lsec", "rsec", None, None),
        P("lsec", None, None, None),
        P("rsec", None, None, None),
        P("lsec", "rsec"),
        P(),
        P(),
    )
    out_specs = (P("lsec", "rsec", None, None), P())
    return jax.shard_map(
        per_device, mesh=mesh, in_specs=in_specs, out_specs=out_specs, check_vma=False
    )
```

profile of v0, /device:TPU:1, one launch (start us, length us, event | category | flops | bytes accessed | tf_op | source)
XLA Modules:
  0.0 713.3 jit_solution(7295831636663205488)
XLA Ops:
  0.6 2.4 fusion
  3.0 81.4 %psum.49 = f32[]{:T(128)} all-reduce(f32[]{:T(128)} %fusion), channel_id=1, replica_groups=mesh['lsec'=8,'rsec'=32] {'lsec','rsec'}, use_global_device_ids=true, to_apply=%region_1.0 | all-reduce | flops 1 | bytes 8 | tf_op jit(solution)/shard_map/psum | solution.py:59
  85.1 1.4 fusion.1
  86.5 0.1 fusion.141
  86.6 0.0 copy-start.1
  86.6 2.1 collective-permute-start
  88.6 2.4 collective-permute-start.1
  91.1 3.7 collective-permute-done
  94.7 4.4 collective-permute-done.1
  99.1 1.1 pad_maximum_fusion.60
  100.3 7.0 collective-permute-start.2
  107.3 3.0 fusion.23
  110.2 1.3 collective-permute-start.3
  111.5 3.0 fusion.25
  114.6 3.1 collective-permute-done.2
  117.7 3.2 fusion.27
  120.8 1.1 collective-permute-done.3
  122.0 6.4 fusion.13
  128.3 85.9 %psum.50 = f32[]{:T(128)} all-reduce(f32[]{:T(128)} %get-tuple-element.20), channel_id=1, replica_groups=mesh['lsec'=8,'rsec'=32] {'lsec','rsec'}, use_global_device_ids=true, to_apply=%region_3.0 | all-reduce | flops 1 | bytes 8 | tf_op jit(solution)/shard_map/psum | solution.py:70
  214.9 2.7 multiply_reduce_fusion.2
  217.6 73.4 %psum.51 = f32[]{:T(128)} all-reduce(f32[]{:T(128)} %multiply_reduce_fusion.2), channel_id=1, replica_groups=mesh['lsec'=8,'rsec'=32] {'lsec','rsec'}, use_global_device_ids=true, to_apply=%region_5.0 | all-reduce | flops 1 | bytes 8 | tf_op jit(solution)/shard_map/psum | solution.py:72
  291.7 2.0 multiply_convert_fusion.2
  293.7 0.0 copy-start.11
  293.7 0.0 copy-start.12
  293.7 0.1 fusion.140
  293.8 0.0 copy-start.2
  293.8 3.5 collective-permute-start.4
  297.3 1.9 collective-permute-start.5
  299.3 0.6 fusion.143
  300.5 0.6 fusion.142
  301.8 1.6 collective-permute-done.4
  303.4 4.4 collective-permute-done.5
  307.8 1.1 pad_maximum_fusion.57
  309.0 7.2 %collective-permute-start.6 = (bf16[1,4,256,256]{3,2,0,1:T(8,128)(2,1)}, bf16[1,4,256,256]{3,2,0,1:T(8,128)(2,1)}, u32[]{:S(2)}, u32[]{:S(2)}) collective-permute-start(bf16[1,4,256,256]{3,2,0,1:T(8,128)(2,1)} %get-tuple-element.7), channel_id=1, source_target_pairs={{0,32},{32,64},{64,96},{96,128},{128,160},{160,192},{192,224},{1,3... | collective-permute-start | bytes 1572872 | tf_op jit(solution)/shard_map/ppermute | solution.py:19
  316.1 3.0 fusion.30
  319.2 1.3 collective-permute-start.7
  320.5 3.1 fusion.32
  323.6 8.4 %collective-permute-done.6 = bf16[1,4,256,256]{3,2,0,1:T(8,128)(2,1)} collective-permute-done((bf16[1,4,256,256]{3,2,0,1:T(8,128)(2,1)}, bf16[1,4,256,256]{3,2,0,1:T(8,128)(2,1)}, u32[]{:S(2)}, u32[]{:S(2)}) %collective-permute-start.6) | collective-permute-done | bytes 524320 | tf_op jit(solution)/shard_map/ppermute | solution.py:19
  332.0 3.3 fusion.34
  335.3 6.3 fusion.20
  341.6 82.0 %psum.52 = f32[]{:T(128)} all-reduce(f32[]{:T(128)} %get-tuple-element.22), channel_id=1, replica_groups=mesh['lsec'=8,'rsec'=32] {'lsec','rsec'}, use_global_device_ids=true, to_apply=%region_7.0 | all-reduce | flops 1 | bytes 8 | tf_op jit(solution)/shard_map/psum | solution.py:70
  424.2 2.8 multiply_reduce_fusion.1
  427.0 73.4 %psum.53 = f32[]{:T(128)} all-reduce(f32[]{:T(128)} %multiply_reduce_fusion.1), channel_id=1, replica_groups=mesh['lsec'=8,'rsec'=32] {'lsec','rsec'}, use_global_device_ids=true, to_apply=%region_9.0 | all-reduce | flops 1 | bytes 8 | tf_op jit(solution)/shard_map/psum | solution.py:72
  501.1 2.2 multiply_convert_fusion.1
  503.3 0.1 fusion.139
  503.4 2.6 collective-permute-start.8
  506.0 1.9 collective-permute-start.9
  509.2 2.9 collective-permute-done.8
  512.1 4.4 collective-permute-done.9
  516.5 1.1 pad_maximum_fusion.54
  517.6 7.2 %collective-permute-start.10 = (bf16[1,4,256,256]{3,2,0,1:T(8,128)(2,1)}, bf16[1,4,256,256]{3,2,0,1:T(8,128)(2,1)}, u32[]{:S(2)}, u32[]{:S(2)}) collective-permute-start(bf16[1,4,256,256]{3,2,0,1:T(8,128)(2,1)} %get-tuple-element.5), channel_id=1, source_target_pairs={{0,32},{32,64},{64,96},{96,128},{128,160},{160,192},{192,224},{1,3... | collective-permute-start | bytes 1572872 | tf_op jit(solution)/shard_map/ppermute | solution.py:19
  524.8 3.0 fusion.37
  527.9 1.3 collective-permute-start.11
  529.2 3.1 fusion.39
  532.3 2.4 collective-permute-done.10
  534.7 3.3 fusion.41
  538.0 1.6 collective-permute-done.11
  539.6 6.3 fusion.6
  545.9 86.2 %psum.54 = f32[]{:T(128)} all-reduce(f32[]{:T(128)} %get-tuple-element.24), channel_id=1, replica_groups=mesh['lsec'=8,'rsec'=32] {'lsec','rsec'}, use_global_device_ids=true, to_apply=%region_11.0 | all-reduce | flops 1 | bytes 8 | tf_op jit(solution)/shard_map/psum | solution.py:70
  632.7 2.7 multiply_reduce_fusion
  635.4 73.4 %psum.55 = f32[]{:T(128)} all-reduce(f32[]{:T(128)} %multiply_reduce_fusion), channel_id=1, replica_groups=mesh['lsec'=8,'rsec'=32] {'lsec','rsec'}, use_global_device_ids=true, to_apply=%region_13.0 | all-reduce | flops 1 | bytes 8 | tf_op jit(solution)/shard_map/psum | solution.py:72
  709.5 2.1 multiply_convert_fusion
  711.6 1.0 copy.13
  712.7 0.6 pad_maximum_fusion.63
  (23 shorter events, 0.0 us)
Async XLA Ops:
  86.6 20.7 %copy-start.1 = (bf16[4,4,256,256]{3,2,1,0:T(8,128)(2,1)S(1)}, bf16[4,4,256,256]{3,2,1,0:T(8,128)(2,1)}, u32[]{:S(2)}) copy-start(bf16[4,4,256,256]{3,2,1,0:T(8,128)(2,1)} %param.7) | copy-start | bytes 6291460
  86.6 8.2 %collective-permute-start = (bf16[4,1,256,256]{3,2,0,1:T(8,128)(2,1)S(1)}, bf16[4,1,256,256]{3,2,0,1:T(8,128)(2,1)S(1)}, u32[]{:S(2)}, u32[]{:S(2)}) collective-permute-start(bf16[4,1,256,256]{3,2,0,1:T(8,128)(2,1)S(1)} %get-tuple-element.14), channel_id=1, source_target_pairs={{0,1},{1,2},{2,3},{3,4},{4,5},{5,6},{6,7},{7,8},{8,9},{9,10},{10,1... | collective-permute-start | bytes 1572872 | tf_op jit(solution)/shard_map/ppermute | solution.py:19
  88.6 10.5 %collective-permute-start.1 = (bf16[4,1,256,256]{3,2,0,1:T(8,128)(2,1)S(1)}, bf16[4,1,256,256]{3,2,0,1:T(8,128)(2,1)S(1)}, u32[]{:S(2)}, u32[]{:S(2)}) collective-permute-start(bf16[4,1,256,256]{3,2,0,1:T(8,128)(2,1)S(1)} %get-tuple-element.15), channel_id=1, source_target_pairs={{1,0},{2,1},{3,2},{4,3},{5,4},{6,5},{7,6},{8,7},{9,8},{10,9},{11,1... | collective-permute-start | bytes 1572872 | tf_op jit(solution)/shard_map/ppermute | solution.py:22
  94.7 4.4 copy-start.8
  99.1 1.1 copy-start.9
  100.3 17.4 %collective-permute-start.2 = (bf16[1,4,256,256]{3,2,0,1:T(8,128)(2,1)}, bf16[1,4,256,256]{3,2,0,1:T(8,128)(2,1)}, u32[]{:S(2)}, u32[]{:S(2)}) collective-permute-start(bf16[1,4,256,256]{3,2,0,1:T(8,128)(2,1)} %get-tuple-element.9), channel_id=1, source_target_pairs={{0,32},{32,64},{64,96},{96,128},{128,160},{160,192},{192,224},{1,3... | collective-permute-start | bytes 1572872 | tf_op jit(solution)/shard_map/ppermute | solution.py:19
  110.2 11.7 %collective-permute-start.3 = (bf16[1,4,256,256]{3,2,0,1:T(8,128)(2,1)}, bf16[1,4,256,256]{3,2,0,1:T(8,128)(2,1)}, u32[]{:S(2)}, u32[]{:S(2)}) collective-permute-start(bf16[1,4,256,256]{3,2,0,1:T(8,128)(2,1)} %get-tuple-element.8), channel_id=1, source_target_pairs={{32,0},{64,32},{96,64},{128,96},{160,128},{192,160},{224,192},{33,... | collective-permute-start | bytes 1572872 | tf_op jit(solution)/shard_map/ppermute | solution.py:22
  114.5 7.4 %copy-start.10 = (f32[4,2]{0,1:T(2,128)S(1)}, f32[4,2]{0,1:T(2,128)}, u32[]{:S(2)}) copy-start(f32[4,2]{0,1:T(2,128)} %param.9) | copy-start | bytes 100
  120.8 94.0 %copy-start = (bf16[4,2,256,256]{3,2,1,0:T(8,128)(2,1)S(1)}, bf16[4,2,256,256]{3,2,1,0:T(8,128)(2,1)}, u32[]{:S(2)}) copy-start(bf16[4,2,256,256]{3,2,1,0:T(8,128)(2,1)} %param.6) | copy-start | bytes 3145732
  293.7 5.6 copy-start.11
  293.7 6.8 copy-start.12
  293.8 22.4 %copy-start.2 = (bf16[2,4,256,256]{3,2,1,0:T(8,128)(2,1)S(1)}, bf16[2,4,256,256]{3,2,1,0:T(8,128)(2,1)}, u32[]{:S(2)}) copy-start(bf16[2,4,256,256]{3,2,1,0:T(8,128)(2,1)} %param.8) | copy-start | bytes 3145732
  293.8 9.6 %collective-permute-start.4 = (bf16[4,1,256,256]{3,2,0,1:T(8,128)(2,1)S(1)}, bf16[4,1,256,256]{3,2,0,1:T(8,128)(2,1)S(1)}, u32[]{:S(2)}, u32[]{:S(2)}) collective-permute-start(bf16[4,1,256,256]{3,2,0,1:T(8,128)(2,1)S(1)} %get-tuple-element.12), channel_id=1, source_target_pairs={{0,1},{1,2},{2,3},{3,4},{4,5},{5,6},{6,7},{7,8},{8,9},{9,10},{10,1... | collective-permute-start | bytes 1572872 | tf_op jit(solution)/shard_map/ppermute | solution.py:19
  297.3 10.5 %collective-permute-start.5 = (bf16[4,1,256,256]{3,2,0,1:T(8,128)(2,1)S(1)}, bf16[4,1,256,256]{3,2,0,1:T(8,128)(2,1)S(1)}, u32[]{:S(2)}, u32[]{:S(2)}) collective-permute-start(bf16[4,1,256,256]{3,2,0,1:T(8,128)(2,1)S(1)} %get-tuple-element.13), channel_id=1, source_target_pairs={{1,0},{2,1},{3,2},{4,3},{5,4},{6,5},{7,6},{8,7},{9,8},{10,9},{11,1... | collective-permute-start | bytes 1572872 | tf_op jit(solution)/shard_map/ppermute | solution.py:22
  303.4 4.4 copy-start.4
  307.8 1.1 copy-start.5
  309.0 23.0 %collective-permute-start.6 = (bf16[1,4,256,256]{3,2,0,1:T(8,128)(2,1)}, bf16[1,4,256,256]{3,2,0,1:T(8,128)(2,1)}, u32[]{:S(2)}, u32[]{:S(2)}) collective-permute-start(bf16[1,4,256,256]{3,2,0,1:T(8,128)(2,1)} %get-tuple-element.7), channel_id=1, source_target_pairs={{0,32},{32,64},{64,96},{96,128},{128,160},{160,192},{192,224},{1,3... | collective-permute-start | bytes 1572872 | tf_op jit(solution)/shard_map/ppermute | solution.py:19
  319.2 16.1 %collective-permute-start.7 = (bf16[1,4,256,256]{3,2,0,1:T(8,128)(2,1)}, bf16[1,4,256,256]{3,2,0,1:T(8,128)(2,1)}, u32[]{:S(2)}, u32[]{:S(2)}) collective-permute-start(bf16[1,4,256,256]{3,2,0,1:T(8,128)(2,1)} %get-tuple-element.6), channel_id=1, source_target_pairs={{32,0},{64,32},{96,64},{128,96},{160,128},{192,160},{224,192},{33,... | collective-permute-start | bytes 1572872 | tf_op jit(solution)/shard_map/ppermute | solution.py:22
  503.4 21.5 %copy-start.3 = (bf16[2,4,256,256]{3,2,1,0:T(8,128)(2,1)S(1)}, bf16[2,4,256,256]{3,2,1,0:T(8,128)(2,1)}, u32[]{:S(2)}) copy-start(bf16[2,4,256,256]{3,2,1,0:T(8,128)(2,1)} %param.8) | copy-start | bytes 3145732
  503.4 8.7 %collective-permute-start.8 = (bf16[4,1,256,256]{3,2,0,1:T(8,128)(2,1)S(1)}, bf16[4,1,256,256]{3,2,0,1:T(8,128)(2,1)S(1)}, u32[]{:S(2)}, u32[]{:S(2)}) collective-permute-start(bf16[4,1,256,256]{3,2,0,1:T(8,128)(2,1)S(1)} %get-tuple-element.10), channel_id=1, source_target_pairs={{0,1},{1,2},{2,3},{3,4},{4,5},{5,6},{6,7},{7,8},{8,9},{9,10},{10,1... | collective-permute-start | bytes 1572872 | tf_op jit(solution)/shard_map/ppermute | solution.py:19
  506.0 10.5 %collective-permute-start.9 = (bf16[4,1,256,256]{3,2,0,1:T(8,128)(2,1)S(1)}, bf16[4,1,256,256]{3,2,0,1:T(8,128)(2,1)S(1)}, u32[]{:S(2)}, u32[]{:S(2)}) collective-permute-start(bf16[4,1,256,256]{3,2,0,1:T(8,128)(2,1)S(1)} %get-tuple-element.11), channel_id=1, source_target_pairs={{1,0},{2,1},{3,2},{4,3},{5,4},{6,5},{7,6},{8,7},{9,8},{10,9},{11,1... | collective-permute-start | bytes 1572872 | tf_op jit(solution)/shard_map/ppermute | solution.py:22
  512.1 4.4 copy-start.6
  516.5 1.1 copy-start.7
  517.6 17.0 %collective-permute-start.10 = (bf16[1,4,256,256]{3,2,0,1:T(8,128)(2,1)}, bf16[1,4,256,256]{3,2,0,1:T(8,128)(2,1)}, u32[]{:S(2)}, u32[]{:S(2)}) collective-permute-start(bf16[1,4,256,256]{3,2,0,1:T(8,128)(2,1)} %get-tuple-element.5), channel_id=1, source_target_pairs={{0,32},{32,64},{64,96},{96,128},{128,160},{160,192},{192,224},{1,3... | collective-permute-start | bytes 1572872 | tf_op jit(solution)/shard_map/ppermute | solution.py:19
  527.9 11.7 %collective-permute-start.11 = (bf16[1,4,256,256]{3,2,0,1:T(8,128)(2,1)}, bf16[1,4,256,256]{3,2,0,1:T(8,128)(2,1)}, u32[]{:S(2)}, u32[]{:S(2)}) collective-permute-start(bf16[1,4,256,256]{3,2,0,1:T(8,128)(2,1)} %get-tuple-element.4), channel_id=1, source_target_pairs={{32,0},{64,32},{96,64},{128,96},{160,128},{192,160},{224,192},{33,... | collective-permute-start | bytes 1572872 | tf_op jit(solution)/shard_map/ppermute | solution.py:22
where the time goes:
time: 715 us; the launch traced here: 713 us
  blocking collectives  556 us (78%)
  matrix products  47 us (7%)
  starting transfers between devices  39.6 us (6%)
  waiting for transfers between devices  38.1 us (5%)
  other arithmetic  22.3 us (3%)
  between operations  8.15 us (1%)
    psum x3, blocking collectives, per_device(): theta = lax.psum(jnp.sum(vals * sigma), ('lsec', 'rsec')) * count  254 us
    psum x3, blocking collectives, per_device(): norm_sq = lax.psum(jnp.sum(resid * resid), ('lsec', 'rsec')) * count  220 us
    psum x1, blocking collectives, per_device(): start = lax.psum(jnp.sum(start_vals * start_vals), ('lsec', 'rsec')) * count  81.4 us
    dot_general x12, matrix products, add_terms(): jnp.einsum('abik,blk->abil', inner, right_env[:, term], preferred_element...  47 us
    ppermute x6, starting transfers between devices, padded(): lax.ppermute(lax.slice_in_dim(block, block.shape[dim] - width, None, axis...  29.5 us
    ppermute x6, waiting for transfers between devices, padded(): lax.ppermute(lax.slice_in_dim(block, block.shape[dim] - width, None, axis...  22.2 us
    ppermute x6, waiting for transfers between devices, padded(): lax.ppermute(lax.slice_in_dim(block, 0, width, axis=dim), axis, backward)  15.9 us
  transfers between devices with their start and end apart: 12, of which 11 were waited for; matrix products, arithmetic and copies ran while one was open for 4% of the time, Pallas kernels for 0%

commit v1 on v0

v1 whole, which is shorter than its diff:
```python
import jax
import jax.numpy as jnp
from jax import lax
from jax.sharding import PartitionSpec as P

DIAG = 2
HOPS = 1
ITERS = 3
AXES = ("lsec", "rsec")
eps = 1e-06
SHIFT = 1.75
SHRINK = 8.0


def shift_blocks(block, down, right):
    rows, cols = lax.axis_size("lsec"), lax.axis_size("rsec")
    pairs = [
        (row * cols + col, (row + down) * cols + col + right)
        for row in range(rows)
        for col in range(cols)
        if 0 <= row + down < rows and 0 <= col + right < cols
    ]
    return lax.ppermute(block, AXES, pairs)


def add_terms(left_env, right_env, source, first, number, total):
    for term in range(first, first + number):
        inner = jnp.einsum(
            "aij,abjk->abik", left_env[:, term], source, preferred_element_type=jnp.float32
        ).astype(jnp.bfloat16)
        total = total + jnp.einsum(
            "abik,blk->abil", inner, right_env[:, term], preferred_element_type=jnp.float32
        )
    return total


def matvec(vec, left_env, right_env, energies):
    total = energies[:, :, None, None] * vec.astype(jnp.float32)
    total = add_terms(left_env, right_env, vec, 0, DIAG, total)
    from_right = shift_blocks(vec[:-1, :1], 0, -1)
    from_left = shift_blocks(vec[1:, -1:], 0, 1)
    from_up = shift_blocks(vec[-1:, 1:], 1, 0)
    from_down = shift_blocks(vec[:1, :-1], -1, 0)
    up_right = shift_blocks(vec[-1:, :1], 1, -1)
    down_left = shift_blocks(vec[:1, -1:], -1, 1)
    plus_blocks = jnp.concatenate(
        [
            jnp.concatenate([from_up, up_right], axis=1),
            jnp.concatenate([vec[:-1, 1:], from_right], axis=1),
        ],
        axis=0,
    )
    minus_blocks = jnp.concatenate(
        [
            jnp.concatenate([from_left, vec[1:, :-1]], axis=1),
            jnp.concatenate([down_left, from_down], axis=1),
        ],
        axis=0,
    )
    total = add_terms(left_env, right_env, plus_blocks, DIAG, HOPS, total)
    total = add_terms(left_env, right_env, minus_blocks, DIAG + HOPS, HOPS, total)
    return total


def coefficient(coef_num, coef_den, step):
    if step == 0:
        return jnp.float32(0.0)
    return coef_num[step - 1].astype(jnp.float32) / coef_den[step - 1].astype(jnp.float32)


def stepwise(psi, left_env, right_env, energies, coef_num, coef_den, count):
    start_vals = psi.astype(jnp.float32)
    start = lax.psum(jnp.sum(start_vals * start_vals), AXES) * count
    vec = (start_vals * lax.rsqrt(start + eps)).astype(jnp.bfloat16)
    previous = jnp.zeros(psi.shape, jnp.float32)
    thetas = []
    for step in range(ITERS):
        sigma = matvec(vec, left_env, right_env, energies)
        vals = vec.astype(jnp.float32)
        coef = coefficient(coef_num, coef_den, step)
        theta = lax.psum(jnp.sum(vals * sigma), AXES) * count
        resid = sigma - theta * vals - coef * previous
        norm_sq = lax.psum(jnp.sum(resid * resid), AXES) * count
        thetas.append(theta)
        previous = vals
        vec = (resid * lax.rsqrt(norm_sq + eps)).astype(jnp.bfloat16)
    return (vec, jnp.stack(thetas))


def gather_sum(parts):
    devices = lax.axis_size("lsec") * lax.axis_size("rsec")
    row = jnp.zeros((1, 128), jnp.float32).at[0, : parts.shape[0]].set(parts)
    sent = jnp.broadcast_to(row[None], (devices, 1, 128))
    return jnp.sum(lax.all_to_all(sent, AXES, 0, 0), axis=(0, 1))


def recursion(gram, coef_num, coef_den):
    def quad(left, right):
        return sum(
            left[i] * right[j] * gram[min(i, j)][max(i, j)]
            for i in range(len(left))
            for j in range(len(right))
        )

    scale = lax.rsqrt(gram[0][0] + eps)
    vec, previous = [scale], []
    thetas, fine = [], jnp.bool_(True)
    for step in range(ITERS):
        moved = [jnp.float32(0.0)] + vec
        theta = quad(vec, [SHIFT * entry for entry in vec]) + quad(vec, moved)
        thetas.append(theta)
        coef = coefficient(coef_num, coef_den, step)
        resid = list(moved)
        for i, entry in enumerate(vec):
            resid[i] = resid[i] + (SHIFT - theta) * entry
        for i, entry in enumerate(previous):
            resid[i] = resid[i] - coef * entry
        norm_sq = quad(resid, resid)
        lead = resid[-1]
        fine = fine & (lead * lead * gram[step + 1][step + 1] <= SHRINK * (norm_sq + eps))
        norm = lax.rsqrt(jnp.maximum(norm_sq, 0.0) + eps)
        previous = vec
        vec = [entry * norm for entry in resid]
    return vec, thetas, fine


def per_device(psi, left_env, right_env, energies, coef_num, coef_den):
    count = 1.0 / float(psi.size * lax.axis_size("lsec") * lax.axis_size("rsec"))
    basis = [psi]
    parts = [jnp.sum(psi.astype(jnp.float32) ** 2)]
    for step in range(ITERS):
        image = matvec(basis[-1], left_env, right_env, energies - SHIFT)
        if step < ITERS - 1:
            image = image.astype(jnp.bfloat16)
        basis.append(image)
        vals = image.astype(jnp.float32)
        for other in basis:
            parts.append(jnp.sum(vals * other.astype(jnp.float32)))
    sums = gather_sum(jnp.stack(parts) * count)
    gram = [[None] * (ITERS + 1) for _ in range(ITERS + 1)]
    place = 0
    for right in range(ITERS + 1):
        for left in range(right + 1):
            gram[left][right] = sums[place]
            place += 1
    weights, thetas, fine = recursion(gram, coef_num, coef_den)

    def combine():
        total = weights[0] * psi.astype(jnp.float32)
        for weight, vec in zip(weights[1:], basis[1:]):
            total = total + weight * vec.astype(jnp.float32)
        return total.astype(jnp.bfloat16), jnp.stack(thetas)

    def again():
        return stepwise(psi, left_env, right_env, energies, coef_num, coef_den, count)

    return lax.cond(fine, combine, again)


def solution(mesh):
    in_specs = (
        P("lsec", "rsec", None, None),
        P("lsec", None, None, None),
        P("rsec", None, None, None),
        P("lsec", "rsec"),
        P(),
        P(),
    )
    out_specs = (P("lsec", "rsec", None, None), P())
    return jax.shard_map(
        per_device, mesh=mesh, in_specs=in_specs, out_specs=out_specs, check_vma=False
    )
```

time: 715 us -> 207 us (0.29)
  blocking collectives: 556 us -> 0 us
  starting transfers between devices: 39.6 us -> 72.4 us
  between operations: 8.15 us -> 38.4 us
  local copies, waits for them, and re-layouts: 2.49 us -> 22.9 us
  other arithmetic: 22.3 us -> 3.73 us
  waiting for transfers between devices: 38.1 us -> 20.1 us
    psum x7 -> x0, blocking collectives: 556 us -> none  [the longest x3 254 us: per_device(): theta = lax.psum(jnp.sum(vals * sigma), ('lsec', 'rsec')) * count]
    ppermute x12 -> x18, waiting for transfers between devices: 38.1 us -> 11.2 us  [shift_blocks(): return lax.ppermute(block, AXES, pairs)]
    all_to_all x0 -> x1, starting transfers between devices: none -> 16.6 us  [gather_sum(): return jnp.sum(lax.all_to_all(sent, AXES, 0, 0), axis=(0, 1))]
    ppermute x12 -> x18, starting transfers between devices: 39.6 us -> 55.7 us  [shift_blocks(): return lax.ppermute(block, AXES, pairs)]
    reduce_sum x4 -> x1, other arithmetic: 10.7 us -> 0.05 us  [gather_sum(): return jnp.sum(lax.all_to_all(sent, AXES, 0, 0), axis=(0, 1))]
    all_to_all x0 -> x1, waiting for transfers between devices: none -> 8.86 us  [gather_sum(): return jnp.sum(lax.all_to_all(sent, AXES, 0, 0), axis=(0, 1))]
  transfers between devices with their start and end apart: 12 -> 19, of which waited for: 11 -> 6; matrix products, arithmetic and copies ran while one was open for 4% -> 16% of each run, Pallas kernels for 0% -> 0%
where the time goes in v1:
time: 207 us; the launch traced here: 205 us
  starting transfers between devices  72.4 us (35%)
  matrix products  47.5 us (23%)
  between operations  38.4 us (19%)
  local copies, waits for them, and re-layouts  22.9 us (11%)
  waiting for transfers between devices  20.1 us (10%)
  other arithmetic  3.73 us (2%)
    ppermute x18, starting transfers between devices, shift_blocks(): return lax.ppermute(block, AXES, pairs)  55.7 us
    dot_general x12, matrix products, add_terms(): jnp.einsum('abik,blk->abil', inner, right_env[:, term], preferred_element...  47.5 us
    all_to_all x1, starting transfers between devices, gather_sum(): return jnp.sum(lax.all_to_all(sent, AXES, 0, 0), axis=(0, 1))  16.6 us
    ppermute x18, waiting for transfers between devices, shift_blocks(): return lax.ppermute(block, AXES, pairs)  11.2 us
    all_to_all x1, waiting for transfers between devices, gather_sum(): return jnp.sum(lax.all_to_all(sent, AXES, 0, 0), axis=(0, 1))  8.86 us
    unnamed x26, local copies, waits for them, and re-layouts  7.83 us
    another operation x1, local copies, waits for them, and re-layouts, per_device(): sums = gather_sum(jnp.stack(parts) * count)  6.54 us
  transfers between devices with their start and end apart: 19, of which 6 were waited for; matrix products, arithmetic and copies ran while one was open for 16% of the time, Pallas kernels for 0%

profile of v1, /device:TPU:1, one launch (start us, length us, event | category | flops | bytes accessed | tf_op | source)
XLA Modules:
  0.0 205.2 jit_solution(423675083954398420)
XLA Ops:
  0.6 1.2 fusion.374
  1.9 0.7 copy.166
  2.6 1.3 collective-permute-start.23
  3.9 0.8 copy.157
  4.7 6.9 %collective-permute-start.18 = (bf16[1,1,256,256]{2,3,0,1:T(8,128)(2,1)}, bf16[1,1,256,256]{2,3,0,1:T(8,128)(2,1)}, u32[]{:S(2)}, u32[]{:S(2)}) collective-permute-start(bf16[1,1,256,256]{2,3,0,1:T(8,128)(2,1)} %copy.157), channel_id=1, source_target_pairs={{0,32},{1,33},{2,34},{3,35},{4,36},{5,37},{6,38},{7,39},{8,40},{9,... | collective-permute-start | bytes 393224 | tf_op jit(solution)/shard_map/ppermute | solution.py:23
  11.6 0.8 copy.158
  12.3 7.0 %collective-permute-start.19 = (bf16[1,1,256,256]{2,3,0,1:T(8,128)(2,1)}, bf16[1,1,256,256]{2,3,0,1:T(8,128)(2,1)}, u32[]{:S(2)}, u32[]{:S(2)}) collective-permute-start(bf16[1,1,256,256]{2,3,0,1:T(8,128)(2,1)} %copy.158), channel_id=1, source_target_pairs={{1,32},{2,33},{3,34},{4,35},{5,36},{6,37},{7,38},{8,39},{9,40},{10... | collective-permute-start | bytes 393224 | tf_op jit(solution)/shard_map/ppermute | solution.py:23
  19.4 0.9 fusion.373
  20.2 1.9 copy.160
  22.2 1.9 collective-permute-start.20
  24.1 0.9 copy.163
  25.0 3.6 %collective-permute-start.21 = (bf16[3,1,256,256]{2,3,0,1:T(8,128)(2,1)}, bf16[3,1,256,256]{2,3,0,1:T(8,128)(2,1)}, u32[]{:S(2)}, u32[]{:S(2)}) collective-permute-start(bf16[3,1,256,256]{2,3,0,1:T(8,128)(2,1)} %copy.163), channel_id=1, source_target_pairs={{0,1},{1,2},{2,3},{3,4},{4,5},{5,6},{6,7},{7,8},{8,9},{9,10},{10,1... | collective-permute-start | bytes 1179656 | tf_op jit(solution)/shard_map/ppermute | solution.py:23
  28.7 3.3 %fusion.163 = f32[2,4,256,256]{3,2,1,0:T(8,128)} fusion(bf16[4,4,256,256]{3,2,1,0:T(8,128)(2,1)} %param.11, bf16[4,2,256,256]{3,2,1,0:T(8,128)(2,1)S(1)} %copy-done, bf16[2,4,256,256]{3,2,1,0:T(8,128)(2,1)S(1)} %copy-done.1), kind=kOutput, calls=%fused_computation.182 | convolution fusion | flops 537395200 | bytes 3932160 | tf_op jit(solution)/shard_map/abik,blk->abil/dot_general | solution.py:31
  31.9 3.3 %fusion.165 = f32[2,4,256,256]{3,2,1,0:T(8,128)} fusion(bf16[4,4,256,256]{3,2,1,0:T(8,128)(2,1)} %param.11, bf16[4,2,256,256]{3,2,1,0:T(8,128)(2,1)S(1)} %copy-done, bf16[2,4,256,256]{3,2,1,0:T(8,128)(2,1)S(1)} %copy-done.1), kind=kOutput, calls=%fused_computation.184 | convolution fusion | flops 537395200 | bytes 3932160 | tf_op jit(solution)/shard_map/abik,blk->abil/dot_general | solution.py:31
  35.3 0.7 copy.165
  36.0 0.2 copy.164
  36.2 0.2 copy.159
  36.4 0.6 compare_reduce_fusion
  37.0 1.3 collective-permute-start.22
  38.3 3.4 %fusion.167 = f32[2,4,256,256]{3,2,1,0:T(8,128)} fusion(bf16[3,1,256,256]{2,3,0,1:T(8,128)(2,1)} %collective-permute-done.20, bf16[3,1,256,256]{2,3,0,1:T(8,128)(2,1)S(1)} %copy.159, bf16[1,1,256,256]{2,3,0,1:T(8,128)(2,1)} %collective-permute-done.19, bf16[1,1,256,256]{2,3,0,1:T(8,128)(2,1)} %collective-permute-done.18, ...), kind=kOutput, calls=%fused_computation.186 | convolution fusion | flops 538968064 | bytes 3932160 | tf_op jit(solution)/shard_map/abik,blk->abil/dot_general | solution.py:31
  41.7 3.3 %collective-permute-done.22 = bf16[1,1,256,256]{2,3,0,1:T(8,128)(2,1)S(1)} collective-permute-done((bf16[1,1,256,256]{2,3,0,1:T(8,128)(2,1)}, bf16[1,1,256,256]{2,3,0,1:T(8,128)(2,1)S(1)}, u32[]{:S(2)}, u32[]{:S(2)}) %collective-permute-start.22) | collective-permute-done | bytes 131104 | tf_op jit(solution)/shard_map/ppermute | solution.py:23
  45.0 0.6 copy-done.6
  45.7 4.4 %fusion.144 = bf16[4,2,256,256]{3,2,0,1:T(8,128)(2,1)S(1)} fusion(f32[2,4,256,256]{3,2,1,0:T(8,128)} %fusion.167, f32[2,4,256,256]{3,2,1,0:T(8,128)} %fusion.165, f32[2,4,256,256]{3,2,1,0:T(8,128)} %fusion.163, bf16[1,1,256,256]{2,3,0,1:T(8,128)(2,1)} %copy-done.5, bf16[1,1,256,256]{2,3,0,1:T(8,128)(2,1)} %copy-done.6, ...), kind=kOutput, calls=%fused_computation.150 | convolution fusion | flops 542638080 | bytes 10224640 | tf_op jit(solution)/shard_map/abik,blk->abil/dot_general | solution.py:31
  50.0 1.1 fusion.371
  51.1 3.3 %fusion.172 = f32[2,4,256,256]{3,2,1,0:T(8,128)} fusion(bf16[4,2,256,256]{3,2,0,1:T(8,128)(2,1)S(1)} %fusion.144, bf16[4,4,256,256]{3,2,1,0:T(8,128)(2,1)} %param.11, bf16[2,4,256,256]{3,2,1,0:T(8,128)(2,1)S(1)} %copy-done.1), kind=kOutput, calls=%fused_computation.191 | convolution fusion | flops 537395200 | bytes 3932160 | tf_op jit(solution)/shard_map/abik,blk->abil/dot_general | solution.py:31
  54.4 1.9 collective-permute-start.26
  56.3 0.8 fusion.372
  57.1 3.1 %collective-permute-start.25 = (bf16[1,1,256,256]{3,2,0,1:T(8,128)(2,1)}, bf16[1,1,256,256]{3,2,0,1:T(8,128)(2,1)}, u32[]{:S(2)}, u32[]{:S(2)}) collective-permute-start(bf16[1,1,256,256]{3,2,0,1:T(8,128)(2,1)} %get-tuple-element.220), channel_id=1, source_target_pairs={{1,32},{2,33},{3,34},{4,35},{5,36},{6,37},{7,38},{8,39},{9,40},{10... | collective-permute-start | bytes 393224 | tf_op jit(solution)/shard_map/ppermute | solution.py:23
  60.3 2.7 %collective-permute-start.24 = (bf16[1,1,256,256]{3,2,0,1:T(8,128)(2,1)}, bf16[1,1,256,256]{3,2,0,1:T(8,128)(2,1)}, u32[]{:S(2)}, u32[]{:S(2)}) collective-permute-start(bf16[1,1,256,256]{3,2,0,1:T(8,128)(2,1)} %get-tuple-element.221), channel_id=1, source_target_pairs={{0,32},{1,33},{2,34},{3,35},{4,36},{5,37},{6,38},{7,39},{8,40},{9,... | collective-permute-start | bytes 393224 | tf_op jit(solution)/shard_map/ppermute | solution.py:23
  62.9 4.7 %collective-permute-start.27 = (bf16[3,1,256,256]{3,2,0,1:T(8,128)(2,1)}, bf16[3,1,256,256]{3,2,0,1:T(8,128)(2,1)}, u32[]{:S(2)}, u32[]{:S(2)}) collective-permute-start(bf16[3,1,256,256]{3,2,0,1:T(8,128)(2,1)} %get-tuple-element.214), channel_id=1, source_target_pairs={{0,1},{1,2},{2,3},{3,4},{4,5},{5,6},{6,7},{7,8},{8,9},{9,10},{10,1... | collective-permute-start | bytes 1179656 | tf_op jit(solution)/shard_map/ppermute | solution.py:23
  67.6 3.3 %fusion.170 = f32[2,4,256,256]{3,2,1,0:T(8,128)} fusion(bf16[4,2,256,256]{3,2,0,1:T(8,128)(2,1)S(1)} %fusion.144, bf16[4,4,256,256]{3,2,1,0:T(8,128)(2,1)} %param.11, bf16[2,4,256,256]{3,2,1,0:T(8,128)(2,1)S(1)} %copy-done.1), kind=kOutput, calls=%fused_computation.189 | convolution fusion | flops 537395200 | bytes 3932160 | tf_op jit(solution)/shard_map/abik,blk->abil/dot_general | solution.py:31
  70.9 1.3 collective-permute-start.28
  72.2 1.3 collective-permute-start.29
  73.5 3.6 %fusion.174 = f32[2,4,256,256]{3,2,1,0:T(8,128)} fusion(bf16[3,1,256,256]{3,2,0,1:T(8,128)(2,1)} %collective-permute-done.26, bf16[3,1,256,256]{3,2,0,1:T(8,128)(2,1)} %get-tuple-element.217, bf16[1,1,256,256]{3,2,0,1:T(8,128)(2,1)} %collective-permute-done.25, bf16[1,1,256,256]{3,2,0,1:T(8,128)(2,1)} %collective-permute-done.24, ...), kind=kOutput, calls=%fused_computation.193 | convolution fusion | flops 538968064 | bytes 3932160 | tf_op jit(solution)/shard_map/abik,blk->abil/dot_general | solution.py:31
  77.1 1.8 collective-permute-done.28
  79.0 2.1 %collective-permute-done.29 = bf16[1,1,256,256]{3,2,0,1:T(8,128)(2,1)} collective-permute-done((bf16[1,1,256,256]{3,2,0,1:T(8,128)(2,1)}, bf16[1,1,256,256]{3,2,0,1:T(8,128)(2,1)}, u32[]{:S(2)}, u32[]{:S(2)}) %collective-permute-start.29) | collective-permute-done | bytes 131104 | tf_op jit(solution)/shard_map/ppermute | solution.py:23
  81.1 4.5 %fusion.152 = bf16[4,2,256,256]{3,2,0,1:T(8,128)(2,1)S(1)} fusion(bf16[4,2,256,256]{3,2,0,1:T(8,128)(2,1)S(1)} %fusion.144, f32[2,4,256,256]{3,2,1,0:T(8,128)} %fusion.174, f32[2,4,256,256]{3,2,1,0:T(8,128)} %fusion.172, f32[2,4,256,256]{3,2,1,0:T(8,128)} %fusion.170, bf16[1,1,256,256]{3,2,0,1:T(8,128)(2,1)} %collective-permute-done.29, ...), kind=kOutput, calls=%fused_computation.158 | convolution fusion | flops 542638080 | bytes 10223648 | tf_op jit(solution)/shard_map/abik,blk->abil/dot_general | solution.py:31
  85.6 1.0 fusion.369
  86.6 3.4 %fusion.179 = f32[2,4,256,256]{3,2,1,0:T(8,128)} fusion(bf16[4,2,256,256]{3,2,0,1:T(8,128)(2,1)S(1)} %fusion.152, bf16[4,4,256,256]{3,2,1,0:T(8,128)(2,1)} %param.11, bf16[2,4,256,256]{3,2,1,0:T(8,128)(2,1)} %param.12), kind=kOutput, calls=%fused_computation.198 | convolution fusion | flops 537395200 | bytes 3932160 | tf_op jit(solution)/shard_map/abik,blk->abil/dot_general | solution.py:31
  90.0 3.4 %collective-permute-start.32 = (bf16[3,1,256,256]{3,2,0,1:T(8,128)(2,1)}, bf16[3,1,256,256]{3,2,0,1:T(8,128)(2,1)}, u32[]{:S(2)}, u32[]{:S(2)}) collective-permute-start(bf16[3,1,256,256]{3,2,0,1:T(8,128)(2,1)} %get-tuple-element.208), channel_id=1, source_target_pairs={{1,0},{2,1},{3,2},{4,3},{5,4},{6,5},{7,6},{8,7},{9,8},{10,9},{11,1... | collective-permute-start | bytes 1179656 | tf_op jit(solution)/shard_map/ppermute | solution.py:23
  93.5 0.8 fusion.370
  94.3 5.7 %collective-permute-start.31 = (bf16[1,1,256,256]{3,2,0,1:T(8,128)(2,1)}, bf16[1,1,256,256]{3,2,0,1:T(8,128)(2,1)}, u32[]{:S(2)}, u32[]{:S(2)}) collective-permute-start(bf16[1,1,256,256]{3,2,0,1:T(8,128)(2,1)} %get-tuple-element.212), channel_id=1, source_target_pairs={{1,32},{2,33},{3,34},{4,35},{5,36},{6,37},{7,38},{8,39},{9,40},{10... | collective-permute-start | bytes 393224 | tf_op jit(solution)/shard_map/ppermute | solution.py:23
  99.9 3.1 %collective-permute-start.30 = (bf16[1,1,256,256]{3,2,0,1:T(8,128)(2,1)}, bf16[1,1,256,256]{3,2,0,1:T(8,128)(2,1)}, u32[]{:S(2)}, u32[]{:S(2)}) collective-permute-start(bf16[1,1,256,256]{3,2,0,1:T(8,128)(2,1)} %get-tuple-element.213), channel_id=1, source_target_pairs={{0,32},{1,33},{2,34},{3,35},{4,36},{5,37},{6,38},{7,39},{8,40},{9,... | collective-permute-start | bytes 393224 | tf_op jit(solution)/shard_map/ppermute | solution.py:23
  103.0 4.1 %collective-permute-start.33 = (bf16[3,1,256,256]{3,2,0,1:T(8,128)(2,1)}, bf16[3,1,256,256]{3,2,0,1:T(8,128)(2,1)}, u32[]{:S(2)}, u32[]{:S(2)}) collective-permute-start(bf16[3,1,256,256]{3,2,0,1:T(8,128)(2,1)} %get-tuple-element.206), channel_id=1, source_target_pairs={{0,1},{1,2},{2,3},{3,4},{4,5},{5,6},{6,7},{7,8},{8,9},{9,10},{10,1... | collective-permute-start | bytes 1179656 | tf_op jit(solution)/shard_map/ppermute | solution.py:23
  107.0 3.3 %fusion.177 = f32[2,4,256,256]{3,2,1,0:T(8,128)} fusion(bf16[4,2,256,256]{3,2,0,1:T(8,128)(2,1)S(1)} %fusion.152, bf16[4,4,256,256]{3,2,1,0:T(8,128)(2,1)} %param.11, bf16[2,4,256,256]{3,2,1,0:T(8,128)(2,1)} %param.12), kind=kOutput, calls=%fused_computation.196 | convolution fusion | flops 537395200 | bytes 3932160 | tf_op jit(solution)/shard_map/abik,blk->abil/dot_general | solution.py:31
  110.4 1.3 collective-permute-start.34
  111.7 1.3 collective-permute-start.35
  113.0 3.7 %fusion.181 = f32[2,4,256,256]{3,2,1,0:T(8,128)} fusion(bf16[3,1,256,256]{3,2,0,1:T(8,128)(2,1)} %collective-permute-done.32, bf16[3,1,256,256]{3,2,0,1:T(8,128)(2,1)} %get-tuple-element.209, bf16[1,1,256,256]{3,2,0,1:T(8,128)(2,1)} %collective-permute-done.31, bf16[1,1,256,256]{3,2,0,1:T(8,128)(2,1)} %collective-permute-done.30, ...), kind=kOutput, calls=%fused_computation.200 | convolution fusion | flops 538968064 | bytes 3932160 | tf_op jit(solution)/shard_map/abik,blk->abil/dot_general | solution.py:31
  116.7 1.8 collective-permute-done.34
  118.5 2.2 %collective-permute-done.35 = bf16[1,1,256,256]{3,2,0,1:T(8,128)(2,1)} collective-permute-done((bf16[1,1,256,256]{3,2,0,1:T(8,128)(2,1)}, bf16[1,1,256,256]{3,2,0,1:T(8,128)(2,1)}, u32[]{:S(2)}, u32[]{:S(2)}) %collective-permute-start.35) | collective-permute-done | bytes 131104 | tf_op jit(solution)/shard_map/ppermute | solution.py:23
  120.7 7.9 %multiply_reduce_fusion.3 = (f32[]{:T(128)}, f32[]{:T(128)}, f32[]{:T(128)}, f32[]{:T(128)}, f32[]{:T(128)}, /*index=5*/f32[]{:T(128)}, f32[]{:T(128)}, f32[]{:T...) fusion(bf16[4,2,256,256]{3,2,0,1:T(8,128)(2,1)S(1)} %fusion.152, bf16[4,2,256,256]{3,2,0,1:T(8,128)(2,1)S(1)} %fusion.144, ...), kind=kOutput, calls=%fused_computation.168 | convolution fusion | flops 553648128 | bytes 13369416 | tf_op jit(solution)/shard_map/abik,blk->abil/dot_general | solution.py:31
  128.6 6.5 %stack.67 = f32[10]{0:T(128)S(1)} concatenate(f32[1]{0:T(128)} %bitcast.56, f32[1]{0:T(128)} %bitcast.85, f32[1]{0:T(128)} %bitcast.86, f32[1]{0:T(128)} %bitcast.99, f32[1]{0:T(128)} %bitcast.100, f32[1]{0:T(128)} %bitcast.101, f32[1]{0:T(128)} %bitcast.110, f32[1]{0:T(128)} %bitcast.111, f32[1]{0:T(128)} %bitcast.112, f32[1]{0:T(128)} %bitcast.113), dimensions={0} | concatenate | bytes 80 | tf_op jit(solution)/shard_map/stack | solution.py:139
  135.1 0.7 broadcast_select_fusion
  135.8 0.7 broadcast_in_dim.5
  136.5 16.6 %all-to-all-start = ((f32[256,1,128]{2,1,0:T(1,128)}), f32[256,1,128]{2,1,0:T(1,128)S(1)}, u32[]{:S(2)}, u32[]{:S(2)}) async-start(f32[256,1,128]{2,1,0:T(1,128)} %broadcast_in_dim.5), calls=%async_computation | async-start | bytes 262144 | tf_op jit(solution)/shard_map/all_to_all | solution.py:94
  153.2 0.6 fusion.376
  155.1 0.6 fusion.375
  157.1 8.9 %all-to-all-done = f32[256,1,128]{2,1,0:T(1,128)S(1)} async-done(((f32[256,1,128]{2,1,0:T(1,128)}), f32[256,1,128]{2,1,0:T(1,128)S(1)}, u32[]{:S(2)}, u32[]{:S(2)}) %all-to-all-start) | async-done | bytes 131104 | tf_op jit(solution)/shard_map/all_to_all | solution.py:94
  166.1 0.7 fusion.377
  201.4 2.8 %conditional.3 = (f32[3]{0:T(128)S(1)}, bf16[4,2,256,256]{3,2,1,0:T(8,128)(2,1)S(1)}) conditional(s32[]{:T(128)} %convert_element_type.283, (bf16[4,2,256,256]{3,2,1,0:T(8,128)(2,1)S(1)}, f32[4,2]{0,1:T(2,128)S(1)}, bf16[4,4,256,256]{3,2,1,0:T(8,128)(2,1)}, bf16[2,4,256,256]{3,2,1,0:T(8,128)(2,1)}, s32[2]{0:T(128)S(1)}, ...), branch_computations={%region_12.0_spmd, %region_27.0_spmd} | conditional | flops 6502219776 | bytes 137367744
  201.8 2.3 %add_convert_fusion = bf16[4,2,256,256]{3,2,0,1:T(8,128)(2,1)S(1)} fusion(f32[4,2,256,256]{3,2,0,1:T(8,128)} %get-tuple-element.70, bf16[4,2,256,256]{3,2,0,1:T(8,128)(2,1)S(1)} %get-tuple-element.68, bf16[4,2,256,256]{3,2,0,1:T(8,128)(2,1)S(1)} %get-tuple-element.66, bf16[4,2,256,256]{3,2,1,0:T(8,128)(2,1)S(1)} %get-tuple-element.141, f32[]{:T(128)S(6)} %mul.744, ...), kind=kLoop, calls=%fused_computation.131 | loop fusion | flops 5767168 | bytes 6291472 | tf_op jit(solution)/shard_map/cond/branch_0_fun/convert_element_type | solution.py:86
  204.1 0.1 copy.152
  204.2 0.1 pad_maximum_fusion.1
  204.3 1.0 copy-done.4
  (32 shorter events, 0.1 us)
Async XLA Ops:
  0.6 18.7 %copy-start = (bf16[4,2,256,256]{3,2,1,0:T(8,128)(2,1)S(1)}, bf16[4,2,256,256]{3,2,1,0:T(8,128)(2,1)}, u32[]{:S(2)}) copy-start(bf16[4,2,256,256]{3,2,1,0:T(8,128)(2,1)} %param.10) | copy-start | bytes 3145732
  2.6 39.1 %collective-permute-start.23 = (bf16[1,1,256,256]{2,3,0,1:T(8,128)(2,1)}, bf16[1,1,256,256]{2,3,0,1:T(8,128)(2,1)S(1)}, u32[]{:S(2)}, u32[]{:S(2)}) collective-permute-start(bf16[1,1,256,256]{2,3,0,1:T(8,128)(2,1)} %copy.166), channel_id=1, source_target_pairs={{32,0},{33,1},{34,2},{35,3},{36,4},{37,5},{38,6},{39,7},{40,8},{41... | collective-permute-start | bytes 393224 | tf_op jit(solution)/shard_map/ppermute | solution.py:23
  4.7 32.4 %collective-permute-start.18 = (bf16[1,1,256,256]{2,3,0,1:T(8,128)(2,1)}, bf16[1,1,256,256]{2,3,0,1:T(8,128)(2,1)}, u32[]{:S(2)}, u32[]{:S(2)}) collective-permute-start(bf16[1,1,256,256]{2,3,0,1:T(8,128)(2,1)} %copy.157), channel_id=1, source_target_pairs={{0,32},{1,33},{2,34},{3,35},{4,36},{5,37},{6,38},{7,39},{8,40},{9,... | collective-permute-start | bytes 393224 | tf_op jit(solution)/shard_map/ppermute | solution.py:23
  12.3 16.3 %copy-start.1 = (bf16[2,4,256,256]{3,2,1,0:T(8,128)(2,1)S(1)}, bf16[2,4,256,256]{3,2,1,0:T(8,128)(2,1)}, u32[]{:S(2)}) copy-start(bf16[2,4,256,256]{3,2,1,0:T(8,128)(2,1)} %param.12) | copy-start | bytes 3145732
  12.3 26.0 %collective-permute-start.19 = (bf16[1,1,256,256]{2,3,0,1:T(8,128)(2,1)}, bf16[1,1,256,256]{2,3,0,1:T(8,128)(2,1)}, u32[]{:S(2)}, u32[]{:S(2)}) collective-permute-start(bf16[1,1,256,256]{2,3,0,1:T(8,128)(2,1)} %copy.158), channel_id=1, source_target_pairs={{1,32},{2,33},{3,34},{4,35},{5,36},{6,37},{7,38},{8,39},{9,40},{10... | collective-permute-start | bytes 393224 | tf_op jit(solution)/shard_map/ppermute | solution.py:23
  22.2 16.2 %collective-permute-start.20 = (bf16[3,1,256,256]{2,3,0,1:T(8,128)(2,1)}, bf16[3,1,256,256]{2,3,0,1:T(8,128)(2,1)}, u32[]{:S(2)}, u32[]{:S(2)}) collective-permute-start(bf16[3,1,256,256]{2,3,0,1:T(8,128)(2,1)} %copy.160), channel_id=1, source_target_pairs={{1,0},{2,1},{3,2},{4,3},{5,4},{6,5},{7,6},{8,7},{9,8},{10,9},{11,1... | collective-permute-start | bytes 1179656 | tf_op jit(solution)/shard_map/ppermute | solution.py:23
  25.0 20.7 %collective-permute-start.21 = (bf16[3,1,256,256]{2,3,0,1:T(8,128)(2,1)}, bf16[3,1,256,256]{2,3,0,1:T(8,128)(2,1)}, u32[]{:S(2)}, u32[]{:S(2)}) collective-permute-start(bf16[3,1,256,256]{2,3,0,1:T(8,128)(2,1)} %copy.163), channel_id=1, source_target_pairs={{0,1},{1,2},{2,3},{3,4},{4,5},{5,6},{6,7},{7,8},{8,9},{9,10},{10,1... | collective-permute-start | bytes 1179656 | tf_op jit(solution)/shard_map/ppermute | solution.py:23
  31.9 3.3 %copy-start.7 = (f32[4,2]{0,1:T(2,128)S(1)}, f32[4,2]{0,1:T(2,128)}, u32[]{:S(2)}) copy-start(f32[4,2]{0,1:T(2,128)} %param.13) | copy-start | bytes 100
  37.0 8.0 %collective-permute-start.22 = (bf16[1,1,256,256]{2,3,0,1:T(8,128)(2,1)}, bf16[1,1,256,256]{2,3,0,1:T(8,128)(2,1)S(1)}, u32[]{:S(2)}, u32[]{:S(2)}) collective-permute-start(bf16[1,1,256,256]{2,3,0,1:T(8,128)(2,1)} %copy.165), channel_id=1, source_target_pairs={{32,1},{33,2},{34,3},{35,4},{36,5},{37,6},{38,7},{39,8},{40,9},{41... | collective-permute-start | bytes 393224 | tf_op jit(solution)/shard_map/ppermute | solution.py:23
  41.7 3.3 %copy-start.5 = (bf16[1,1,256,256]{2,3,0,1:T(8,128)(2,1)}, bf16[1,1,256,256]{2,3,0,1:T(8,128)(2,1)S(1)}, u32[]{:S(2)}) copy-start(bf16[1,1,256,256]{2,3,0,1:T(8,128)(2,1)S(1)} %collective-permute-done.23) | copy-start | bytes 393220
  45.0 0.6 copy-start.6
  54.4 19.1 %collective-permute-start.26 = (bf16[3,1,256,256]{3,2,0,1:T(8,128)(2,1)}, bf16[3,1,256,256]{3,2,0,1:T(8,128)(2,1)}, u32[]{:S(2)}, u32[]{:S(2)}) collective-permute-start(bf16[3,1,256,256]{3,2,0,1:T(8,128)(2,1)} %get-tuple-element.216), channel_id=1, source_target_pairs={{1,0},{2,1},{3,2},{4,3},{5,4},{6,5},{7,6},{8,7},{9,8},{10,9},{11,1... | collective-permute-start | bytes 1179656 | tf_op jit(solution)/shard_map/ppermute | solution.py:23
  57.1 15.0 %collective-permute-start.25 = (bf16[1,1,256,256]{3,2,0,1:T(8,128)(2,1)}, bf16[1,1,256,256]{3,2,0,1:T(8,128)(2,1)}, u32[]{:S(2)}, u32[]{:S(2)}) collective-permute-start(bf16[1,1,256,256]{3,2,0,1:T(8,128)(2,1)} %get-tuple-element.220), channel_id=1, source_target_pairs={{1,32},{2,33},{3,34},{4,35},{5,36},{6,37},{7,38},{8,39},{9,40},{10... | collective-permute-start | bytes 393224 | tf_op jit(solution)/shard_map/ppermute | solution.py:23
  60.3 13.2 %collective-permute-start.24 = (bf16[1,1,256,256]{3,2,0,1:T(8,128)(2,1)}, bf16[1,1,256,256]{3,2,0,1:T(8,128)(2,1)}, u32[]{:S(2)}, u32[]{:S(2)}) collective-permute-start(bf16[1,1,256,256]{3,2,0,1:T(8,128)(2,1)} %get-tuple-element.221), channel_id=1, source_target_pairs={{0,32},{1,33},{2,34},{3,35},{4,36},{5,37},{6,38},{7,39},{8,40},{9,... | collective-permute-start | bytes 393224 | tf_op jit(solution)/shard_map/ppermute | solution.py:23
  62.9 18.1 %collective-permute-start.27 = (bf16[3,1,256,256]{3,2,0,1:T(8,128)(2,1)}, bf16[3,1,256,256]{3,2,0,1:T(8,128)(2,1)}, u32[]{:S(2)}, u32[]{:S(2)}) collective-permute-start(bf16[3,1,256,256]{3,2,0,1:T(8,128)(2,1)} %get-tuple-element.214), channel_id=1, source_target_pairs={{0,1},{1,2},{2,3},{3,4},{4,5},{5,6},{6,7},{7,8},{8,9},{9,10},{10,1... | collective-permute-start | bytes 1179656 | tf_op jit(solution)/shard_map/ppermute | solution.py:23
  70.9 8.1 %collective-permute-start.28 = (bf16[1,1,256,256]{3,2,0,1:T(8,128)(2,1)}, bf16[1,1,256,256]{3,2,0,1:T(8,128)(2,1)}, u32[]{:S(2)}, u32[]{:S(2)}) collective-permute-start(bf16[1,1,256,256]{3,2,0,1:T(8,128)(2,1)} %get-tuple-element.218), channel_id=1, source_target_pairs={{32,1},{33,2},{34,3},{35,4},{36,5},{37,6},{38,7},{39,8},{40,9},{41... | collective-permute-start | bytes 393224 | tf_op jit(solution)/shard_map/ppermute | solution.py:23
  72.2 8.9 %collective-permute-start.29 = (bf16[1,1,256,256]{3,2,0,1:T(8,128)(2,1)}, bf16[1,1,256,256]{3,2,0,1:T(8,128)(2,1)}, u32[]{:S(2)}, u32[]{:S(2)}) collective-permute-start(bf16[1,1,256,256]{3,2,0,1:T(8,128)(2,1)} %get-tuple-element.219), channel_id=1, source_target_pairs={{32,0},{33,1},{34,2},{35,3},{36,4},{37,5},{38,6},{39,7},{40,8},{41... | collective-permute-start | bytes 393224 | tf_op jit(solution)/shard_map/ppermute | solution.py:23
  90.0 23.0 %collective-permute-start.32 = (bf16[3,1,256,256]{3,2,0,1:T(8,128)(2,1)}, bf16[3,1,256,256]{3,2,0,1:T(8,128)(2,1)}, u32[]{:S(2)}, u32[]{:S(2)}) collective-permute-start(bf16[3,1,256,256]{3,2,0,1:T(8,128)(2,1)} %get-tuple-element.208), channel_id=1, source_target_pairs={{1,0},{2,1},{3,2},{4,3},{5,4},{6,5},{7,6},{8,7},{9,8},{10,9},{11,1... | collective-permute-start | bytes 1179656 | tf_op jit(solution)/shard_map/ppermute | solution.py:23
  94.3 17.4 %collective-permute-start.31 = (bf16[1,1,256,256]{3,2,0,1:T(8,128)(2,1)}, bf16[1,1,256,256]{3,2,0,1:T(8,128)(2,1)}, u32[]{:S(2)}, u32[]{:S(2)}) collective-permute-start(bf16[1,1,256,256]{3,2,0,1:T(8,128)(2,1)} %get-tuple-element.212), channel_id=1, source_target_pairs={{1,32},{2,33},{3,34},{4,35},{5,36},{6,37},{7,38},{8,39},{9,40},{10... | collective-permute-start | bytes 393224 | tf_op jit(solution)/shard_map/ppermute | solution.py:23
  99.9 13.1 %collective-permute-start.30 = (bf16[1,1,256,256]{3,2,0,1:T(8,128)(2,1)}, bf16[1,1,256,256]{3,2,0,1:T(8,128)(2,1)}, u32[]{:S(2)}, u32[]{:S(2)}) collective-permute-start(bf16[1,1,256,256]{3,2,0,1:T(8,128)(2,1)} %get-tuple-element.213), channel_id=1, source_target_pairs={{0,32},{1,33},{2,34},{3,35},{4,36},{5,37},{6,38},{7,39},{8,40},{9,... | collective-permute-start | bytes 393224 | tf_op jit(solution)/shard_map/ppermute | solution.py:23
  103.0 17.7 %collective-permute-start.33 = (bf16[3,1,256,256]{3,2,0,1:T(8,128)(2,1)}, bf16[3,1,256,256]{3,2,0,1:T(8,128)(2,1)}, u32[]{:S(2)}, u32[]{:S(2)}) collective-permute-start(bf16[3,1,256,256]{3,2,0,1:T(8,128)(2,1)} %get-tuple-element.206), channel_id=1, source_target_pairs={{0,1},{1,2},{2,3},{3,4},{4,5},{5,6},{6,7},{7,8},{8,9},{9,10},{10,1... | collective-permute-start | bytes 1179656 | tf_op jit(solution)/shard_map/ppermute | solution.py:23
  110.4 8.1 %collective-permute-start.34 = (bf16[1,1,256,256]{3,2,0,1:T(8,128)(2,1)}, bf16[1,1,256,256]{3,2,0,1:T(8,128)(2,1)}, u32[]{:S(2)}, u32[]{:S(2)}) collective-permute-start(bf16[1,1,256,256]{3,2,0,1:T(8,128)(2,1)} %get-tuple-element.210), channel_id=1, source_target_pairs={{32,1},{33,2},{34,3},{35,4},{36,5},{37,6},{38,7},{39,8},{40,9},{41... | collective-permute-start | bytes 393224 | tf_op jit(solution)/shard_map/ppermute | solution.py:23
  111.7 9.0 %collective-permute-start.35 = (bf16[1,1,256,256]{3,2,0,1:T(8,128)(2,1)}, bf16[1,1,256,256]{3,2,0,1:T(8,128)(2,1)}, u32[]{:S(2)}, u32[]{:S(2)}) collective-permute-start(bf16[1,1,256,256]{3,2,0,1:T(8,128)(2,1)} %get-tuple-element.211), channel_id=1, source_target_pairs={{32,0},{33,1},{34,2},{35,3},{36,4},{37,5},{38,6},{39,7},{40,8},{41... | collective-permute-start | bytes 393224 | tf_op jit(solution)/shard_map/ppermute | solution.py:23
  120.7 32.4 %copy-start.8 = (s32[2]{0:T(128)S(1)}, s32[2]{0:T(128)}, u32[]{:S(2)}) copy-start(s32[2]{0:T(128)} %param.14) | copy-start | bytes 28
  120.7 34.4 %copy-start.9 = (s32[2]{0:T(128)S(1)}, s32[2]{0:T(128)}, u32[]{:S(2)}) copy-start(s32[2]{0:T(128)} %param.15) | copy-start | bytes 28
  136.5 29.5 %all-to-all-start = ((f32[256,1,128]{2,1,0:T(1,128)}), f32[256,1,128]{2,1,0:T(1,128)S(1)}, u32[]{:S(2)}, u32[]{:S(2)}) async-start(f32[256,1,128]{2,1,0:T(1,128)} %broadcast_in_dim.5), calls=%async_computation | async-start | bytes 262144 | tf_op jit(solution)/shard_map/all_to_all | solution.py:94
  204.2 1.0 copy-start.4
  204.3 1.0 copy-start.10

commit v2 on v1

--- a/solution.py
+++ b/solution.py
@@ -1,6 +1,8 @@
 import jax
 import jax.numpy as jnp
 from jax import lax
+from jax.experimental import pallas as pl
+from jax.experimental.pallas import tpu as pltpu
 from jax.sharding import PartitionSpec as P
 
 DIAG = 2
@@ -87,14 +89,155 @@
     return (vec, jnp.stack(thetas))
 
 
-def gather_sum(parts):
-    devices = lax.axis_size("lsec") * lax.axis_size("rsec")
-    row = jnp.zeros((1, 128), jnp.float32).at[0, : parts.shape[0]].set(parts)
-    sent = jnp.broadcast_to(row[None], (devices, 1, 128))
-    return jnp.sum(lax.all_to_all(sent, AXES, 0, 0), axis=(0, 1))
-
-
-def recursion(gram, coef_num, coef_den):
+ROWS, COLS, BLOCKS = 4, 2, 8
+SUMS = 10
+VMEM = pl.BlockSpec(memory_space=pltpu.VMEM)
+SMEM = pl.BlockSpec(memory_space=pltpu.SMEM)
+PARAMS = pltpu.CompilerParams(vmem_limit_bytes=40 * 1024 * 1024)
+
+
+def dot(left, right):
+    return lax.dot_general(
+        left, right, (((1,), (0,)), ((), ())), preferred_element_type=jnp.float32
+    )
+
+
+def dot_t(left, right):
+    return lax.dot_general(
+        left, right, (((1,), (1,)), ((), ())), preferred_element_type=jnp.float32
+    )
+
+
+def not_at(place):
+    return (lax.axis_index("rsec") != place).astype(jnp.float32)
+
+
+def masked(block, keep):
+    return (block.astype(jnp.float32) * keep).astype(jnp.bfloat16)
+
+
+def pack_kernel(last, psi_ref, right_ref, energy_ref, pack_ref, left_out, up_out, corner_out, low_out):
+    size = psi_ref.shape[-1]
+    inner = not_at(last)
+    for place in range(2):
+        pack_ref[place * size : (place + 1) * size] = masked(psi_ref[place + 1, 1], inner)
+        left_out[place] = psi_ref[place, 0]
+    pack_ref[2 * size : 3 * size] = psi_ref[3, 1]
+    for term in range(4):
+        pack_ref[(3 + term) * size : (4 + term) * size] = right_ref[1, term]
+    rest = jnp.full((16, size), energy_ref[3, 1], jnp.float32)
+    for place in range(3):
+        part = rest.astype(jnp.bfloat16)
+        start = 7 * size + 16 * place
+        pack_ref[start : start + 16] = part
+        rest = rest - part.astype(jnp.float32)
+    up_out[0] = psi_ref[3, 1]
+    corner_out[0] = psi_ref[3, 0]
+    low_out[0] = psi_ref[0, 0]
+    low_out[1] = masked(psi_ref[0, 1], inner)
+
+
+def place_in(row, lane, value):
+    lanes = lax.broadcasted_iota(jnp.int32, row.shape, row.ndim - 1)
+    return jnp.where(lanes == lane, value, row)
+
+
+def step_kernel(step, last, *refs):
+    energy_ref, left_ref, right_ref, psi_ref, pack_ref, *refs = refs
+    size = psi_ref.shape[-1]
+    if step == 0:
+        from_right, from_up, from_corner, from_low, *refs = refs
+    else:
+        sums_in, *refs = refs
+        vecs, refs = refs[:step], refs[step:]
+        from_right, from_left, from_top, from_low, *refs = refs
+    if step < ITERS - 1:
+        new_ref, to_left, to_right, to_top, to_low, sums_ref = refs
+    else:
+        new_ref, back_ref, sums_ref = refs
+    first_keep, last_keep = not_at(0), not_at(last)
+
+    def start_block(k):
+        if k == 6:
+            return pack_ref[2 * size : 3 * size]
+        return psi_ref[k // 2, k % 2] if k < 6 else psi_ref[3, 0]
+
+    def own(k):
+        return start_block(k) if step == 0 else vecs[-1][k]
+
+    def left_halo(place):
+        return pack_ref[place * size : (place + 1) * size] if step == 0 else from_left[place]
+
+    def top_halo(place):
+        if step == 0:
+            return (from_up, from_corner)[place][0]
+        return from_top[place]
+
+    def sources(k):
+        plus = {0: lambda: top_halo(0), 1: lambda: top_halo(1), 2: lambda: own(1), 3: lambda: from_right[0],
+                4: lambda: own(3), 5: lambda: from_right[1], 6: lambda: own(4), 7: lambda: own(5)}[k]()
+        minus = {0: lambda: left_halo(0), 1: lambda: own(2), 2: lambda: left_halo(1), 3: lambda: own(4),
+                 4: lambda: own(6), 5: lambda: own(7), 6: lambda: from_low[0], 7: lambda: from_low[1]}[k]()
+        return [own(k)] * DIAG + [plus, minus]
+
+    def right_block(k, term):
+        if k == 6:
+            return pack_ref[(3 + term) * size : (4 + term) * size]
+        return right_ref[k % 2 if k < 6 else 0, term]
+
+    totals = [jnp.zeros((8, size), jnp.float32) for _ in range(step + 2 + (step == 0))]
+
+    def add_product(place, one, other):
+        product = one * other
+        totals[place] = totals[place] + jnp.sum(product.reshape(size // 8, 8, size), axis=0)
+
+    for k in range(BLOCKS):
+        if k == 6:
+            energy = sum(
+                pack_ref[7 * size + 16 * place : 7 * size + 16 * place + 16].astype(jnp.float32)
+                for place in range(3)
+            )[:1]
+        else:
+            energy = energy_ref[k // 2, k % 2] if k < 6 else energy_ref[3, 0]
+        total = (energy - SHIFT) * own(k).astype(jnp.float32)
+        for term, source in enumerate(sources(k)):
+            inner = dot(left_ref[k // 2, term], source)
+            if (k, term) in ((6, DIAG), (4, DIAG + HOPS)):
+                inner = inner * first_keep
+            total = total + dot_t(inner.astype(jnp.bfloat16), right_block(k, term))
+        image = total.astype(jnp.bfloat16)
+        new_ref[k] = image
+        vals = image.astype(jnp.float32)
+        start_vals = start_block(k).astype(jnp.float32)
+        if step == 0:
+            add_product(0, start_vals, start_vals)
+            add_product(1, start_vals, vals)
+            add_product(2, vals, vals)
+        else:
+            add_product(0, start_vals, vals)
+            for place, vec in enumerate(vecs):
+                add_product(place + 1, vec[k].astype(jnp.float32), vals)
+            add_product(step + 1, vals, vals)
+        if step < ITERS - 1:
+            for place, out, slot, keep in (
+                (0, to_left, 0, None), (2, to_left, 1, None), (3, to_right, 0, None), (5, to_right, 1, None),
+                (6, to_top, 0, None), (7, to_top, 1, first_keep), (0, to_low, 0, None), (1, to_low, 1, last_keep),
+            ):
+                if place == k:
+                    out[slot] = image if keep is None else masked(image, keep)
+        elif k == 6:
+            for place, vec in enumerate(vecs):
+                back_ref[place] = vec[k]
+            back_ref[step] = image
+    row = jnp.zeros((1, 128), jnp.float32) if step == 0 else sums_in[0:1]
+    start = {0: 0, 1: 3, 2: 6}[step]
+    for place, total in enumerate(totals):
+        value = jnp.sum(jnp.sum(total, axis=0, keepdims=True), axis=1, keepdims=True)
+        row = place_in(row, start + place, value)
+    sums_ref[...] = jnp.broadcast_to(row, sums_ref.shape)
+
+
+def recursion(gram, coefs):
     def quad(left, right):
         return sum(
             left[i] * right[j] * gram[min(i, j)][max(i, j)]
@@ -104,57 +247,143 @@
 
     scale = lax.rsqrt(gram[0][0] + eps)
     vec, previous = [scale], []
-    thetas, fine = [], jnp.bool_(True)
+    thetas, fine = [], jnp.ones_like(scale)
     for step in range(ITERS):
-        moved = [jnp.float32(0.0)] + vec
+        moved = [jnp.zeros_like(scale)] + vec
         theta = quad(vec, [SHIFT * entry for entry in vec]) + quad(vec, moved)
         thetas.append(theta)
-        coef = coefficient(coef_num, coef_den, step)
         resid = list(moved)
         for i, entry in enumerate(vec):
             resid[i] = resid[i] + (SHIFT - theta) * entry
         for i, entry in enumerate(previous):
-            resid[i] = resid[i] - coef * entry
+            resid[i] = resid[i] - coefs[step] * entry
         norm_sq = quad(resid, resid)
         lead = resid[-1]
-        fine = fine & (lead * lead * gram[step + 1][step + 1] <= SHRINK * (norm_sq + eps))
+        held = lead * lead * gram[step + 1][step + 1] <= SHRINK * (norm_sq + eps)
+        fine = jnp.where(held, fine, 0.0)
         norm = lax.rsqrt(jnp.maximum(norm_sq, 0.0) + eps)
         previous = vec
         vec = [entry * norm for entry in resid]
     return vec, thetas, fine
 
 
-def per_device(psi, left_env, right_env, energies, coef_num, coef_den):
-    count = 1.0 / float(psi.size * lax.axis_size("lsec") * lax.axis_size("rsec"))
-    basis = [psi]
-    parts = [jnp.sum(psi.astype(jnp.float32) ** 2)]
-    for step in range(ITERS):
-        image = matvec(basis[-1], left_env, right_env, energies - SHIFT)
-        if step < ITERS - 1:
-            image = image.astype(jnp.bfloat16)
-        basis.append(image)
-        vals = image.astype(jnp.float32)
-        for other in basis:
-            parts.append(jnp.sum(vals * other.astype(jnp.float32)))
-    sums = gather_sum(jnp.stack(parts) * count)
+def combine_kernel(count, num_ref, den_ref, sums_ref, psi_ref, one_ref, two_ref, three_ref, back_ref, out_ref, row_ref):
+    sums = jnp.sum(sums_ref[...], axis=0, keepdims=True) * count
+    lanes = lax.broadcasted_iota(jnp.int32, sums.shape, 1)
+    entries = [
+        jnp.sum(jnp.where(lanes == place, sums, 0.0), axis=1, keepdims=True) for place in range(SUMS)
+    ]
     gram = [[None] * (ITERS + 1) for _ in range(ITERS + 1)]
     place = 0
     for right in range(ITERS + 1):
         for left in range(right + 1):
-            gram[left][right] = sums[place]
+            gram[left][right] = entries[place]
             place += 1
-    weights, thetas, fine = recursion(gram, coef_num, coef_den)
-
-    def combine():
-        total = weights[0] * psi.astype(jnp.float32)
-        for weight, vec in zip(weights[1:], basis[1:]):
-            total = total + weight * vec.astype(jnp.float32)
-        return total.astype(jnp.bfloat16), jnp.stack(thetas)
-
-    def again():
-        return stepwise(psi, left_env, right_env, energies, coef_num, coef_den, count)
-
-    return lax.cond(fine, combine, again)
+    coefs = [jnp.zeros_like(entries[0])]
+    for step in range(ITERS - 1):
+        num = jnp.full(entries[0].shape, num_ref[step], jnp.int32).astype(jnp.float32)
+        den = jnp.full(entries[0].shape, den_ref[step], jnp.int32).astype(jnp.float32)
+        coefs.append(num / den)
+    weights, thetas, fine = recursion(gram, coefs)
+    row = jnp.zeros((1, 128), jnp.float32)
+    for place, value in enumerate(thetas + [fine]):
+        row = place_in(row, place, value)
+    row_ref[...] = row
+    for i in range(ROWS):
+        for j in range(COLS):
+            k = 2 * i + j + (i == 3)
+            blocks = [psi_ref[i, j]]
+            if k == 8:
+                blocks += [back_ref[0], back_ref[1], back_ref[2]]
+            else:
+                blocks += [one_ref[k], two_ref[k], three_ref[k]]
+            total = weights[0] * blocks[0].astype(jnp.float32)
+            for weight, block in zip(weights[1:], blocks[1:]):
+                total = total + weight * block.astype(jnp.float32)
+            out_ref[i, j] = total.astype(jnp.bfloat16)
+
+
+def move(block, down, right, around):
+    rows, cols = lax.axis_size("lsec"), lax.axis_size("rsec")
+    pairs = [
+        (row * cols + col, (row + down) * cols + (col + right) % cols)
+        for row in range(rows)
+        for col in range(cols)
+        if 0 <= row + down < rows and (around or 0 <= col + right < cols)
+    ]
+    return lax.ppermute(block, AXES, pairs)
+
+
+def call(kernel, in_specs, out_shapes, flops, *args):
+    nbytes = sum(a.size * a.dtype.itemsize for a in args)
+    nbytes += sum(s.size * s.dtype.itemsize for s in out_shapes)
+    return pl.pallas_call(
+        kernel,
+        in_specs=in_specs,
+        out_specs=[VMEM] * len(out_shapes),
+        out_shape=out_shapes,
+        compiler_params=PARAMS,
+        cost_estimate=pl.CostEstimate(flops=flops, bytes_accessed=nbytes, transcendentals=0),
+    )(*args)
+
+
+def per_device(psi, left_env, right_env, energies, coef_num, coef_den):
+    size = psi.shape[-1]
+    devices = lax.axis_size("lsec") * lax.axis_size("rsec")
+    last = lax.axis_size("rsec") - 1
+    count = 1.0 / float(psi.size * devices)
+
+    def blocks(number):
+        return jax.ShapeDtypeStruct((number, size, size), jnp.bfloat16)
+
+    pack, to_left, to_up, to_corner, to_low = call(
+        lambda *refs: pack_kernel(last, *refs),
+        [VMEM, VMEM, SMEM],
+        [jax.ShapeDtypeStruct((7 * size + 48, size), jnp.bfloat16), blocks(2), blocks(1), blocks(1), blocks(2)],
+        0, psi, right_env, energies,
+    )
+    pack = move(pack, 0, 1, True)
+    halos = [
+        move(to_left, 0, -1, False),
+        move(to_up, 1, 0, False),
+        move(to_corner, 1, -1, False),
+        move(to_low, -1, 1, True),
+    ]
+    fixed = [energies, left_env, right_env, psi, pack]
+    vecs, sums = [], []
+    for step in range(ITERS):
+        final = step == ITERS - 1
+        row = jax.ShapeDtypeStruct((devices if final else 8, 128), jnp.float32)
+        outs = [blocks(BLOCKS), blocks(ITERS), row] if final else [blocks(BLOCKS)] + [blocks(2)] * 4 + [row]
+        ins = fixed + sums + vecs + halos
+        result = call(
+            lambda *refs, step=step: step_kernel(step, last, *refs),
+            [SMEM] + [VMEM] * (len(ins) - 1), outs, 2 * 64 * size**3, *ins,
+        )
+        vecs.append(result[0])
+        sums = [result[-1]]
+        if not final:
+            to_left, to_right, to_top, to_low = result[1:5]
+            halos = [
+                move(to_left, 0, -1, False),
+                move(to_right, 0, 1, False),
+                move(to_top, 1, -1, True),
+                move(to_low, -1, 1, True),
+            ]
+    back = move(result[1], 0, -1, True)
+    gathered = lax.all_to_all(sums[0].reshape(devices, 1, 128), AXES, 0, 0).reshape(devices, 128)
+    vec, row = call(
+        lambda *refs: combine_kernel(count, *refs),
+        [SMEM, SMEM] + [VMEM] * 6,
+        [jax.ShapeDtypeStruct(psi.shape, jnp.bfloat16), jax.ShapeDtypeStruct((1, 128), jnp.float32)],
+        0, coef_num, coef_den, gathered, psi, *vecs, back,
+    )
+    thetas = row[0, :ITERS]
+    return lax.cond(
+        row[0, ITERS] > 0.5,
+        lambda: (vec, thetas),
+        lambda: stepwise(psi, left_env, right_env, energies, coef_num, coef_den, count),
+    )
 
 
 def solution(mesh):

time: 207 us -> 124 us (0.60)
  matrix products: 47.5 us -> 0 us
  between operations: 38.4 us -> 1.54 us
  local copies, waits for them, and re-layouts: 22.9 us -> 2.05 us
  Pallas kernels: 0 us -> 17.6 us
  waiting for transfers between devices: 20.1 us -> 37.6 us
  starting transfers between devices: 72.4 us -> 64.8 us
  other arithmetic: 3.73 us -> 0 us
    dot_general x12 -> x0, matrix products: 47.5 us -> none  [add_terms(): jnp.einsum('abik,blk->abil', inner, right_env[:, term], preferred_element...]
    pallas_call x0 -> x5, Pallas kernels: none -> 17.6 us  [call(): pl.pallas_call(kernel, in_specs=in_specs, out_specs=[VMEM] * len(out_shap...]
    ppermute x18 -> x14, waiting for transfers between devices: 11.2 us -> 24.7 us  [move(): return lax.ppermute(block, AXES, pairs)]
    ppermute x18 -> x14, starting transfers between devices: 55.7 us -> 47.4 us  [move(): return lax.ppermute(block, AXES, pairs)]
    slice x9 -> x1, local copies, waits for them, and re-layouts: 7.69 us -> 0.58 us  [per_device(): row[0, ITERS] > 0.5]
    another operation x2 -> x0, local copies, waits for them, and re-layouts: 6.61 us -> none  [the longest x1 6.54 us: per_device(): sums = gather_sum(jnp.stack(parts) * count)]
    unnamed x26 -> x21, local copies, waits for them, and re-layouts: 7.83 us -> 1.47 us
    all_to_all x1, waiting for transfers between devices: 8.86 us -> 12.9 us  [per_device(): lax.all_to_all(sums[0].reshape(devices, 1, 128), AXES, 0, 0)]
  transfers between devices with their start and end apart: 19 -> 15, of which waited for: 6 -> 7; matrix products, arithmetic and copies ran while one was open for 16% -> 0% of each run, Pallas kernels for 0% -> 0%
where the time goes in v2:
time: 124 us
  starting transfers between devices  64.8 us (52%)
  waiting for transfers between devices  37.6 us (30%)
  Pallas kernels  17.6 us (14%)
  local copies, waits for them, and re-layouts  2.05 us (2%)
  between operations  1.54 us (1%)
    ppermute x14, starting transfers between devices, move(): return lax.ppermute(block, AXES, pairs)  47.4 us
    ppermute x14, waiting for transfers between devices, move(): return lax.ppermute(block, AXES, pairs)  24.7 us
    pallas_call x5, Pallas kernels, call(): pl.pallas_call(kernel, in_specs=in_specs, out_specs=[VMEM] * len(out_shap...  17.6 us
    all_to_all x1, starting transfers between devices, per_device(): lax.all_to_all(sums[0].reshape(devices, 1, 128), AXES, 0, 0)  17.4 us
    all_to_all x1, waiting for transfers between devices, per_device(): lax.all_to_all(sums[0].reshape(devices, 1, 128), AXES, 0, 0)  12.9 us
  transfers between devices with their start and end apart: 15, of which 7 were waited for; matrix products, arithmetic and copies ran while one was open for 0% of the time, Pallas kernels for 0%

profile of v2, /device:TPU:1, one launch (start us, length us, event | category | flops | bytes accessed | tf_op | source)
XLA Modules:
  0.0 123.6 jit_solution(6750972696694191000)
XLA Ops:
  0.6 0.0 copy-start
  0.6 0.0 copy-start.7
  0.7 0.9 copy.23.refs_2_.refs_0_
  1.6 1.7 %shard_map.81 = (bf16[1840,256]{1,0:T(8,128)(2,1)S(1)}, bf16[2,256,256]{2,1,0:T(8,128)(2,1)S(1)}, bf16[1,256,256]{2,1,0:T(8,128)(2,1)S(1)}, bf16[1,256,256]{2,1,0:T(8,128)(2,1)S(1)}, bf16[2,256,256]{2,1,0:T(8,128)(2,1)S(1)}) custom-call(bf16[4,2,256,256]{3,2,1,0:T(8,128)(2,1)} %refs_3_.7, bf16[2,4,256,256]{3,2,1,0:T(8,128)(2,1)} %refs_2_.6, ...), custom_call_target="tpu_custom_call" | custom-call | bytes 3825696 | tf_op jit(solution)/shard_map/pallas_call | solution.py:320
  3.2 2.8 %collective-permute-start.18 = (bf16[1840,256]{1,0:T(8,128)(2,1)S(1)}, bf16[1840,256]{1,0:T(8,128)(2,1)S(1)}, u32[]{:S(2)}, u32[]{:S(2)}) collective-permute-start(bf16[1840,256]{1,0:T(8,128)(2,1)S(1)} %get-tuple-element.52), channel_id=1, source_target_pairs={{0,1},{1,2},{2,3},{3,4},{4,5},{5,6},{6,7},{7,8},{8,9},{9,10},{10,1... | collective-permute-start | bytes 2826248 | tf_op jit(solution)/shard_map/ppermute | solution.py:314
  6.0 2.5 %collective-permute-start.19 = (bf16[2,256,256]{2,1,0:T(8,128)(2,1)S(1)}, bf16[2,256,256]{2,1,0:T(8,128)(2,1)S(1)}, u32[]{:S(2)}, u32[]{:S(2)}) collective-permute-start(bf16[2,256,256]{2,1,0:T(8,128)(2,1)S(1)} %get-tuple-element.53), channel_id=1, source_target_pairs={{1,0},{2,1},{3,2},{4,3},{5,4},{6,5},{7,6},{8,7},{9,8},{10,9},{11,1... | collective-permute-start | bytes 786440 | tf_op jit(solution)/shard_map/ppermute | solution.py:314
  8.5 1.3 %collective-permute-start.22 = (bf16[2,256,256]{2,1,0:T(8,128)(2,1)S(1)}, bf16[2,256,256]{2,1,0:T(8,128)(2,1)S(1)}, u32[]{:S(2)}, u32[]{:S(2)}) collective-permute-start(bf16[2,256,256]{2,1,0:T(8,128)(2,1)S(1)} %get-tuple-element.56), channel_id=1, source_target_pairs={{32,1},{33,2},{34,3},{35,4},{36,5},{37,6},{38,7},{39,8},{40,9},{41... | collective-permute-start | bytes 786440 | tf_op jit(solution)/shard_map/ppermute | solution.py:314
  9.8 5.5 %collective-permute-start.20 = (bf16[1,256,256]{2,1,0:T(8,128)(2,1)S(1)}, bf16[1,256,256]{2,1,0:T(8,128)(2,1)S(1)}, u32[]{:S(2)}, u32[]{:S(2)}) collective-permute-start(bf16[1,256,256]{2,1,0:T(8,128)(2,1)S(1)} %get-tuple-element.54), channel_id=1, source_target_pairs={{0,32},{1,33},{2,34},{3,35},{4,36},{5,37},{6,38},{7,39},{8,40},{9,... | collective-permute-start | bytes 393224 | tf_op jit(solution)/shard_map/ppermute | solution.py:314
  15.3 0.0 copy-start.5
  15.3 0.0 copy-start.8
  15.3 5.7 %collective-permute-start.21 = (bf16[1,256,256]{2,1,0:T(8,128)(2,1)S(1)}, bf16[1,256,256]{2,1,0:T(8,128)(2,1)S(1)}, u32[]{:S(2)}, u32[]{:S(2)}) collective-permute-start(bf16[1,256,256]{2,1,0:T(8,128)(2,1)S(1)} %get-tuple-element.55), channel_id=1, source_target_pairs={{1,32},{2,33},{3,34},{4,35},{5,36},{6,37},{7,38},{8,39},{9,40},{10... | collective-permute-start | bytes 393224 | tf_op jit(solution)/shard_map/ppermute | solution.py:314
  21.0 4.4 %collective-permute-done.20.refs_6_ = bf16[1,256,256]{2,1,0:T(8,128)(2,1)S(1)} collective-permute-done((bf16[1,256,256]{2,1,0:T(8,128)(2,1)S(1)}, bf16[1,256,256]{2,1,0:T(8,128)(2,1)S(1)}, u32[]{:S(2)}, u32[]{:S(2)}) %collective-permute-start.20) | collective-permute-done | bytes 131104 | tf_op jit(solution)/shard_map/ppermute | solution.py:314
  25.4 3.1 %collective-permute-done.21.refs_7_ = bf16[1,256,256]{2,1,0:T(8,128)(2,1)S(1)} collective-permute-done((bf16[1,256,256]{2,1,0:T(8,128)(2,1)S(1)}, bf16[1,256,256]{2,1,0:T(8,128)(2,1)S(1)}, u32[]{:S(2)}, u32[]{:S(2)}) %collective-permute-start.21) | collective-permute-done | bytes 131104 | tf_op jit(solution)/shard_map/ppermute | solution.py:314
  28.4 0.0 collective-permute-done.19.refs_5_
  28.4 0.0 collective-permute-done.22.refs_8_
  28.4 0.0 collective-permute-done.18.refs_4_
  28.4 0.0 copy-done
  28.5 0.0 copy-done.7
  28.5 4.3 %shard_map.82 = (bf16[8,256,256]{2,1,0:T(8,128)(2,1)S(1)}, bf16[2,256,256]{2,1,0:T(8,128)(2,1)S(1)}, bf16[2,256,256]{2,1,0:T(8,128)(2,1)S(1)}, bf16[2,256,256]{2...) custom-call(f32[4,2]{1,0:T(4,128)S(1)} %copy.23.refs_2_.refs_0_, ...), custom_call_target="tpu_custom_call" | custom-call | flops 2147483648 | bytes 8024096 | tf_op jit(solution)/shard_map/pallas_call | solution.py:320
  32.7 1.9 %collective-permute-start.23 = (bf16[2,256,256]{2,1,0:T(8,128)(2,1)S(1)}, bf16[2,256,256]{2,1,0:T(8,128)(2,1)S(1)}, u32[]{:S(2)}, u32[]{:S(2)}) collective-permute-start(bf16[2,256,256]{2,1,0:T(8,128)(2,1)S(1)} %get-tuple-element.59), channel_id=1, source_target_pairs={{1,0},{2,1},{3,2},{4,3},{5,4},{6,5},{7,6},{8,7},{9,8},{10,9},{11,1... | collective-permute-start | bytes 786440 | tf_op jit(solution)/shard_map/ppermute | solution.py:314
  34.6 4.1 %collective-permute-start.24 = (bf16[2,256,256]{2,1,0:T(8,128)(2,1)S(1)}, bf16[2,256,256]{2,1,0:T(8,128)(2,1)S(1)}, u32[]{:S(2)}, u32[]{:S(2)}) collective-permute-start(bf16[2,256,256]{2,1,0:T(8,128)(2,1)S(1)} %get-tuple-element.60), channel_id=1, source_target_pairs={{0,1},{1,2},{2,3},{3,4},{4,5},{5,6},{6,7},{7,8},{8,9},{9,10},{10,1... | collective-permute-start | bytes 786440 | tf_op jit(solution)/shard_map/ppermute | solution.py:314
  38.8 5.0 %collective-permute-start.25 = (bf16[2,256,256]{2,1,0:T(8,128)(2,1)S(1)}, bf16[2,256,256]{2,1,0:T(8,128)(2,1)S(1)}, u32[]{:S(2)}, u32[]{:S(2)}) collective-permute-start(bf16[2,256,256]{2,1,0:T(8,128)(2,1)S(1)} %get-tuple-element.61), channel_id=1, source_target_pairs={{0,63},{1,32},{2,33},{3,34},{4,35},{5,36},{6,37},{7,38},{8,39},{9,... | collective-permute-start | bytes 786440 | tf_op jit(solution)/shard_map/ppermute | solution.py:314
  43.8 1.3 %collective-permute-start.26 = (bf16[2,256,256]{2,1,0:T(8,128)(2,1)S(1)}, bf16[2,256,256]{2,1,0:T(8,128)(2,1)S(1)}, u32[]{:S(2)}, u32[]{:S(2)}) collective-permute-start(bf16[2,256,256]{2,1,0:T(8,128)(2,1)S(1)} %get-tuple-element.62), channel_id=1, source_target_pairs={{32,1},{33,2},{34,3},{35,4},{36,5},{37,6},{38,7},{39,8},{40,9},{41... | collective-permute-start | bytes 786440 | tf_op jit(solution)/shard_map/ppermute | solution.py:314
  45.1 0.0 collective-permute-done.23.refs_7_
  45.1 0.0 collective-permute-done.24.refs_8_
  45.1 2.0 %collective-permute-done.25.refs_9_ = bf16[2,256,256]{2,1,0:T(8,128)(2,1)S(1)} collective-permute-done((bf16[2,256,256]{2,1,0:T(8,128)(2,1)S(1)}, bf16[2,256,256]{2,1,0:T(8,128)(2,1)S(1)}, u32[]{:S(2)}, u32[]{:S(2)}) %collective-permute-start.25) | collective-permute-done | bytes 262176 | tf_op jit(solution)/shard_map/ppermute | solution.py:314
  47.1 6.2 %collective-permute-done.26.refs_10_ = bf16[2,256,256]{2,1,0:T(8,128)(2,1)S(1)} collective-permute-done((bf16[2,256,256]{2,1,0:T(8,128)(2,1)S(1)}, bf16[2,256,256]{2,1,0:T(8,128)(2,1)S(1)}, u32[]{:S(2)}, u32[]{:S(2)}) %collective-permute-start.26) | collective-permute-done | bytes 262176 | tf_op jit(solution)/shard_map/ppermute | solution.py:314
  53.3 0.0 copy-done.5
  53.3 0.0 copy-done.8
  53.3 0.0 copy-start.1
  53.3 3.5 %shard_map.83 = (bf16[8,256,256]{2,1,0:T(8,128)(2,1)S(1)}, bf16[2,256,256]{2,1,0:T(8,128)(2,1)S(1)}, bf16[2,256,256]{2,1,0:T(8,128)(2,1)S(1)}, bf16[2,256,256]{2...) custom-call(f32[4,2]{1,0:T(4,128)S(1)} %copy.23.refs_2_.refs_0_, ...), custom_call_target="tpu_custom_call" | custom-call | flops 2147483648 | bytes 9338912 | tf_op jit(solution)/shard_map/pallas_call | solution.py:320
  56.8 5.8 %collective-permute-start.27 = (bf16[2,256,256]{2,1,0:T(8,128)(2,1)S(1)}, bf16[2,256,256]{2,1,0:T(8,128)(2,1)S(1)}, u32[]{:S(2)}, u32[]{:S(2)}) collective-permute-start(bf16[2,256,256]{2,1,0:T(8,128)(2,1)S(1)} %get-tuple-element.65), channel_id=1, source_target_pairs={{1,0},{2,1},{3,2},{4,3},{5,4},{6,5},{7,6},{8,7},{9,8},{10,9},{11,1... | collective-permute-start | bytes 786440 | tf_op jit(solution)/shard_map/ppermute | solution.py:314
  62.6 1.9 %collective-permute-start.28 = (bf16[2,256,256]{2,1,0:T(8,128)(2,1)S(1)}, bf16[2,256,256]{2,1,0:T(8,128)(2,1)S(1)}, u32[]{:S(2)}, u32[]{:S(2)}) collective-permute-start(bf16[2,256,256]{2,1,0:T(8,128)(2,1)S(1)} %get-tuple-element.66), channel_id=1, source_target_pairs={{0,1},{1,2},{2,3},{3,4},{4,5},{5,6},{6,7},{7,8},{8,9},{9,10},{10,1... | collective-permute-start | bytes 786440 | tf_op jit(solution)/shard_map/ppermute | solution.py:314
  64.5 5.1 %collective-permute-start.29 = (bf16[2,256,256]{2,1,0:T(8,128)(2,1)S(1)}, bf16[2,256,256]{2,1,0:T(8,128)(2,1)S(1)}, u32[]{:S(2)}, u32[]{:S(2)}) collective-permute-start(bf16[2,256,256]{2,1,0:T(8,128)(2,1)S(1)} %get-tuple-element.67), channel_id=1, source_target_pairs={{0,63},{1,32},{2,33},{3,34},{4,35},{5,36},{6,37},{7,38},{8,39},{9,... | collective-permute-start | bytes 786440 | tf_op jit(solution)/shard_map/ppermute | solution.py:314
  69.7 1.3 %collective-permute-start.30 = (bf16[2,256,256]{2,1,0:T(8,128)(2,1)S(1)}, bf16[2,256,256]{2,1,0:T(8,128)(2,1)S(1)}, u32[]{:S(2)}, u32[]{:S(2)}) collective-permute-start(bf16[2,256,256]{2,1,0:T(8,128)(2,1)S(1)} %get-tuple-element.68), channel_id=1, source_target_pairs={{32,1},{33,2},{34,3},{35,4},{36,5},{37,6},{38,7},{39,8},{40,9},{41... | collective-permute-start | bytes 786440 | tf_op jit(solution)/shard_map/ppermute | solution.py:314
  71.0 0.0 collective-permute-done.27.refs_8_
  71.0 0.0 collective-permute-done.28.refs_9_
  71.0 2.0 %collective-permute-done.29.refs_10_ = bf16[2,256,256]{2,1,0:T(8,128)(2,1)S(1)} collective-permute-done((bf16[2,256,256]{2,1,0:T(8,128)(2,1)S(1)}, bf16[2,256,256]{2,1,0:T(8,128)(2,1)S(1)}, u32[]{:S(2)}, u32[]{:S(2)}) %collective-permute-start.29) | collective-permute-done | bytes 262176 | tf_op jit(solution)/shard_map/ppermute | solution.py:314
  73.0 7.1 %collective-permute-done.30.refs_11_ = bf16[2,256,256]{2,1,0:T(8,128)(2,1)S(1)} collective-permute-done((bf16[2,256,256]{2,1,0:T(8,128)(2,1)S(1)}, bf16[2,256,256]{2,1,0:T(8,128)(2,1)S(1)}, u32[]{:S(2)}, u32[]{:S(2)}) %collective-permute-start.30) | collective-permute-done | bytes 262176 | tf_op jit(solution)/shard_map/ppermute | solution.py:314
  80.1 0.0 copy-done.1
  80.1 0.0 copy-start.12
  80.1 0.0 copy-start.13
  80.1 4.4 %shard_map.84 = (bf16[8,256,256]{2,1,0:T(8,128)(2,1)S(1)}, bf16[3,256,256]{2,1,0:T(8,128)(2,1)}, f32[256,128]{1,0:T(8,128)}) custom-call(f32[4,2]{1,0:T(4,128)S(1)} %copy.23.refs_2_.refs_0_, bf16[4,4,256,256]{3,2,1,0:T(8,128)(2,1)S(1)} %copy-done.5, bf16[2,4,256,256]{3,2,1,0:T(8,128)(2,1)S(1)} %copy-done.8, bf16[4,2,256,256]{3,2,1,0:T(8,128)(2,1)S(1)} %copy-done.1, ...), custom_call_target="tpu_custom_call" | custom-call | flops 2147483648 | bytes 9859104 | tf_op jit(solution)/shard_map/pallas_call | solution.py:320
  84.6 3.2 %collective-permute-start.31 = (bf16[3,256,256]{2,1,0:T(8,128)(2,1)}, bf16[3,256,256]{2,1,0:T(8,128)(2,1)}, u32[]{:S(2)}, u32[]{:S(2)}) collective-permute-start(bf16[3,256,256]{2,1,0:T(8,128)(2,1)} %get-tuple-element.71), channel_id=1, source_target_pairs={{0,31},{1,0},{2,1},{3,2},{4,3},{5,4},{6,5},{7,6},{8,7},{9,8},{10,9... | collective-permute-start | bytes 1179656 | tf_op jit(solution)/shard_map/ppermute | solution.py:314
  87.8 17.4 %all-to-all-start = ((f32[256,1,128]{2,1,0:T(1,128)}), f32[256,1,128]{2,1,0:T(1,128)S(1)}, u32[]{:S(2)}, u32[]{:S(2)}) async-start(f32[256,1,128]{2,1,0:T(1,128)} %bitcast.55), calls=%async_computation | async-start | bytes 262144 | tf_op jit(solution)/shard_map/all_to_all | solution.py:374
  105.2 12.9 %all-to-all-done = f32[256,1,128]{2,1,0:T(1,128)S(1)} async-done(((f32[256,1,128]{2,1,0:T(1,128)}), f32[256,1,128]{2,1,0:T(1,128)S(1)}, u32[]{:S(2)}, u32[]{:S(2)}) %all-to-all-start) | async-done | bytes 131104 | tf_op jit(solution)/shard_map/all_to_all | solution.py:374
  118.1 0.0 collective-permute-done.31.refs_7_
  118.1 0.0 copy-done.12
  118.1 0.0 copy-done.13
  118.1 0.0 copy-start.2
  118.1 0.0 copy-start.11
  118.1 3.7 %shard_map.85 = (bf16[4,2,256,256]{3,2,1,0:T(8,128)(2,1)}, f32[1,128]{1,0:T(1,128)S(1)}) custom-call(s32[2]{0:T(128)S(1)} %copy-done.12, s32[2]{0:T(128)S(1)} %copy-done.13, f32[256,128]{1,0:T(8,128)S(1)} %bitcast.184, bf16[4,2,256,256]{3,2,1,0:T(8,128)(2,1)} %refs_3_.7, bf16[8,256,256]{2,1,0:T(8,128)(2,1)S(1)} %get-tuple-element.58.refs_6_.refs_4_, ...), custom_call_target="tpu_custom_call" | custom-call | bytes 5767696 | tf_op jit(solution)/shard_map/pallas_call | solution.py:320
  121.8 0.6 slice.131
  123.0 0.0 copy-done.2
  123.0 0.0 copy-done.11
  123.1 0.0 copy-start.14
  123.1 0.5 copy-done.14
  (2 shorter events, 0.0 us)
Async XLA Ops:
  0.6 27.8 %copy-start = (bf16[4,2,256,256]{3,2,1,0:T(8,128)(2,1)S(1)}, bf16[4,2,256,256]{3,2,1,0:T(8,128)(2,1)}, u32[]{:S(2)}) copy-start(bf16[4,2,256,256]{3,2,1,0:T(8,128)(2,1)} %refs_3_.7) | copy-start | bytes 3145732
  0.6 27.8 %copy-start.7 = (bf16[2,4,256,256]{3,2,1,0:T(8,128)(2,1)S(1)}, bf16[2,4,256,256]{3,2,1,0:T(8,128)(2,1)}, u32[]{:S(2)}) copy-start(bf16[2,4,256,256]{3,2,1,0:T(8,128)(2,1)} %refs_2_.6) | copy-start | bytes 3145732
  3.2 25.2 %collective-permute-start.18 = (bf16[1840,256]{1,0:T(8,128)(2,1)S(1)}, bf16[1840,256]{1,0:T(8,128)(2,1)S(1)}, u32[]{:S(2)}, u32[]{:S(2)}) collective-permute-start(bf16[1840,256]{1,0:T(8,128)(2,1)S(1)} %get-tuple-element.52), channel_id=1, source_target_pairs={{0,1},{1,2},{2,3},{3,4},{4,5},{5,6},{6,7},{7,8},{8,9},{9,10},{10,1... | collective-permute-start | bytes 2826248 | tf_op jit(solution)/shard_map/ppermute | solution.py:314
  6.0 22.4 %collective-permute-start.19 = (bf16[2,256,256]{2,1,0:T(8,128)(2,1)S(1)}, bf16[2,256,256]{2,1,0:T(8,128)(2,1)S(1)}, u32[]{:S(2)}, u32[]{:S(2)}) collective-permute-start(bf16[2,256,256]{2,1,0:T(8,128)(2,1)S(1)} %get-tuple-element.53), channel_id=1, source_target_pairs={{1,0},{2,1},{3,2},{4,3},{5,4},{6,5},{7,6},{8,7},{9,8},{10,9},{11,1... | collective-permute-start | bytes 786440 | tf_op jit(solution)/shard_map/ppermute | solution.py:314
  8.5 19.9 %collective-permute-start.22 = (bf16[2,256,256]{2,1,0:T(8,128)(2,1)S(1)}, bf16[2,256,256]{2,1,0:T(8,128)(2,1)S(1)}, u32[]{:S(2)}, u32[]{:S(2)}) collective-permute-start(bf16[2,256,256]{2,1,0:T(8,128)(2,1)S(1)} %get-tuple-element.56), channel_id=1, source_target_pairs={{32,1},{33,2},{34,3},{35,4},{36,5},{37,6},{38,7},{39,8},{40,9},{41... | collective-permute-start | bytes 786440 | tf_op jit(solution)/shard_map/ppermute | solution.py:314
  9.8 15.6 %collective-permute-start.20 = (bf16[1,256,256]{2,1,0:T(8,128)(2,1)S(1)}, bf16[1,256,256]{2,1,0:T(8,128)(2,1)S(1)}, u32[]{:S(2)}, u32[]{:S(2)}) collective-permute-start(bf16[1,256,256]{2,1,0:T(8,128)(2,1)S(1)} %get-tuple-element.54), channel_id=1, source_target_pairs={{0,32},{1,33},{2,34},{3,35},{4,36},{5,37},{6,38},{7,39},{8,40},{9,... | collective-permute-start | bytes 393224 | tf_op jit(solution)/shard_map/ppermute | solution.py:314
  15.3 38.0 %copy-start.5 = (bf16[4,4,256,256]{3,2,1,0:T(8,128)(2,1)S(1)}, bf16[4,4,256,256]{3,2,1,0:T(8,128)(2,1)}, u32[]{:S(2)}) copy-start(bf16[4,4,256,256]{3,2,1,0:T(8,128)(2,1)} %refs_1_.8) | copy-start | bytes 6291460
  15.3 38.0 %copy-start.8 = (bf16[2,4,256,256]{3,2,1,0:T(8,128)(2,1)S(1)}, bf16[2,4,256,256]{3,2,1,0:T(8,128)(2,1)}, u32[]{:S(2)}) copy-start(bf16[2,4,256,256]{3,2,1,0:T(8,128)(2,1)} %refs_2_.6) | copy-start | bytes 3145732
  15.3 13.1 %collective-permute-start.21 = (bf16[1,256,256]{2,1,0:T(8,128)(2,1)S(1)}, bf16[1,256,256]{2,1,0:T(8,128)(2,1)S(1)}, u32[]{:S(2)}, u32[]{:S(2)}) collective-permute-start(bf16[1,256,256]{2,1,0:T(8,128)(2,1)S(1)} %get-tuple-element.55), channel_id=1, source_target_pairs={{1,32},{2,33},{3,34},{4,35},{5,36},{6,37},{7,38},{8,39},{9,40},{10... | collective-permute-start | bytes 393224 | tf_op jit(solution)/shard_map/ppermute | solution.py:314
  32.7 12.4 %collective-permute-start.23 = (bf16[2,256,256]{2,1,0:T(8,128)(2,1)S(1)}, bf16[2,256,256]{2,1,0:T(8,128)(2,1)S(1)}, u32[]{:S(2)}, u32[]{:S(2)}) collective-permute-start(bf16[2,256,256]{2,1,0:T(8,128)(2,1)S(1)} %get-tuple-element.59), channel_id=1, source_target_pairs={{1,0},{2,1},{3,2},{4,3},{5,4},{6,5},{7,6},{8,7},{9,8},{10,9},{11,1... | collective-permute-start | bytes 786440 | tf_op jit(solution)/shard_map/ppermute | solution.py:314
  34.6 10.5 %collective-permute-start.24 = (bf16[2,256,256]{2,1,0:T(8,128)(2,1)S(1)}, bf16[2,256,256]{2,1,0:T(8,128)(2,1)S(1)}, u32[]{:S(2)}, u32[]{:S(2)}) collective-permute-start(bf16[2,256,256]{2,1,0:T(8,128)(2,1)S(1)} %get-tuple-element.60), channel_id=1, source_target_pairs={{0,1},{1,2},{2,3},{3,4},{4,5},{5,6},{6,7},{7,8},{8,9},{9,10},{10,1... | collective-permute-start | bytes 786440 | tf_op jit(solution)/shard_map/ppermute | solution.py:314
  38.8 8.3 %collective-permute-start.25 = (bf16[2,256,256]{2,1,0:T(8,128)(2,1)S(1)}, bf16[2,256,256]{2,1,0:T(8,128)(2,1)S(1)}, u32[]{:S(2)}, u32[]{:S(2)}) collective-permute-start(bf16[2,256,256]{2,1,0:T(8,128)(2,1)S(1)} %get-tuple-element.61), channel_id=1, source_target_pairs={{0,63},{1,32},{2,33},{3,34},{4,35},{5,36},{6,37},{7,38},{8,39},{9,... | collective-permute-start | bytes 786440 | tf_op jit(solution)/shard_map/ppermute | solution.py:314
  43.8 9.5 %collective-permute-start.26 = (bf16[2,256,256]{2,1,0:T(8,128)(2,1)S(1)}, bf16[2,256,256]{2,1,0:T(8,128)(2,1)S(1)}, u32[]{:S(2)}, u32[]{:S(2)}) collective-permute-start(bf16[2,256,256]{2,1,0:T(8,128)(2,1)S(1)} %get-tuple-element.62), channel_id=1, source_target_pairs={{32,1},{33,2},{34,3},{35,4},{36,5},{37,6},{38,7},{39,8},{40,9},{41... | collective-permute-start | bytes 786440 | tf_op jit(solution)/shard_map/ppermute | solution.py:314
  53.3 26.8 %copy-start.1 = (bf16[4,2,256,256]{3,2,1,0:T(8,128)(2,1)S(1)}, bf16[4,2,256,256]{3,2,1,0:T(8,128)(2,1)}, u32[]{:S(2)}) copy-start(bf16[4,2,256,256]{3,2,1,0:T(8,128)(2,1)} %refs_3_.7) | copy-start | bytes 3145732
  56.8 14.2 %collective-permute-start.27 = (bf16[2,256,256]{2,1,0:T(8,128)(2,1)S(1)}, bf16[2,256,256]{2,1,0:T(8,128)(2,1)S(1)}, u32[]{:S(2)}, u32[]{:S(2)}) collective-permute-start(bf16[2,256,256]{2,1,0:T(8,128)(2,1)S(1)} %get-tuple-element.65), channel_id=1, source_target_pairs={{1,0},{2,1},{3,2},{4,3},{5,4},{6,5},{7,6},{8,7},{9,8},{10,9},{11,1... | collective-permute-start | bytes 786440 | tf_op jit(solution)/shard_map/ppermute | solution.py:314
  62.6 8.4 %collective-permute-start.28 = (bf16[2,256,256]{2,1,0:T(8,128)(2,1)S(1)}, bf16[2,256,256]{2,1,0:T(8,128)(2,1)S(1)}, u32[]{:S(2)}, u32[]{:S(2)}) collective-permute-start(bf16[2,256,256]{2,1,0:T(8,128)(2,1)S(1)} %get-tuple-element.66), channel_id=1, source_target_pairs={{0,1},{1,2},{2,3},{3,4},{4,5},{5,6},{6,7},{7,8},{8,9},{9,10},{10,1... | collective-permute-start | bytes 786440 | tf_op jit(solution)/shard_map/ppermute | solution.py:314
  64.5 8.5 %collective-permute-start.29 = (bf16[2,256,256]{2,1,0:T(8,128)(2,1)S(1)}, bf16[2,256,256]{2,1,0:T(8,128)(2,1)S(1)}, u32[]{:S(2)}, u32[]{:S(2)}) collective-permute-start(bf16[2,256,256]{2,1,0:T(8,128)(2,1)S(1)} %get-tuple-element.67), channel_id=1, source_target_pairs={{0,63},{1,32},{2,33},{3,34},{4,35},{5,36},{6,37},{7,38},{8,39},{9,... | collective-permute-start | bytes 786440 | tf_op jit(solution)/shard_map/ppermute | solution.py:314
  69.7 10.4 %collective-permute-start.30 = (bf16[2,256,256]{2,1,0:T(8,128)(2,1)S(1)}, bf16[2,256,256]{2,1,0:T(8,128)(2,1)S(1)}, u32[]{:S(2)}, u32[]{:S(2)}) collective-permute-start(bf16[2,256,256]{2,1,0:T(8,128)(2,1)S(1)} %get-tuple-element.68), channel_id=1, source_target_pairs={{32,1},{33,2},{34,3},{35,4},{36,5},{37,6},{38,7},{39,8},{40,9},{41... | collective-permute-start | bytes 786440 | tf_op jit(solution)/shard_map/ppermute | solution.py:314
  80.1 38.0 %copy-start.12 = (s32[2]{0:T(128)S(1)}, s32[2]{0:T(128)}, u32[]{:S(2)}) copy-start(s32[2]{0:T(128)} %refs_0_.6) | copy-start | bytes 28
  80.1 38.0 %copy-start.13 = (s32[2]{0:T(128)S(1)}, s32[2]{0:T(128)}, u32[]{:S(2)}) copy-start(s32[2]{0:T(128)} %refs_1_.9) | copy-start | bytes 28
  84.6 33.5 %collective-permute-start.31 = (bf16[3,256,256]{2,1,0:T(8,128)(2,1)}, bf16[3,256,256]{2,1,0:T(8,128)(2,1)}, u32[]{:S(2)}, u32[]{:S(2)}) collective-permute-start(bf16[3,256,256]{2,1,0:T(8,128)(2,1)} %get-tuple-element.71), channel_id=1, source_target_pairs={{0,31},{1,0},{2,1},{3,2},{4,3},{5,4},{6,5},{7,6},{8,7},{9,8},{10,9... | collective-permute-start | bytes 1179656 | tf_op jit(solution)/shard_map/ppermute | solution.py:314
  87.8 30.3 %all-to-all-start = ((f32[256,1,128]{2,1,0:T(1,128)}), f32[256,1,128]{2,1,0:T(1,128)S(1)}, u32[]{:S(2)}, u32[]{:S(2)}) async-start(f32[256,1,128]{2,1,0:T(1,128)} %bitcast.55), calls=%async_computation | async-start | bytes 262144 | tf_op jit(solution)/shard_map/all_to_all | solution.py:374
  118.1 4.9 %copy-start.2 = (bf16[4,2,256,256]{3,2,1,0:T(8,128)(2,1)S(1)}, bf16[4,2,256,256]{3,2,1,0:T(8,128)(2,1)}, u32[]{:S(2)}) copy-start(bf16[4,2,256,256]{3,2,1,0:T(8,128)(2,1)} %refs_3_.7) | copy-start | bytes 3145732
  118.1 4.9 %copy-start.11 = (f32[4,2]{0,1:T(2,128)S(1)}, f32[4,2]{0,1:T(2,128)}, u32[]{:S(2)}) copy-start(f32[4,2]{0,1:T(2,128)} %param.11) | copy-start | bytes 100
  123.1 0.5 copy-start.14

commit v3 on v2

--- a/solution.py
+++ b/solution.py
@@ -125,7 +125,7 @@
     pack_ref[2 * size : 3 * size] = psi_ref[3, 1]
     for term in range(4):
         pack_ref[(3 + term) * size : (4 + term) * size] = right_ref[1, term]
-    rest = jnp.full((16, size), energy_ref[3, 1], jnp.float32)
+    rest = jnp.full((16, size), energy_ref[1, 3], jnp.float32)
     for place in range(3):
         part = rest.astype(jnp.bfloat16)
         start = 7 * size + 16 * place
@@ -142,99 +142,169 @@
     return jnp.where(lanes == lane, value, row)
 
 
-def step_kernel(step, last, *refs):
-    energy_ref, left_ref, right_ref, psi_ref, pack_ref, *refs = refs
-    size = psi_ref.shape[-1]
+class Blocks:
+    def __init__(self, step, psi_ref, pack_ref, vec_ref, halo_refs):
+        self.step, self.psi_ref, self.pack_ref, self.vec_ref = step, psi_ref, pack_ref, vec_ref
+        self.size = psi_ref.shape[-1]
+        self.halo_refs = halo_refs
+
+    def packed(self, place):
+        return self.pack_ref[place * self.size : (place + 1) * self.size]
+
+    def start(self, k):
+        if k == 6:
+            return self.packed(2)
+        return self.psi_ref[k // 2, k % 2] if k < 6 else self.psi_ref[3, 0]
+
+    def own(self, k):
+        return self.start(k) if self.step == 0 else self.vec_ref[k]
+
+    def source(self, k, term):
+        if term < DIAG:
+            return self.own(k)
+        if term == DIAG:
+            halo = {0: (0, 0), 1: (0, 1), 3: (3, 0), 5: (3, 1)}
+            inside = {2: 1, 4: 3, 6: 4, 7: 5}
+        else:
+            halo = {0: (2, 0), 2: (2, 1), 6: (1, 0), 7: (1, 1)}
+            inside = {1: 2, 3: 4, 4: 6, 5: 7}
+        if k in inside:
+            return self.own(inside[k])
+        group, place = halo[k]
+        if self.step == 0 and group == 0:
+            return self.halo_refs[(0, 4)[place]][0]
+        if self.step == 0 and group == 2:
+            return self.packed(place)
+        return self.halo_refs[group][place]
+
+    def near(self, k, term):
+        if self.step == 0 and (k == 6 or (k, term) == (4, DIAG + HOPS)):
+            return False
+        if term < DIAG:
+            return True
+        return k in ((2, 4, 6, 7) if term == DIAG else (1, 3, 4, 5))
+
+    def term(self, k, term, left_ref, right_ref, first_keep):
+        inner = dot(left_ref[k // 2, term], self.source(k, term))
+        if (k, term) in ((6, DIAG), (4, DIAG + HOPS)):
+            inner = inner * first_keep
+        right = self.packed(3 + term) if k == 6 else right_ref[k % 2 if k < 6 else 0, term]
+        return dot_t(inner.astype(jnp.bfloat16), right)
+
+    def energy(self, k, energy_ref):
+        if k == 6:
+            start = 7 * self.size
+            parts = [self.pack_ref[start + 16 * i : start + 16 * i + 16].astype(jnp.float32) for i in range(3)]
+            return sum(parts)[:1] - SHIFT
+        return (energy_ref[k % 2, k // 2] if k < 6 else energy_ref[0, 3]) - SHIFT
+
+
+class Sums:
+    def __init__(self, number, size):
+        self.size = size
+        self.totals = [jnp.zeros((8, size), jnp.float32) for _ in range(number)]
+
+    def add(self, place, one, other):
+        product = (one * other).reshape(self.size // 8, 8, self.size)
+        self.totals[place] = self.totals[place] + jnp.sum(product, axis=0)
+
+    def write(self, row, first):
+        for place, total in enumerate(self.totals):
+            value = jnp.sum(jnp.sum(total, axis=0, keepdims=True), axis=1, keepdims=True)
+            row = place_in(row, first + place, value)
+        return row
+
+
+FIRST_SUM = (0, 1, 3, 6)
+
+
+def near_kernel(step, *refs):
+    energy_ref, left_ref, right_ref, psi_ref, *refs = refs
     if step == 0:
-        from_right, from_up, from_corner, from_low, *refs = refs
+        pack_ref, vecs, refs = None, [], refs
     else:
+        pack_ref, *refs = refs
         sums_in, *refs = refs
         vecs, refs = refs[:step], refs[step:]
-        from_right, from_left, from_top, from_low, *refs = refs
-    if step < ITERS - 1:
-        new_ref, to_left, to_right, to_top, to_low, sums_ref = refs
+    total_ref, sums_ref = refs
+    blocks = Blocks(step, psi_ref, pack_ref, vecs[-1] if vecs else None, ())
+    first_keep = not_at(0)
+    sums = Sums(step + 1, blocks.size)
+    for k in range(BLOCKS):
+        terms = [term for term in range(4) if blocks.near(k, term)]
+        if not terms:
+            continue
+        own = blocks.own(k).astype(jnp.float32)
+        total = blocks.energy(k, energy_ref) * own
+        for term in terms:
+            total = total + blocks.term(k, term, left_ref, right_ref, first_keep)
+        total_ref[k] = total
+    for k in range(BLOCKS):
+        if step == 0:
+            vals = psi_ref[k // 2, k % 2].astype(jnp.float32)
+            sums.add(0, vals, vals)
+            continue
+        own = blocks.own(k).astype(jnp.float32)
+        sums.add(0, blocks.start(k).astype(jnp.float32), own)
+        for place, vec in enumerate(vecs[:-1]):
+            sums.add(place + 1, vec[k].astype(jnp.float32), own)
+        sums.add(step, own, own)
+    row = jnp.zeros((1, 128), jnp.float32) if step == 0 else sums_in[0:1]
+    sums_ref[...] = jnp.broadcast_to(sums.write(row, FIRST_SUM[step]), sums_ref.shape)
+
+
+def far_kernel(step, last, *refs):
+    energy_ref, left_ref, right_ref, psi_ref, pack_ref, total_ref, *refs = refs
+    final = step == ITERS - 1
+    if final:
+        sums_in, *refs = refs
+        vecs, refs = refs[:step], refs[step:]
+    elif step > 0:
+        vecs, refs = refs[:1], refs[1:]
     else:
+        vecs = []
+    halos = 4
+    halo_refs, refs = refs[:halos], refs[halos:]
+    if step == 0:
+        up, low, left, corner = halo_refs
+        halo_refs = (up, low, None, left, corner)
+    blocks = Blocks(step, psi_ref, pack_ref, vecs[-1] if vecs else None, halo_refs)
+    first_keep, last_keep = not_at(0), not_at(last)
+    if final:
         new_ref, back_ref, sums_ref = refs
-    first_keep, last_keep = not_at(0), not_at(last)
-
-    def start_block(k):
-        if k == 6:
-            return pack_ref[2 * size : 3 * size]
-        return psi_ref[k // 2, k % 2] if k < 6 else psi_ref[3, 0]
-
-    def own(k):
-        return start_block(k) if step == 0 else vecs[-1][k]
-
-    def left_halo(place):
-        return pack_ref[place * size : (place + 1) * size] if step == 0 else from_left[place]
-
-    def top_halo(place):
-        if step == 0:
-            return (from_up, from_corner)[place][0]
-        return from_top[place]
-
-    def sources(k):
-        plus = {0: lambda: top_halo(0), 1: lambda: top_halo(1), 2: lambda: own(1), 3: lambda: from_right[0],
-                4: lambda: own(3), 5: lambda: from_right[1], 6: lambda: own(4), 7: lambda: own(5)}[k]()
-        minus = {0: lambda: left_halo(0), 1: lambda: own(2), 2: lambda: left_halo(1), 3: lambda: own(4),
-                 4: lambda: own(6), 5: lambda: own(7), 6: lambda: from_low[0], 7: lambda: from_low[1]}[k]()
-        return [own(k)] * DIAG + [plus, minus]
-
-    def right_block(k, term):
-        if k == 6:
-            return pack_ref[(3 + term) * size : (4 + term) * size]
-        return right_ref[k % 2 if k < 6 else 0, term]
-
-    totals = [jnp.zeros((8, size), jnp.float32) for _ in range(step + 2 + (step == 0))]
-
-    def add_product(place, one, other):
-        product = one * other
-        totals[place] = totals[place] + jnp.sum(product.reshape(size // 8, 8, size), axis=0)
-
-    for k in range(BLOCKS):
-        if k == 6:
-            energy = sum(
-                pack_ref[7 * size + 16 * place : 7 * size + 16 * place + 16].astype(jnp.float32)
-                for place in range(3)
-            )[:1]
+        sums = Sums(step + 2, blocks.size)
+    else:
+        new_ref, to_top, to_low, to_left, to_right = refs
+    for k in (0, 1, 6, 7, 2, 3, 4, 5):
+        far = [term for term in range(4) if not blocks.near(k, term)]
+        if len(far) == 4:
+            total = blocks.energy(k, energy_ref) * blocks.own(k).astype(jnp.float32)
         else:
-            energy = energy_ref[k // 2, k % 2] if k < 6 else energy_ref[3, 0]
-        total = (energy - SHIFT) * own(k).astype(jnp.float32)
-        for term, source in enumerate(sources(k)):
-            inner = dot(left_ref[k // 2, term], source)
-            if (k, term) in ((6, DIAG), (4, DIAG + HOPS)):
-                inner = inner * first_keep
-            total = total + dot_t(inner.astype(jnp.bfloat16), right_block(k, term))
+            total = total_ref[k]
+        for term in far:
+            total = total + blocks.term(k, term, left_ref, right_ref, first_keep)
         image = total.astype(jnp.bfloat16)
         new_ref[k] = image
-        vals = image.astype(jnp.float32)
-        start_vals = start_block(k).astype(jnp.float32)
-        if step == 0:
-            add_product(0, start_vals, start_vals)
-            add_product(1, start_vals, vals)
-            add_product(2, vals, vals)
-        else:
-            add_product(0, start_vals, vals)
+        if final:
+            vals = image.astype(jnp.float32)
+            sums.add(0, blocks.start(k).astype(jnp.float32), vals)
             for place, vec in enumerate(vecs):
-                add_product(place + 1, vec[k].astype(jnp.float32), vals)
-            add_product(step + 1, vals, vals)
-        if step < ITERS - 1:
-            for place, out, slot, keep in (
-                (0, to_left, 0, None), (2, to_left, 1, None), (3, to_right, 0, None), (5, to_right, 1, None),
-                (6, to_top, 0, None), (7, to_top, 1, first_keep), (0, to_low, 0, None), (1, to_low, 1, last_keep),
-            ):
-                if place == k:
-                    out[slot] = image if keep is None else masked(image, keep)
-        elif k == 6:
-            for place, vec in enumerate(vecs):
-                back_ref[place] = vec[k]
-            back_ref[step] = image
-    row = jnp.zeros((1, 128), jnp.float32) if step == 0 else sums_in[0:1]
-    start = {0: 0, 1: 3, 2: 6}[step]
-    for place, total in enumerate(totals):
-        value = jnp.sum(jnp.sum(total, axis=0, keepdims=True), axis=1, keepdims=True)
-        row = place_in(row, start + place, value)
-    sums_ref[...] = jnp.broadcast_to(row, sums_ref.shape)
+                sums.add(place + 1, vec[k].astype(jnp.float32), vals)
+            sums.add(step + 1, vals, vals)
+            if k == 6:
+                for place, vec in enumerate(vecs):
+                    back_ref[place] = vec[k]
+                back_ref[step] = image
+            continue
+        for place, out, slot, keep in (
+            (0, to_left, 0, None), (2, to_left, 1, None), (3, to_right, 0, None), (5, to_right, 1, None),
+            (6, to_top, 0, None), (7, to_top, 1, first_keep), (0, to_low, 0, None), (1, to_low, 1, last_keep),
+        ):
+            if place == k:
+                out[slot] = image if keep is None else masked(image, keep)
+    if final:
+        row = sums.write(sums_in[0:1], FIRST_SUM[ITERS])
+        sums_ref[...] = jnp.broadcast_to(row, sums_ref.shape)
 
 
 def recursion(gram, coefs):
@@ -336,40 +406,49 @@
     def blocks(number):
         return jax.ShapeDtypeStruct((number, size, size), jnp.bfloat16)
 
+    levels = energies.T
     pack, to_left, to_up, to_corner, to_low = call(
         lambda *refs: pack_kernel(last, *refs),
         [VMEM, VMEM, SMEM],
         [jax.ShapeDtypeStruct((7 * size + 48, size), jnp.bfloat16), blocks(2), blocks(1), blocks(1), blocks(2)],
-        0, psi, right_env, energies,
+        0, psi, right_env, levels,
     )
     pack = move(pack, 0, 1, True)
-    halos = [
-        move(to_left, 0, -1, False),
-        move(to_up, 1, 0, False),
-        move(to_corner, 1, -1, False),
-        move(to_low, -1, 1, True),
-    ]
-    fixed = [energies, left_env, right_env, psi, pack]
+    to_low = move(to_low, -1, 1, True)
+    to_up = move(to_up, 1, 0, False)
+    to_corner = move(to_corner, 1, -1, False)
+    to_left = move(to_left, 0, -1, False)
+    halos = [to_up, to_low, to_left, to_corner]
+    fixed = [levels, left_env, right_env, psi]
+    row = jax.ShapeDtypeStruct((8, 128), jnp.float32)
     vecs, sums = [], []
     for step in range(ITERS):
         final = step == ITERS - 1
-        row = jax.ShapeDtypeStruct((devices if final else 8, 128), jnp.float32)
-        outs = [blocks(BLOCKS), blocks(ITERS), row] if final else [blocks(BLOCKS)] + [blocks(2)] * 4 + [row]
-        ins = fixed + sums + vecs + halos
+        ins = fixed + ([pack] + sums + vecs if step else [])
+        partial, *sums = call(
+            lambda *refs, step=step: near_kernel(step, *refs),
+            [SMEM] + [VMEM] * (len(ins) - 1),
+            [jax.ShapeDtypeStruct((BLOCKS, size, size), jnp.float32), row],
+            4 * (24 if step else 20) * size**3, *ins,
+        )
+        ins = fixed + [pack, partial] + (sums + vecs if final else vecs[-1:]) + halos
+        if final:
+            outs = [blocks(BLOCKS), blocks(ITERS), jax.ShapeDtypeStruct((devices, 128), jnp.float32)]
+        else:
+            outs = [blocks(BLOCKS)] + [blocks(2)] * 4
         result = call(
-            lambda *refs, step=step: step_kernel(step, last, *refs),
-            [SMEM] + [VMEM] * (len(ins) - 1), outs, 2 * 64 * size**3, *ins,
+            lambda *refs, step=step: far_kernel(step, last, *refs),
+            [SMEM] + [VMEM] * (len(ins) - 1), outs, 4 * (8 if step else 12) * size**3, *ins,
         )
         vecs.append(result[0])
-        sums = [result[-1]]
         if not final:
-            to_left, to_right, to_top, to_low = result[1:5]
-            halos = [
-                move(to_left, 0, -1, False),
-                move(to_right, 0, 1, False),
-                move(to_top, 1, -1, True),
-                move(to_low, -1, 1, True),
-            ]
+            to_top, to_low, to_left, to_right = result[1:5]
+            to_top = move(to_top, 1, -1, True)
+            to_low = move(to_low, -1, 1, True)
+            to_left = move(to_left, 0, -1, False)
+            to_right = move(to_right, 0, 1, False)
+            halos = [to_top, to_low, to_right, to_left]
+    sums = [result[-1]]
     back = move(result[1], 0, -1, True)
     gathered = lax.all_to_all(sums[0].reshape(devices, 1, 128), AXES, 0, 0).reshape(devices, 128)
     vec, row = call(

time: 124 us -> 110 us (0.89)
  waiting for transfers between devices: 37.6 us -> 28.5 us
  starting transfers between devices: 64.8 us -> 59 us
  Pallas kernels: 17.6 us -> 19.5 us
    ppermute x14, waiting for transfers between devices: 24.7 us -> 15.5 us  [move(): return lax.ppermute(block, AXES, pairs)]
    ppermute x14, starting transfers between devices: 47.4 us -> 39.3 us  [move(): return lax.ppermute(block, AXES, pairs)]
    all_to_all x1, starting transfers between devices: 17.4 us -> 19.7 us  [per_device(): lax.all_to_all(sums[0].reshape(devices, 1, 128), AXES, 0, 0)]
    pallas_call x5 -> x8, Pallas kernels: 17.6 us -> 19.5 us  [call(): pl.pallas_call(kernel, in_specs=in_specs, out_specs=[VMEM] * len(out_shap...]
  transfers between devices with their start and end apart: 15 -> 15, of which waited for: 7 -> 8; matrix products, arithmetic and copies ran while one was open for 0% -> 0% of each run, Pallas kernels for 0% -> 8%
where the time goes in v3:
time: 110 us
  starting transfers between devices  59 us (54%)
  waiting for transfers between devices  28.5 us (26%)
  Pallas kernels  19.5 us (18%)
  between operations  1.54 us (1%)
  local copies, waits for them, and re-layouts  1.13 us (1%)
    ppermute x14, starting transfers between devices, move(): return lax.ppermute(block, AXES, pairs)  39.3 us
    all_to_all x1, starting transfers between devices, per_device(): lax.all_to_all(sums[0].reshape(devices, 1, 128), AXES, 0, 0)  19.7 us
    pallas_call x8, Pallas kernels, call(): pl.pallas_call(kernel, in_specs=in_specs, out_specs=[VMEM] * len(out_shap...  19.5 us
    ppermute x14, waiting for transfers between devices, move(): return lax.ppermute(block, AXES, pairs)  15.5 us
    all_to_all x1, waiting for transfers between devices, per_device(): lax.all_to_all(sums[0].reshape(devices, 1, 128), AXES, 0, 0)  12.9 us
  transfers between devices with their start and end apart: 15, of which 8 were waited for; matrix products, arithmetic and copies ran while one was open for 0% of the time, Pallas kernels for 8%

profile of v3, /device:TPU:1, one launch (start us, length us, event | category | flops | bytes accessed | tf_op | source)
XLA Modules:
  0.0 109.6 jit_solution(15499785473626574602)
XLA Ops:
  0.6 0.0 copy-start
  0.6 0.0 copy-start.6
  0.7 0.0 copy-start.13
  0.7 1.8 %shard_map.81 = (bf16[1840,256]{1,0:T(8,128)(2,1)S(1)}, bf16[2,256,256]{2,1,0:T(8,128)(2,1)S(1)}, bf16[1,256,256]{2,1,0:T(8,128)(2,1)S(1)}, bf16[1,256,256]{2,1,0:T(8,128)(2,1)S(1)}, bf16[2,256,256]{2,1,0:T(8,128)(2,1)S(1)}) custom-call(bf16[4,2,256,256]{3,2,1,0:T(8,128)(2,1)} %refs_3_.13, bf16[2,4,256,256]{3,2,1,0:T(8,128)(2,1)} %refs_2_.11, f32[2,4]{1,0:T(2,128)} %bitcast.186), custom_call_target="tpu_custom_call" | custom-call | bytes 3825696 | tf_op jit(solution)/shard_map/pallas_call | solution.py:390
  2.5 2.8 %collective-permute-start.18 = (bf16[1840,256]{1,0:T(8,128)(2,1)S(1)}, bf16[1840,256]{1,0:T(8,128)(2,1)S(1)}, u32[]{:S(2)}, u32[]{:S(2)}) collective-permute-start(bf16[1840,256]{1,0:T(8,128)(2,1)S(1)} %get-tuple-element.56), channel_id=1, source_target_pairs={{0,1},{1,2},{2,3},{3,4},{4,5},{5,6},{6,7},{7,8},{8,9},{9,10},{10,1... | collective-permute-start | bytes 2826248 | tf_op jit(solution)/shard_map/ppermute | solution.py:384
  5.3 1.3 %collective-permute-start.20 = (bf16[2,256,256]{2,1,0:T(8,128)(2,1)S(1)}, bf16[2,256,256]{2,1,0:T(8,128)(2,1)S(1)}, u32[]{:S(2)}, u32[]{:S(2)}) collective-permute-start(bf16[2,256,256]{2,1,0:T(8,128)(2,1)S(1)} %get-tuple-element.60), channel_id=1, source_target_pairs={{32,1},{33,2},{34,3},{35,4},{36,5},{37,6},{38,7},{39,8},{40,9},{41... | collective-permute-start | bytes 786440 | tf_op jit(solution)/shard_map/ppermute | solution.py:384
  6.5 2.5 %collective-permute-start.21 = (bf16[2,256,256]{2,1,0:T(8,128)(2,1)S(1)}, bf16[2,256,256]{2,1,0:T(8,128)(2,1)S(1)}, u32[]{:S(2)}, u32[]{:S(2)}) collective-permute-start(bf16[2,256,256]{2,1,0:T(8,128)(2,1)S(1)} %get-tuple-element.61), channel_id=1, source_target_pairs={{1,0},{2,1},{3,2},{4,3},{5,4},{6,5},{7,6},{8,7},{9,8},{10,9},{11,1... | collective-permute-start | bytes 786440 | tf_op jit(solution)/shard_map/ppermute | solution.py:384
  9.0 5.3 %collective-permute-start.19 = (bf16[1,256,256]{2,1,0:T(8,128)(2,1)S(1)}, bf16[1,256,256]{2,1,0:T(8,128)(2,1)S(1)}, u32[]{:S(2)}, u32[]{:S(2)}) collective-permute-start(bf16[1,256,256]{2,1,0:T(8,128)(2,1)S(1)} %get-tuple-element.59), channel_id=1, source_target_pairs={{0,32},{1,33},{2,34},{3,35},{4,36},{5,37},{6,38},{7,39},{8,40},{9,... | collective-permute-start | bytes 393224 | tf_op jit(solution)/shard_map/ppermute | solution.py:384
  14.4 0.0 copy-start.4
  14.4 5.1 %collective-permute-start.22 = (bf16[1,256,256]{2,1,0:T(8,128)(2,1)S(1)}, bf16[1,256,256]{2,1,0:T(8,128)(2,1)S(1)}, u32[]{:S(2)}, u32[]{:S(2)}) collective-permute-start(bf16[1,256,256]{2,1,0:T(8,128)(2,1)S(1)} %get-tuple-element.62), channel_id=1, source_target_pairs={{1,32},{2,33},{3,34},{4,35},{5,36},{6,37},{7,38},{8,39},{9,40},{10... | collective-permute-start | bytes 393224 | tf_op jit(solution)/shard_map/ppermute | solution.py:384
  19.5 0.0 copy-done
  19.5 0.0 copy-done.6
  19.5 0.0 copy-done.13
  19.5 3.3 %shard_map.82 = (f32[8,256,256]{2,1,0:T(8,128)S(1)}, f32[8,128]{1,0:T(8,128)S(1)}) custom-call(f32[2,4]{1,0:T(2,128)S(1)} %bitcast.187, bf16[4,4,256,256]{3,2,1,0:T(8,128)(2,1)} %refs_1_.14, bf16[2,4,256,256]{3,2,1,0:T(8,128)(2,1)S(1)} %copy-done.6, bf16[4,2,256,256]{3,2,1,0:T(8,128)(2,1)S(1)} %copy-done), custom_call_target="tpu_custom_call" | custom-call | flops 1342177280 | bytes 6295584 | tf_op jit(solution)/shard_map/pallas_call | solution.py:390
  22.8 1.5 %collective-permute-done.19.refs_6_ = bf16[1,256,256]{2,1,0:T(8,128)(2,1)S(1)} collective-permute-done((bf16[1,256,256]{2,1,0:T(8,128)(2,1)S(1)}, bf16[1,256,256]{2,1,0:T(8,128)(2,1)S(1)}, u32[]{:S(2)}, u32[]{:S(2)}) %collective-permute-start.19) | collective-permute-done | bytes 131104 | tf_op jit(solution)/shard_map/ppermute | solution.py:384
  24.3 3.1 %collective-permute-done.22.refs_9_ = bf16[1,256,256]{2,1,0:T(8,128)(2,1)S(1)} collective-permute-done((bf16[1,256,256]{2,1,0:T(8,128)(2,1)S(1)}, bf16[1,256,256]{2,1,0:T(8,128)(2,1)S(1)}, u32[]{:S(2)}, u32[]{:S(2)}) %collective-permute-start.22) | collective-permute-done | bytes 131104 | tf_op jit(solution)/shard_map/ppermute | solution.py:384
  27.3 0.0 collective-permute-done.20.refs_7_
  27.3 2.0 %collective-permute-done.21.refs_8_ = bf16[2,256,256]{2,1,0:T(8,128)(2,1)S(1)} collective-permute-done((bf16[2,256,256]{2,1,0:T(8,128)(2,1)S(1)}, bf16[2,256,256]{2,1,0:T(8,128)(2,1)S(1)}, u32[]{:S(2)}, u32[]{:S(2)}) %collective-permute-start.21) | collective-permute-done | bytes 262176 | tf_op jit(solution)/shard_map/ppermute | solution.py:384
  29.4 0.0 collective-permute-done.18.refs_4_
  29.4 0.0 copy-done.4
  29.4 1.6 %shard_map.83 = (bf16[8,256,256]{2,1,0:T(8,128)(2,1)S(1)}, bf16[2,256,256]{2,1,0:T(8,128)(2,1)S(1)}, bf16[2,256,256]{2,1,0:T(8,128)(2,1)S(1)}, bf16[2,256,256]{2,1,0:T(8,128)(2,1)S(1)}, bf16[2,256,256]{2,1,0:T(8,128)(2,1)S(1)}) custom-call(f32[2,4]{1,0:T(2,128)S(1)} %bitcast.188, bf16[4,4,256,256]{3,2,1,0:T(8,128)(2,1)S(1)} %copy-done.4, ...), custom_call_target="tpu_custom_call" | custom-call | flops 805306368 | bytes 10117152 | tf_op jit(solution)/shard_map/pallas_call | solution.py:390
  31.0 5.1 %collective-permute-start.23 = (bf16[2,256,256]{2,1,0:T(8,128)(2,1)S(1)}, bf16[2,256,256]{2,1,0:T(8,128)(2,1)S(1)}, u32[]{:S(2)}, u32[]{:S(2)}) collective-permute-start(bf16[2,256,256]{2,1,0:T(8,128)(2,1)S(1)} %get-tuple-element.66), channel_id=1, source_target_pairs={{0,63},{1,32},{2,33},{3,34},{4,35},{5,36},{6,37},{7,38},{8,39},{9,... | collective-permute-start | bytes 786440 | tf_op jit(solution)/shard_map/ppermute | solution.py:384
  36.1 1.3 %collective-permute-start.24 = (bf16[2,256,256]{2,1,0:T(8,128)(2,1)S(1)}, bf16[2,256,256]{2,1,0:T(8,128)(2,1)S(1)}, u32[]{:S(2)}, u32[]{:S(2)}) collective-permute-start(bf16[2,256,256]{2,1,0:T(8,128)(2,1)S(1)} %get-tuple-element.67), channel_id=1, source_target_pairs={{32,1},{33,2},{34,3},{35,4},{36,5},{37,6},{38,7},{39,8},{40,9},{41... | collective-permute-start | bytes 786440 | tf_op jit(solution)/shard_map/ppermute | solution.py:384
  37.4 1.9 %collective-permute-start.25 = (bf16[2,256,256]{2,1,0:T(8,128)(2,1)S(1)}, bf16[2,256,256]{2,1,0:T(8,128)(2,1)S(1)}, u32[]{:S(2)}, u32[]{:S(2)}) collective-permute-start(bf16[2,256,256]{2,1,0:T(8,128)(2,1)S(1)} %get-tuple-element.68), channel_id=1, source_target_pairs={{0,1},{1,2},{2,3},{3,4},{4,5},{5,6},{6,7},{7,8},{8,9},{9,10},{10,1... | collective-permute-start | bytes 786440 | tf_op jit(solution)/shard_map/ppermute | solution.py:384
  39.3 2.4 %collective-permute-start.26 = (bf16[2,256,256]{2,1,0:T(8,128)(2,1)S(1)}, bf16[2,256,256]{2,1,0:T(8,128)(2,1)S(1)}, u32[]{:S(2)}, u32[]{:S(2)}) collective-permute-start(bf16[2,256,256]{2,1,0:T(8,128)(2,1)S(1)} %get-tuple-element.69), channel_id=1, source_target_pairs={{1,0},{2,1},{3,2},{4,3},{5,4},{6,5},{7,6},{8,7},{9,8},{10,9},{11,1... | collective-permute-start | bytes 786440 | tf_op jit(solution)/shard_map/ppermute | solution.py:384
  41.7 2.5 %shard_map.84 = (f32[8,256,256]{2,1,0:T(8,128)S(1)}, f32[8,128]{1,0:T(8,128)S(1)}) custom-call(f32[2,4]{1,0:T(2,128)S(1)} %bitcast.189, bf16[4,4,256,256]{3,2,1,0:T(8,128)(2,1)S(1)} %copy-done.4, bf16[2,4,256,256]{3,2,1,0:T(8,128)(2,1)S(1)} %copy-done.6, bf16[4,2,256,256]{3,2,1,0:T(8,128)(2,1)S(1)} %copy-done, ...), custom_call_target="tpu_custom_call" | custom-call | flops 1610612736 | bytes 8290336 | tf_op jit(solution)/shard_map/pallas_call | solution.py:390
  44.2 0.0 collective-permute-done.23.refs_7_
  44.2 3.8 %collective-permute-done.24.refs_8_ = bf16[2,256,256]{2,1,0:T(8,128)(2,1)S(1)} collective-permute-done((bf16[2,256,256]{2,1,0:T(8,128)(2,1)S(1)}, bf16[2,256,256]{2,1,0:T(8,128)(2,1)S(1)}, u32[]{:S(2)}, u32[]{:S(2)}) %collective-permute-start.24) | collective-permute-done | bytes 262176 | tf_op jit(solution)/shard_map/ppermute | solution.py:384
  48.1 0.0 collective-permute-done.25.refs_9_
  48.1 0.6 collective-permute-done.26.refs_10_
  48.7 1.4 %shard_map.85 = (bf16[8,256,256]{2,1,0:T(8,128)(2,1)S(1)}, bf16[2,256,256]{2,1,0:T(8,128)(2,1)S(1)}, bf16[2,256,256]{2,1,0:T(8,128)(2,1)S(1)}, bf16[2,256,256]{2,1,0:T(8,128)(2,1)S(1)}, bf16[2,256,256]{2,1,0:T(8,128)(2,1)S(1)}) custom-call(f32[2,4]{1,0:T(2,128)S(1)} %bitcast.190, bf16[4,4,256,256]{3,2,1,0:T(8,128)(2,1)S(1)} %copy-done.4, ...), custom_call_target="tpu_custom_call" | custom-call | flops 536870912 | bytes 11427872 | tf_op jit(solution)/shard_map/pallas_call | solution.py:390
  50.1 2.8 %collective-permute-start.27 = (bf16[2,256,256]{2,1,0:T(8,128)(2,1)S(1)}, bf16[2,256,256]{2,1,0:T(8,128)(2,1)S(1)}, u32[]{:S(2)}, u32[]{:S(2)}) collective-permute-start(bf16[2,256,256]{2,1,0:T(8,128)(2,1)S(1)} %get-tuple-element.73), channel_id=1, source_target_pairs={{0,63},{1,32},{2,33},{3,34},{4,35},{5,36},{6,37},{7,38},{8,39},{9,... | collective-permute-start | bytes 786440 | tf_op jit(solution)/shard_map/ppermute | solution.py:384
  52.9 1.3 %collective-permute-start.28 = (bf16[2,256,256]{2,1,0:T(8,128)(2,1)S(1)}, bf16[2,256,256]{2,1,0:T(8,128)(2,1)S(1)}, u32[]{:S(2)}, u32[]{:S(2)}) collective-permute-start(bf16[2,256,256]{2,1,0:T(8,128)(2,1)S(1)} %get-tuple-element.74), channel_id=1, source_target_pairs={{32,1},{33,2},{34,3},{35,4},{36,5},{37,6},{38,7},{39,8},{40,9},{41... | collective-permute-start | bytes 786440 | tf_op jit(solution)/shard_map/ppermute | solution.py:384
  54.2 5.7 %collective-permute-start.29 = (bf16[2,256,256]{2,1,0:T(8,128)(2,1)S(1)}, bf16[2,256,256]{2,1,0:T(8,128)(2,1)S(1)}, u32[]{:S(2)}, u32[]{:S(2)}) collective-permute-start(bf16[2,256,256]{2,1,0:T(8,128)(2,1)S(1)} %get-tuple-element.75), channel_id=1, source_target_pairs={{0,1},{1,2},{2,3},{3,4},{4,5},{5,6},{6,7},{7,8},{8,9},{9,10},{10,1... | collective-permute-start | bytes 786440 | tf_op jit(solution)/shard_map/ppermute | solution.py:384
  59.9 1.9 %collective-permute-start.30 = (bf16[2,256,256]{2,1,0:T(8,128)(2,1)S(1)}, bf16[2,256,256]{2,1,0:T(8,128)(2,1)S(1)}, u32[]{:S(2)}, u32[]{:S(2)}) collective-permute-start(bf16[2,256,256]{2,1,0:T(8,128)(2,1)S(1)} %get-tuple-element.76), channel_id=1, source_target_pairs={{1,0},{2,1},{3,2},{4,3},{5,4},{6,5},{7,6},{8,7},{9,8},{10,9},{11,1... | collective-permute-start | bytes 786440 | tf_op jit(solution)/shard_map/ppermute | solution.py:384
  61.8 2.5 %shard_map.86 = (f32[8,256,256]{2,1,0:T(8,128)S(1)}, f32[8,128]{1,0:T(8,128)S(1)}) custom-call(f32[2,4]{1,0:T(2,128)S(1)} %bitcast.191, bf16[4,4,256,256]{3,2,1,0:T(8,128)(2,1)S(1)} %copy-done.4, bf16[2,4,256,256]{3,2,1,0:T(8,128)(2,1)S(1)} %copy-done.6, bf16[4,2,256,256]{3,2,1,0:T(8,128)(2,1)S(1)} %copy-done, ...), custom_call_target="tpu_custom_call" | custom-call | flops 1610612736 | bytes 9338912 | tf_op jit(solution)/shard_map/pallas_call | solution.py:390
  64.3 0.0 collective-permute-done.27.refs_9_
  64.4 1.3 %collective-permute-done.28.refs_10_ = bf16[2,256,256]{2,1,0:T(8,128)(2,1)S(1)} collective-permute-done((bf16[2,256,256]{2,1,0:T(8,128)(2,1)S(1)}, bf16[2,256,256]{2,1,0:T(8,128)(2,1)S(1)}, u32[]{:S(2)}, u32[]{:S(2)}) %collective-permute-start.28) | collective-permute-done | bytes 262176 | tf_op jit(solution)/shard_map/ppermute | solution.py:384
  65.7 3.1 %collective-permute-done.29.refs_11_ = bf16[2,256,256]{2,1,0:T(8,128)(2,1)S(1)} collective-permute-done((bf16[2,256,256]{2,1,0:T(8,128)(2,1)S(1)}, bf16[2,256,256]{2,1,0:T(8,128)(2,1)S(1)}, u32[]{:S(2)}, u32[]{:S(2)}) %collective-permute-start.29) | collective-permute-done | bytes 262176 | tf_op jit(solution)/shard_map/ppermute | solution.py:384
  68.8 0.0 collective-permute-done.30.refs_12_
  68.8 0.0 copy-start.14
  68.8 0.0 copy-start.15
  68.8 2.7 %shard_map.87 = (bf16[8,256,256]{2,1,0:T(8,128)(2,1)S(1)}, bf16[3,256,256]{2,1,0:T(8,128)(2,1)}, f32[256,128]{1,0:T(8,128)}) custom-call(f32[2,4]{1,0:T(2,128)S(1)} %bitcast.192, bf16[4,4,256,256]{3,2,1,0:T(8,128)(2,1)S(1)} %copy-done.4, bf16[2,4,256,256]{3,2,1,0:T(8,128)(2,1)S(1)} %copy-done.6, bf16[4,2,256,256]{3,2,1,0:T(8,128)(2,1)S(1)} %copy-done, ...), custom_call_target="tpu_custom_call" | custom-call | flops 536870912 | bytes 11956256 | tf_op jit(solution)/shard_map/pallas_call | solution.py:390
  71.5 0.0 collective-permute-start.31
  71.5 19.7 %all-to-all-start = ((f32[256,1,128]{2,1,0:T(1,128)}), f32[256,1,128]{2,1,0:T(1,128)S(1)}, u32[]{:S(2)}, u32[]{:S(2)}) async-start(f32[256,1,128]{2,1,0:T(1,128)} %bitcast.56), calls=%async_computation | async-start | bytes 262144 | tf_op jit(solution)/shard_map/all_to_all | solution.py:453
  91.2 12.9 %all-to-all-done = f32[256,1,128]{2,1,0:T(1,128)S(1)} async-done(((f32[256,1,128]{2,1,0:T(1,128)}), f32[256,1,128]{2,1,0:T(1,128)S(1)}, u32[]{:S(2)}, u32[]{:S(2)}) %all-to-all-start) | async-done | bytes 131104 | tf_op jit(solution)/shard_map/all_to_all | solution.py:453
  104.1 0.0 collective-permute-done.31.refs_7_
  104.1 0.0 copy-done.14
  104.1 0.0 copy-done.15
  104.1 0.0 copy-start.1
  104.2 3.6 %shard_map.88 = (bf16[4,2,256,256]{3,2,1,0:T(8,128)(2,1)}, f32[1,128]{1,0:T(1,128)S(1)}) custom-call(s32[2]{0:T(128)S(1)} %copy-done.14, s32[2]{0:T(128)S(1)} %copy-done.15, f32[256,128]{1,0:T(8,128)S(1)} %bitcast.185, bf16[4,2,256,256]{3,2,1,0:T(8,128)(2,1)} %refs_3_.13, bf16[8,256,256]{2,1,0:T(8,128)(2,1)S(1)} %get-tuple-element.63.refs_6_.refs_7_.refs_4_, ...), custom_call_target="tpu_custom_call" | custom-call | bytes 5767696 | tf_op jit(solution)/shard_map/pallas_call | solution.py:390
  107.8 0.6 slice.131
  109.0 0.0 copy-done.1
  109.1 0.0 copy-start.16
  109.1 0.5 copy-done.16
  (2 shorter events, 0.0 us)
Async XLA Ops:
  0.6 18.9 %copy-start = (bf16[4,2,256,256]{3,2,1,0:T(8,128)(2,1)S(1)}, bf16[4,2,256,256]{3,2,1,0:T(8,128)(2,1)}, u32[]{:S(2)}) copy-start(bf16[4,2,256,256]{3,2,1,0:T(8,128)(2,1)} %refs_3_.13) | copy-start | bytes 3145732
  0.6 18.9 %copy-start.6 = (bf16[2,4,256,256]{3,2,1,0:T(8,128)(2,1)S(1)}, bf16[2,4,256,256]{3,2,1,0:T(8,128)(2,1)}, u32[]{:S(2)}) copy-start(bf16[2,4,256,256]{3,2,1,0:T(8,128)(2,1)} %refs_2_.11) | copy-start | bytes 3145732
  0.7 18.9 %copy-start.13 = (f32[4,2]{0,1:T(2,128)S(1)}, f32[4,2]{0,1:T(2,128)}, u32[]{:S(2)}) copy-start(f32[4,2]{0,1:T(2,128)} %param.11) | copy-start | bytes 100
  2.5 26.9 %collective-permute-start.18 = (bf16[1840,256]{1,0:T(8,128)(2,1)S(1)}, bf16[1840,256]{1,0:T(8,128)(2,1)S(1)}, u32[]{:S(2)}, u32[]{:S(2)}) collective-permute-start(bf16[1840,256]{1,0:T(8,128)(2,1)S(1)} %get-tuple-element.56), channel_id=1, source_target_pairs={{0,1},{1,2},{2,3},{3,4},{4,5},{5,6},{6,7},{7,8},{8,9},{9,10},{10,1... | collective-permute-start | bytes 2826248 | tf_op jit(solution)/shard_map/ppermute | solution.py:384
  5.3 22.1 %collective-permute-start.20 = (bf16[2,256,256]{2,1,0:T(8,128)(2,1)S(1)}, bf16[2,256,256]{2,1,0:T(8,128)(2,1)S(1)}, u32[]{:S(2)}, u32[]{:S(2)}) collective-permute-start(bf16[2,256,256]{2,1,0:T(8,128)(2,1)S(1)} %get-tuple-element.60), channel_id=1, source_target_pairs={{32,1},{33,2},{34,3},{35,4},{36,5},{37,6},{38,7},{39,8},{40,9},{41... | collective-permute-start | bytes 786440 | tf_op jit(solution)/shard_map/ppermute | solution.py:384
  6.5 22.8 %collective-permute-start.21 = (bf16[2,256,256]{2,1,0:T(8,128)(2,1)S(1)}, bf16[2,256,256]{2,1,0:T(8,128)(2,1)S(1)}, u32[]{:S(2)}, u32[]{:S(2)}) collective-permute-start(bf16[2,256,256]{2,1,0:T(8,128)(2,1)S(1)} %get-tuple-element.61), channel_id=1, source_target_pairs={{1,0},{2,1},{3,2},{4,3},{5,4},{6,5},{7,6},{8,7},{9,8},{10,9},{11,1... | collective-permute-start | bytes 786440 | tf_op jit(solution)/shard_map/ppermute | solution.py:384
  9.0 15.2 %collective-permute-start.19 = (bf16[1,256,256]{2,1,0:T(8,128)(2,1)S(1)}, bf16[1,256,256]{2,1,0:T(8,128)(2,1)S(1)}, u32[]{:S(2)}, u32[]{:S(2)}) collective-permute-start(bf16[1,256,256]{2,1,0:T(8,128)(2,1)S(1)} %get-tuple-element.59), channel_id=1, source_target_pairs={{0,32},{1,33},{2,34},{3,35},{4,36},{5,37},{6,38},{7,39},{8,40},{9,... | collective-permute-start | bytes 393224 | tf_op jit(solution)/shard_map/ppermute | solution.py:384
  14.4 15.0 %copy-start.4 = (bf16[4,4,256,256]{3,2,1,0:T(8,128)(2,1)S(1)}, bf16[4,4,256,256]{3,2,1,0:T(8,128)(2,1)}, u32[]{:S(2)}) copy-start(bf16[4,4,256,256]{3,2,1,0:T(8,128)(2,1)} %refs_1_.14) | copy-start | bytes 6291460
  14.4 13.0 %collective-permute-start.22 = (bf16[1,256,256]{2,1,0:T(8,128)(2,1)S(1)}, bf16[1,256,256]{2,1,0:T(8,128)(2,1)S(1)}, u32[]{:S(2)}, u32[]{:S(2)}) collective-permute-start(bf16[1,256,256]{2,1,0:T(8,128)(2,1)S(1)} %get-tuple-element.62), channel_id=1, source_target_pairs={{1,32},{2,33},{3,34},{4,35},{5,36},{6,37},{7,38},{8,39},{9,40},{10... | collective-permute-start | bytes 393224 | tf_op jit(solution)/shard_map/ppermute | solution.py:384
  31.0 13.2 %collective-permute-start.23 = (bf16[2,256,256]{2,1,0:T(8,128)(2,1)S(1)}, bf16[2,256,256]{2,1,0:T(8,128)(2,1)S(1)}, u32[]{:S(2)}, u32[]{:S(2)}) collective-permute-start(bf16[2,256,256]{2,1,0:T(8,128)(2,1)S(1)} %get-tuple-element.66), channel_id=1, source_target_pairs={{0,63},{1,32},{2,33},{3,34},{4,35},{5,36},{6,37},{7,38},{8,39},{9,... | collective-permute-start | bytes 786440 | tf_op jit(solution)/shard_map/ppermute | solution.py:384
  36.1 12.0 %collective-permute-start.24 = (bf16[2,256,256]{2,1,0:T(8,128)(2,1)S(1)}, bf16[2,256,256]{2,1,0:T(8,128)(2,1)S(1)}, u32[]{:S(2)}, u32[]{:S(2)}) collective-permute-start(bf16[2,256,256]{2,1,0:T(8,128)(2,1)S(1)} %get-tuple-element.67), channel_id=1, source_target_pairs={{32,1},{33,2},{34,3},{35,4},{36,5},{37,6},{38,7},{39,8},{40,9},{41... | collective-permute-start | bytes 786440 | tf_op jit(solution)/shard_map/ppermute | solution.py:384
  37.4 10.7 %collective-permute-start.25 = (bf16[2,256,256]{2,1,0:T(8,128)(2,1)S(1)}, bf16[2,256,256]{2,1,0:T(8,128)(2,1)S(1)}, u32[]{:S(2)}, u32[]{:S(2)}) collective-permute-start(bf16[2,256,256]{2,1,0:T(8,128)(2,1)S(1)} %get-tuple-element.68), channel_id=1, source_target_pairs={{0,1},{1,2},{2,3},{3,4},{4,5},{5,6},{6,7},{7,8},{8,9},{9,10},{10,1... | collective-permute-start | bytes 786440 | tf_op jit(solution)/shard_map/ppermute | solution.py:384
  39.3 9.4 %collective-permute-start.26 = (bf16[2,256,256]{2,1,0:T(8,128)(2,1)S(1)}, bf16[2,256,256]{2,1,0:T(8,128)(2,1)S(1)}, u32[]{:S(2)}, u32[]{:S(2)}) collective-permute-start(bf16[2,256,256]{2,1,0:T(8,128)(2,1)S(1)} %get-tuple-element.69), channel_id=1, source_target_pairs={{1,0},{2,1},{3,2},{4,3},{5,4},{6,5},{7,6},{8,7},{9,8},{10,9},{11,1... | collective-permute-start | bytes 786440 | tf_op jit(solution)/shard_map/ppermute | solution.py:384
  50.1 14.2 %collective-permute-start.27 = (bf16[2,256,256]{2,1,0:T(8,128)(2,1)S(1)}, bf16[2,256,256]{2,1,0:T(8,128)(2,1)S(1)}, u32[]{:S(2)}, u32[]{:S(2)}) collective-permute-start(bf16[2,256,256]{2,1,0:T(8,128)(2,1)S(1)} %get-tuple-element.73), channel_id=1, source_target_pairs={{0,63},{1,32},{2,33},{3,34},{4,35},{5,36},{6,37},{7,38},{8,39},{9,... | collective-permute-start | bytes 786440 | tf_op jit(solution)/shard_map/ppermute | solution.py:384
  52.9 12.8 %collective-permute-start.28 = (bf16[2,256,256]{2,1,0:T(8,128)(2,1)S(1)}, bf16[2,256,256]{2,1,0:T(8,128)(2,1)S(1)}, u32[]{:S(2)}, u32[]{:S(2)}) collective-permute-start(bf16[2,256,256]{2,1,0:T(8,128)(2,1)S(1)} %get-tuple-element.74), channel_id=1, source_target_pairs={{32,1},{33,2},{34,3},{35,4},{36,5},{37,6},{38,7},{39,8},{40,9},{41... | collective-permute-start | bytes 786440 | tf_op jit(solution)/shard_map/ppermute | solution.py:384
  54.2 14.6 %collective-permute-start.29 = (bf16[2,256,256]{2,1,0:T(8,128)(2,1)S(1)}, bf16[2,256,256]{2,1,0:T(8,128)(2,1)S(1)}, u32[]{:S(2)}, u32[]{:S(2)}) collective-permute-start(bf16[2,256,256]{2,1,0:T(8,128)(2,1)S(1)} %get-tuple-element.75), channel_id=1, source_target_pairs={{0,1},{1,2},{2,3},{3,4},{4,5},{5,6},{6,7},{7,8},{8,9},{9,10},{10,1... | collective-permute-start | bytes 786440 | tf_op jit(solution)/shard_map/ppermute | solution.py:384
  59.9 8.9 %collective-permute-start.30 = (bf16[2,256,256]{2,1,0:T(8,128)(2,1)S(1)}, bf16[2,256,256]{2,1,0:T(8,128)(2,1)S(1)}, u32[]{:S(2)}, u32[]{:S(2)}) collective-permute-start(bf16[2,256,256]{2,1,0:T(8,128)(2,1)S(1)} %get-tuple-element.76), channel_id=1, source_target_pairs={{1,0},{2,1},{3,2},{4,3},{5,4},{6,5},{7,6},{8,7},{9,8},{10,9},{11,1... | collective-permute-start | bytes 786440 | tf_op jit(solution)/shard_map/ppermute | solution.py:384
  68.8 35.3 %copy-start.14 = (s32[2]{0:T(128)S(1)}, s32[2]{0:T(128)}, u32[]{:S(2)}) copy-start(s32[2]{0:T(128)} %refs_0_.3) | copy-start | bytes 28
  68.8 35.3 %copy-start.15 = (s32[2]{0:T(128)S(1)}, s32[2]{0:T(128)}, u32[]{:S(2)}) copy-start(s32[2]{0:T(128)} %refs_1_.15) | copy-start | bytes 28
  71.5 32.6 %collective-permute-start.31 = (bf16[3,256,256]{2,1,0:T(8,128)(2,1)}, bf16[3,256,256]{2,1,0:T(8,128)(2,1)}, u32[]{:S(2)}, u32[]{:S(2)}) collective-permute-start(bf16[3,256,256]{2,1,0:T(8,128)(2,1)} %get-tuple-element.79), channel_id=1, source_target_pairs={{0,31},{1,0},{2,1},{3,2},{4,3},{5,4},{6,5},{7,6},{8,7},{9,8},{10,9... | collective-permute-start | bytes 1179656 | tf_op jit(solution)/shard_map/ppermute | solution.py:384
  71.5 32.6 %all-to-all-start = ((f32[256,1,128]{2,1,0:T(1,128)}), f32[256,1,128]{2,1,0:T(1,128)S(1)}, u32[]{:S(2)}, u32[]{:S(2)}) async-start(f32[256,1,128]{2,1,0:T(1,128)} %bitcast.56), calls=%async_computation | async-start | bytes 262144 | tf_op jit(solution)/shard_map/all_to_all | solution.py:453
  104.1 4.9 %copy-start.1 = (bf16[4,2,256,256]{3,2,1,0:T(8,128)(2,1)S(1)}, bf16[4,2,256,256]{3,2,1,0:T(8,128)(2,1)}, u32[]{:S(2)}) copy-start(bf16[4,2,256,256]{3,2,1,0:T(8,128)(2,1)} %refs_3_.13) | copy-start | bytes 3145732
  109.1 0.5 copy-start.16

commit v4 on v3

--- a/solution.py
+++ b/solution.py
@@ -116,25 +116,30 @@
     return (block.astype(jnp.float32) * keep).astype(jnp.bfloat16)
 
 
-def pack_kernel(last, psi_ref, right_ref, energy_ref, pack_ref, left_out, up_out, corner_out, low_out):
-    size = psi_ref.shape[-1]
-    inner = not_at(last)
-    for place in range(2):
-        pack_ref[place * size : (place + 1) * size] = masked(psi_ref[place + 1, 1], inner)
-        left_out[place] = psi_ref[place, 0]
-    pack_ref[2 * size : 3 * size] = psi_ref[3, 1]
-    for term in range(4):
-        pack_ref[(3 + term) * size : (4 + term) * size] = right_ref[1, term]
-    rest = jnp.full((16, size), energy_ref[1, 3], jnp.float32)
+def write_energy(ref, start, value):
+    rest = jnp.full((16, ref.shape[-1]), value, jnp.float32)
     for place in range(3):
         part = rest.astype(jnp.bfloat16)
-        start = 7 * size + 16 * place
-        pack_ref[start : start + 16] = part
+        ref[start + 16 * place : start + 16 * place + 16] = part
         rest = rest - part.astype(jnp.float32)
-    up_out[0] = psi_ref[3, 1]
-    corner_out[0] = psi_ref[3, 0]
-    low_out[0] = psi_ref[0, 0]
-    low_out[1] = masked(psi_ref[0, 1], inner)
+
+
+def pack_kernel(psi_ref, right_ref, energy_ref, right_out, left_out, top_out, low_out, corner_out):
+    size = psi_ref.shape[-1]
+    for place, (i, j) in enumerate(((2, 1), (3, 0), (3, 1))):
+        right_out[place * size : (place + 1) * size] = psi_ref[i, j]
+        write_energy(right_out, 11 * size + 48 * place, energy_ref[j, i])
+    left_out[:size] = psi_ref[0, 0]
+    write_energy(left_out, 5 * size, energy_ref[0, 0])
+    for term in range(4):
+        for col in range(COLS):
+            start = (3 + 4 * col + term) * size
+            right_out[start : start + size] = right_ref[col, term]
+        left_out[(1 + term) * size : (2 + term) * size] = right_ref[0, term]
+    top_out[0] = masked(psi_ref[3, 0], not_at(0))
+    top_out[1] = psi_ref[3, 1]
+    low_out[0] = psi_ref[0, 1]
+    corner_out[0] = psi_ref[0, 0]
 
 
 def place_in(row, lane, value):
@@ -142,61 +147,70 @@
     return jnp.where(lanes == lane, value, row)
 
 
+HELD = {0: (0, 1), 2: (1, 0), 3: (1, 1), 5: (2, 0)}
+PACKED = {4: 0, 6: 1, 7: 2}
+COLUMN = {4: 1, 6: 0, 7: 1}
+
+
 class Blocks:
-    def __init__(self, step, psi_ref, pack_ref, vec_ref, halo_refs):
-        self.step, self.psi_ref, self.pack_ref, self.vec_ref = step, psi_ref, pack_ref, vec_ref
+    def __init__(self, step, psi_ref, packs, vec_ref, halo_refs, last):
+        self.step, self.psi_ref, self.vec_ref, self.halo_refs = step, psi_ref, vec_ref, halo_refs
+        self.from_left, self.from_right = packs
         self.size = psi_ref.shape[-1]
-        self.halo_refs = halo_refs
-
-    def packed(self, place):
-        return self.pack_ref[place * self.size : (place + 1) * self.size]
+        first, last = not_at(0), not_at(last)
+        self.cut = {(4, 2): first, (7, 5): first, (3, 1): last}
 
     def start(self, k):
-        if k == 6:
-            return self.packed(2)
-        return self.psi_ref[k // 2, k % 2] if k < 6 else self.psi_ref[3, 0]
+        if k in HELD:
+            return self.psi_ref[HELD[k]]
+        if k == 1:
+            return self.from_right[: self.size]
+        return self.from_left[PACKED[k] * self.size : (PACKED[k] + 1) * self.size]
 
     def own(self, k):
         return self.start(k) if self.step == 0 else self.vec_ref[k]
 
+    def place(self, k, term):
+        return k if term < DIAG else k - 2 if term == DIAG else k + 2
+
     def source(self, k, term):
-        if term < DIAG:
-            return self.own(k)
-        if term == DIAG:
-            halo = {0: (0, 0), 1: (0, 1), 3: (3, 0), 5: (3, 1)}
-            inside = {2: 1, 4: 3, 6: 4, 7: 5}
-        else:
-            halo = {0: (2, 0), 2: (2, 1), 6: (1, 0), 7: (1, 1)}
-            inside = {1: 2, 3: 4, 4: 6, 5: 7}
-        if k in inside:
-            return self.own(inside[k])
-        group, place = halo[k]
-        if self.step == 0 and group == 0:
-            return self.halo_refs[(0, 4)[place]][0]
-        if self.step == 0 and group == 2:
-            return self.packed(place)
-        return self.halo_refs[group][place]
+        place = self.place(k, term)
+        if 0 <= place < BLOCKS:
+            return self.own(place)
+        top = place < 0
+        if self.step == 0 and not top:
+            return self.halo_refs[1 + k % 2][0]
+        return self.halo_refs[0 if top else 1][k % 2]
 
     def near(self, k, term):
-        if self.step == 0 and (k == 6 or (k, term) == (4, DIAG + HOPS)):
-            return False
-        if term < DIAG:
-            return True
-        return k in ((2, 4, 6, 7) if term == DIAG else (1, 3, 4, 5))
-
-    def term(self, k, term, left_ref, right_ref, first_keep):
+        place = self.place(k, term)
+        if self.step == 0:
+            return k in HELD and place in HELD
+        return 0 <= place < BLOCKS
+
+    def right(self, k, term, right_ref):
+        if k in HELD:
+            return right_ref[HELD[k][1], term]
+        if k == 1:
+            return self.from_right[(1 + term) * self.size : (2 + term) * self.size]
+        start = (3 + 4 * COLUMN[k] + term) * self.size
+        return self.from_left[start : start + self.size]
+
+    def term(self, k, term, left_ref, right_ref):
         inner = dot(left_ref[k // 2, term], self.source(k, term))
-        if (k, term) in ((6, DIAG), (4, DIAG + HOPS)):
-            inner = inner * first_keep
-        right = self.packed(3 + term) if k == 6 else right_ref[k % 2 if k < 6 else 0, term]
-        return dot_t(inner.astype(jnp.bfloat16), right)
+        place = self.place(k, term)
+        keep = self.cut.get((max(k, place), min(k, place))) if term >= DIAG else None
+        if keep is not None:
+            inner = inner * keep
+        return dot_t(inner.astype(jnp.bfloat16), self.right(k, term, right_ref))
 
     def energy(self, k, energy_ref):
-        if k == 6:
-            start = 7 * self.size
-            parts = [self.pack_ref[start + 16 * i : start + 16 * i + 16].astype(jnp.float32) for i in range(3)]
-            return sum(parts)[:1] - SHIFT
-        return (energy_ref[k % 2, k // 2] if k < 6 else energy_ref[0, 3]) - SHIFT
+        if k in HELD:
+            i, j = HELD[k]
+            return energy_ref[j, i] - SHIFT
+        ref, start = (self.from_right, 5 * self.size) if k == 1 else (self.from_left, 11 * self.size + 48 * PACKED[k])
+        parts = [ref[start + 16 * i : start + 16 * i + 16].astype(jnp.float32) for i in range(3)]
+        return sum(parts)[:1] - SHIFT
 
 
 class Sums:
@@ -218,26 +232,22 @@
 FIRST_SUM = (0, 1, 3, 6)
 
 
-def near_kernel(step, *refs):
+def near_kernel(step, last, *refs):
     energy_ref, left_ref, right_ref, psi_ref, *refs = refs
     if step == 0:
-        pack_ref, vecs, refs = None, [], refs
+        packs, vecs = (None, None), []
     else:
-        pack_ref, *refs = refs
-        sums_in, *refs = refs
-        vecs, refs = refs[:step], refs[step:]
+        packs, sums_in, vecs, refs = refs[:2], refs[2], refs[3 : 3 + step], refs[3 + step :]
     total_ref, sums_ref = refs
-    blocks = Blocks(step, psi_ref, pack_ref, vecs[-1] if vecs else None, ())
-    first_keep = not_at(0)
+    blocks = Blocks(step, psi_ref, packs, vecs[-1] if vecs else None, (), last)
     sums = Sums(step + 1, blocks.size)
     for k in range(BLOCKS):
         terms = [term for term in range(4) if blocks.near(k, term)]
         if not terms:
             continue
-        own = blocks.own(k).astype(jnp.float32)
-        total = blocks.energy(k, energy_ref) * own
+        total = blocks.energy(k, energy_ref) * blocks.own(k).astype(jnp.float32)
         for term in terms:
-            total = total + blocks.term(k, term, left_ref, right_ref, first_keep)
+            total = total + blocks.term(k, term, left_ref, right_ref)
         total_ref[k] = total
     for k in range(BLOCKS):
         if step == 0:
@@ -254,35 +264,29 @@
 
 
 def far_kernel(step, last, *refs):
-    energy_ref, left_ref, right_ref, psi_ref, pack_ref, total_ref, *refs = refs
+    energy_ref, left_ref, right_ref, psi_ref, *refs = refs
+    packs, total_ref, refs = refs[:2], refs[2], refs[3:]
     final = step == ITERS - 1
     if final:
-        sums_in, *refs = refs
-        vecs, refs = refs[:step], refs[step:]
-    elif step > 0:
-        vecs, refs = refs[:1], refs[1:]
+        sums_in, vecs, refs = refs[0], refs[1 : 1 + step], refs[1 + step :]
     else:
-        vecs = []
-    halos = 4
+        vecs, refs = refs[: min(step, 1)], refs[min(step, 1) :]
+    halos = 3 if step == 0 else 2
     halo_refs, refs = refs[:halos], refs[halos:]
-    if step == 0:
-        up, low, left, corner = halo_refs
-        halo_refs = (up, low, None, left, corner)
-    blocks = Blocks(step, psi_ref, pack_ref, vecs[-1] if vecs else None, halo_refs)
-    first_keep, last_keep = not_at(0), not_at(last)
+    blocks = Blocks(step, psi_ref, packs, vecs[-1] if vecs else None, halo_refs, last)
     if final:
-        new_ref, back_ref, sums_ref = refs
+        new_ref, back_left, back_right, sums_ref = refs
         sums = Sums(step + 2, blocks.size)
     else:
-        new_ref, to_top, to_low, to_left, to_right = refs
-    for k in (0, 1, 6, 7, 2, 3, 4, 5):
+        new_ref, to_top, to_low = refs
+    for k in range(BLOCKS):
         far = [term for term in range(4) if not blocks.near(k, term)]
         if len(far) == 4:
             total = blocks.energy(k, energy_ref) * blocks.own(k).astype(jnp.float32)
         else:
             total = total_ref[k]
         for term in far:
-            total = total + blocks.term(k, term, left_ref, right_ref, first_keep)
+            total = total + blocks.term(k, term, left_ref, right_ref)
         image = total.astype(jnp.bfloat16)
         new_ref[k] = image
         if final:
@@ -291,17 +295,19 @@
             for place, vec in enumerate(vecs):
                 sums.add(place + 1, vec[k].astype(jnp.float32), vals)
             sums.add(step + 1, vals, vals)
-            if k == 6:
+            if k not in HELD:
+                out, first = (back_right, 0) if k == 1 else (back_left, ITERS * PACKED[k])
                 for place, vec in enumerate(vecs):
-                    back_ref[place] = vec[k]
-                back_ref[step] = image
-            continue
-        for place, out, slot, keep in (
-            (0, to_left, 0, None), (2, to_left, 1, None), (3, to_right, 0, None), (5, to_right, 1, None),
-            (6, to_top, 0, None), (7, to_top, 1, first_keep), (0, to_low, 0, None), (1, to_low, 1, last_keep),
-        ):
-            if place == k:
-                out[slot] = image if keep is None else masked(image, keep)
+                    out[first + place] = vec[k]
+                out[first + step] = image
+        elif k == 0:
+            to_low[0] = masked(image, not_at(last))
+        elif k == 1:
+            to_low[1] = image
+        elif k == 6:
+            to_top[0] = masked(image, not_at(1))
+        elif k == 7:
+            to_top[1] = image
     if final:
         row = sums.write(sums_in[0:1], FIRST_SUM[ITERS])
         sums_ref[...] = jnp.broadcast_to(row, sums_ref.shape)
@@ -337,7 +343,7 @@
     return vec, thetas, fine
 
 
-def combine_kernel(count, num_ref, den_ref, sums_ref, psi_ref, one_ref, two_ref, three_ref, back_ref, out_ref, row_ref):
+def combine_kernel(count, num_ref, den_ref, sums_ref, psi_ref, one_ref, two_ref, three_ref, right_back, left_back, out_ref, row_ref):
     sums = jnp.sum(sums_ref[...], axis=0, keepdims=True) * count
     lanes = lax.broadcasted_iota(jnp.int32, sums.shape, 1)
     entries = [
@@ -359,27 +365,29 @@
     for place, value in enumerate(thetas + [fine]):
         row = place_in(row, place, value)
     row_ref[...] = row
+    held = {where: k for k, where in HELD.items()}
+    back = {(0, 0): (left_back, 0), (2, 1): (right_back, 0), (3, 0): (right_back, 1), (3, 1): (right_back, 2)}
     for i in range(ROWS):
         for j in range(COLS):
-            k = 2 * i + j + (i == 3)
             blocks = [psi_ref[i, j]]
-            if k == 8:
-                blocks += [back_ref[0], back_ref[1], back_ref[2]]
+            if (i, j) in held:
+                blocks += [ref[held[i, j]] for ref in (one_ref, two_ref, three_ref)]
             else:
-                blocks += [one_ref[k], two_ref[k], three_ref[k]]
+                ref, place = back[i, j]
+                blocks += [ref[ITERS * place + step] for step in range(ITERS)]
             total = weights[0] * blocks[0].astype(jnp.float32)
             for weight, block in zip(weights[1:], blocks[1:]):
                 total = total + weight * block.astype(jnp.float32)
             out_ref[i, j] = total.astype(jnp.bfloat16)
 
 
-def move(block, down, right, around):
+def move(block, down, right, skipped=None):
     rows, cols = lax.axis_size("lsec"), lax.axis_size("rsec")
     pairs = [
         (row * cols + col, (row + down) * cols + (col + right) % cols)
         for row in range(rows)
         for col in range(cols)
-        if 0 <= row + down < rows and (around or 0 <= col + right < cols)
+        if 0 <= row + down < rows and col != skipped
     ]
     return lax.ppermute(block, AXES, pairs)
 
@@ -407,55 +415,50 @@
         return jax.ShapeDtypeStruct((number, size, size), jnp.bfloat16)
 
     levels = energies.T
-    pack, to_left, to_up, to_corner, to_low = call(
-        lambda *refs: pack_kernel(last, *refs),
+    to_right, to_left, top, low, corner = call(
+        pack_kernel,
         [VMEM, VMEM, SMEM],
-        [jax.ShapeDtypeStruct((7 * size + 48, size), jnp.bfloat16), blocks(2), blocks(1), blocks(1), blocks(2)],
+        [
+            jax.ShapeDtypeStruct((11 * size + 144, size), jnp.bfloat16),
+            jax.ShapeDtypeStruct((5 * size + 48, size), jnp.bfloat16),
+            blocks(2), blocks(1), blocks(1),
+        ],
         0, psi, right_env, levels,
     )
-    pack = move(pack, 0, 1, True)
-    to_low = move(to_low, -1, 1, True)
-    to_up = move(to_up, 1, 0, False)
-    to_corner = move(to_corner, 1, -1, False)
-    to_left = move(to_left, 0, -1, False)
-    halos = [to_up, to_low, to_left, to_corner]
+    packs = [move(to_right, 0, 1), move(to_left, 0, -1)]
+    halos = [move(top, 1, -1), move(low, -1, 2, last), move(corner, -1, 1)]
     fixed = [levels, left_env, right_env, psi]
     row = jax.ShapeDtypeStruct((8, 128), jnp.float32)
     vecs, sums = [], []
     for step in range(ITERS):
         final = step == ITERS - 1
-        ins = fixed + ([pack] + sums + vecs if step else [])
+        ins = fixed + (packs + sums + vecs if step else [])
         partial, *sums = call(
-            lambda *refs, step=step: near_kernel(step, *refs),
+            lambda *refs, step=step: near_kernel(step, last, *refs),
             [SMEM] + [VMEM] * (len(ins) - 1),
             [jax.ShapeDtypeStruct((BLOCKS, size, size), jnp.float32), row],
-            4 * (24 if step else 20) * size**3, *ins,
+            4 * (28 if step else 12) * size**3, *ins,
         )
-        ins = fixed + [pack, partial] + (sums + vecs if final else vecs[-1:]) + halos
+        ins = fixed + packs + [partial] + (sums + vecs if final else vecs[-1:]) + halos
         if final:
-            outs = [blocks(BLOCKS), blocks(ITERS), jax.ShapeDtypeStruct((devices, 128), jnp.float32)]
+            outs = [blocks(BLOCKS), blocks(3 * ITERS), blocks(ITERS), jax.ShapeDtypeStruct((devices, 128), jnp.float32)]
         else:
-            outs = [blocks(BLOCKS)] + [blocks(2)] * 4
+            outs = [blocks(BLOCKS), blocks(2), blocks(2)]
         result = call(
             lambda *refs, step=step: far_kernel(step, last, *refs),
-            [SMEM] + [VMEM] * (len(ins) - 1), outs, 4 * (8 if step else 12) * size**3, *ins,
+            [SMEM] + [VMEM] * (len(ins) - 1), outs, 4 * (4 if step else 20) * size**3, *ins,
         )
         vecs.append(result[0])
         if not final:
-            to_top, to_low, to_left, to_right = result[1:5]
-            to_top = move(to_top, 1, -1, True)
-            to_low = move(to_low, -1, 1, True)
-            to_left = move(to_left, 0, -1, False)
-            to_right = move(to_right, 0, 1, False)
-            halos = [to_top, to_low, to_right, to_left]
-    sums = [result[-1]]
-    back = move(result[1], 0, -1, True)
-    gathered = lax.all_to_all(sums[0].reshape(devices, 1, 128), AXES, 0, 0).reshape(devices, 128)
+            halos = [move(result[1], 1, -2), move(result[2], -1, 2)]
+    right_back = move(result[1], 0, -1)
+    left_back = move(result[2], 0, 1)
+    gathered = lax.all_to_all(result[3].reshape(devices, 1, 128), AXES, 0, 0).reshape(devices, 128)
     vec, row = call(
         lambda *refs: combine_kernel(count, *refs),
-        [SMEM, SMEM] + [VMEM] * 6,
+        [SMEM, SMEM] + [VMEM] * 7,
         [jax.ShapeDtypeStruct(psi.shape, jnp.bfloat16), jax.ShapeDtypeStruct((1, 128), jnp.float32)],
-        0, coef_num, coef_den, gathered, psi, *vecs, back,
+        0, coef_num, coef_den, gathered, psi, *vecs, right_back, left_back,
     )
     thetas = row[0, :ITERS]
     return lax.cond(

time: 110 us -> 113 us (1.027)
  waiting for transfers between devices: 28.5 us -> 49 us
  starting transfers between devices: 59 us -> 38.7 us
  local copies, waits for them, and re-layouts: 1.13 us -> 3.31 us
    ppermute x14 -> x11, waiting for transfers between devices: 15.5 us -> 36 us  [move(): return lax.ppermute(block, AXES, pairs)]
    ppermute x14 -> x11, starting transfers between devices: 39.3 us -> 27 us  [move(): return lax.ppermute(block, AXES, pairs)]
    all_to_all x1, starting transfers between devices: 19.7 us -> 11.7 us  [per_device(): lax.all_to_all(result[3].reshape(devices, 1, 128), AXES, 0, 0)]
    unnamed x16 -> x20, local copies, waits for them, and re-layouts: 0.54 us -> 2.73 us
  transfers between devices with their start and end apart: 15 -> 12, of which waited for: 8 -> 7; matrix products, arithmetic and copies ran while one was open for 0% -> 0% of each run, Pallas kernels for 8% -> 7%
where the time goes in v4:
time: 113 us
  waiting for transfers between devices  49 us (43%)
  starting transfers between devices  38.7 us (34%)
  Pallas kernels  20.1 us (18%)
  local copies, waits for them, and re-layouts  3.31 us (3%)
  between operations  1.51 us (1%)
    ppermute x11, waiting for transfers between devices, move(): return lax.ppermute(block, AXES, pairs)  36 us
    ppermute x11, starting transfers between devices, move(): return lax.ppermute(block, AXES, pairs)  27 us
    pallas_call x8, Pallas kernels, call(): pl.pallas_call(kernel, in_specs=in_specs, out_specs=[VMEM] * len(out_shap...  20.1 us
    all_to_all x1, waiting for transfers between devices, per_device(): lax.all_to_all(result[3].reshape(devices, 1, 128), AXES, 0, 0)  12.9 us
    all_to_all x1, starting transfers between devices, per_device(): lax.all_to_all(result[3].reshape(devices, 1, 128), AXES, 0, 0)  11.7 us
    unnamed x20, local copies, waits for them, and re-layouts  2.73 us
  transfers between devices with their start and end apart: 12, of which 7 were waited for; matrix products, arithmetic and copies ran while one was open for 0% of the time, Pallas kernels for 7%

profile of v4, /device:TPU:1, one launch (start us, length us, event | category | flops | bytes accessed | tf_op | source)
XLA Modules:
  0.0 112.8 jit_solution(3659254552586962924)
XLA Ops:
  0.6 0.0 copy-start.2
  0.6 0.0 copy-start.8
  0.7 0.0 copy-start.15
  0.7 1.9 %shard_map.81 = (bf16[2960,256]{1,0:T(8,128)(2,1)S(1)}, bf16[1328,256]{1,0:T(8,128)(2,1)S(1)}, bf16[2,256,256]{2,1,0:T(8,128)(2,1)S(1)}, bf16[1,256,256]{2,1,0:T(8,128)(2,1)S(1)}, bf16[1,256,256]{2,1,0:T(8,128)(2,1)S(1)}) custom-call(bf16[4,2,256,256]{3,2,1,0:T(8,128)(2,1)} %refs_3_.13, bf16[2,4,256,256]{3,2,1,0:T(8,128)(2,1)} %refs_2_.11, f32[2,4]{1,0:T(2,128)} %bitcast.186), custom_call_target="tpu_custom_call" | custom-call | bytes 4816928 | tf_op jit(solution)/shard_map/pallas_call | solution.py:398
  2.5 2.8 %collective-permute-start.18 = (bf16[2960,256]{1,0:T(8,128)(2,1)S(1)}, bf16[2960,256]{1,0:T(8,128)(2,1)S(1)}, u32[]{:S(2)}, u32[]{:S(2)}) collective-permute-start(bf16[2960,256]{1,0:T(8,128)(2,1)S(1)} %get-tuple-element.53), channel_id=1, source_target_pairs={{0,1},{1,2},{2,3},{3,4},{4,5},{5,6},{6,7},{7,8},{8,9},{9,10},{10,1... | collective-permute-start | bytes 4546568 | tf_op jit(solution)/shard_map/ppermute | solution.py:392
  5.3 0.6 collective-permute-start.19
  6.0 9.0 %collective-permute-start.20 = (bf16[2,256,256]{2,1,0:T(8,128)(2,1)S(1)}, bf16[2,256,256]{2,1,0:T(8,128)(2,1)S(1)}, u32[]{:S(2)}, u32[]{:S(2)}) collective-permute-start(bf16[2,256,256]{2,1,0:T(8,128)(2,1)S(1)} %get-tuple-element.57), channel_id=1, source_target_pairs={{0,63},{1,32},{2,33},{3,34},{4,35},{5,36},{6,37},{7,38},{8,39},{9,... | collective-permute-start | bytes 786440 | tf_op jit(solution)/shard_map/ppermute | solution.py:392
  14.9 0.7 collective-permute-start.21
  15.6 0.0 copy-start.6
  15.6 1.4 %collective-permute-start.22 = (bf16[1,256,256]{2,1,0:T(8,128)(2,1)S(1)}, bf16[1,256,256]{2,1,0:T(8,128)(2,1)S(1)}, u32[]{:S(2)}, u32[]{:S(2)}) collective-permute-start(bf16[1,256,256]{2,1,0:T(8,128)(2,1)S(1)} %get-tuple-element.59), channel_id=1, source_target_pairs={{32,1},{33,2},{34,3},{35,4},{36,5},{37,6},{38,7},{39,8},{40,9},{41... | collective-permute-start | bytes 393224 | tf_op jit(solution)/shard_map/ppermute | solution.py:392
  17.1 0.0 copy-done.2
  17.1 0.0 copy-done.8
  17.1 0.0 copy-done.15
  17.1 2.7 %shard_map.82 = (f32[8,256,256]{2,1,0:T(8,128)S(1)}, f32[8,128]{1,0:T(8,128)S(1)}) custom-call(f32[2,4]{1,0:T(2,128)S(1)} %bitcast.187, bf16[4,4,256,256]{3,2,1,0:T(8,128)(2,1)} %refs_1_.12, bf16[2,4,256,256]{3,2,1,0:T(8,128)(2,1)S(1)} %copy-done.8, bf16[4,2,256,256]{3,2,1,0:T(8,128)(2,1)S(1)} %copy-done.2), custom_call_target="tpu_custom_call" | custom-call | flops 805306368 | bytes 6295584 | tf_op jit(solution)/shard_map/pallas_call | solution.py:398
  19.8 0.0 collective-permute-done.21.refs_8_
  19.8 5.5 %collective-permute-done.22.refs_9_ = bf16[1,256,256]{2,1,0:T(8,128)(2,1)S(1)} collective-permute-done((bf16[1,256,256]{2,1,0:T(8,128)(2,1)S(1)}, bf16[1,256,256]{2,1,0:T(8,128)(2,1)S(1)}, u32[]{:S(2)}, u32[]{:S(2)}) %collective-permute-start.22) | collective-permute-done | bytes 131104 | tf_op jit(solution)/shard_map/ppermute | solution.py:392
  25.3 8.2 %collective-permute-done.20.refs_7_ = bf16[2,256,256]{2,1,0:T(8,128)(2,1)S(1)} collective-permute-done((bf16[2,256,256]{2,1,0:T(8,128)(2,1)S(1)}, bf16[2,256,256]{2,1,0:T(8,128)(2,1)S(1)}, u32[]{:S(2)}, u32[]{:S(2)}) %collective-permute-start.20) | collective-permute-done | bytes 262176 | tf_op jit(solution)/shard_map/ppermute | solution.py:392
  33.6 2.5 %collective-permute-done.19.refs_5_ = bf16[1328,256]{1,0:T(8,128)(2,1)S(1)} collective-permute-done((bf16[1328,256]{1,0:T(8,128)(2,1)S(1)}, bf16[1328,256]{1,0:T(8,128)(2,1)S(1)}, u32[]{:S(2)}, u32[]{:S(2)}) %collective-permute-start.19) | collective-permute-done | bytes 679968 | tf_op jit(solution)/shard_map/ppermute | solution.py:392
  36.0 0.0 collective-permute-done.18.refs_4_
  36.0 0.0 copy-done.6
  36.0 2.2 %shard_map.83 = (bf16[8,256,256]{2,1,0:T(8,128)(2,1)S(1)}, bf16[2,256,256]{2,1,0:T(8,128)(2,1)S(1)}, bf16[2,256,256]{2,1,0:T(8,128)(2,1)S(1)}) custom-call(f32[2,4]{1,0:T(2,128)S(1)} %bitcast.188, bf16[4,4,256,256]{3,2,1,0:T(8,128)(2,1)S(1)} %copy-done.6, bf16[2,4,256,256]{3,2,1,0:T(8,128)(2,1)S(1)} %copy-done.8, bf16[4,2,256,256]{3,2,1,0:T(8,128)(2,1)S(1)} %copy-done.2, ...), custom_call_target="tpu_custom_call" | custom-call | flops 1342177280 | bytes 10584096 | tf_op jit(solution)/shard_map/pallas_call | solution.py:398
  38.3 1.3 %collective-permute-start.23 = (bf16[2,256,256]{2,1,0:T(8,128)(2,1)S(1)}, bf16[2,256,256]{2,1,0:T(8,128)(2,1)S(1)}, u32[]{:S(2)}, u32[]{:S(2)}) collective-permute-start(bf16[2,256,256]{2,1,0:T(8,128)(2,1)S(1)} %get-tuple-element.63), channel_id=1, source_target_pairs={{0,62},{1,63},{2,32},{3,33},{4,34},{5,35},{6,36},{7,37},{8,38},{9,... | collective-permute-start | bytes 786440 | tf_op jit(solution)/shard_map/ppermute | solution.py:392
  39.6 1.3 %collective-permute-start.24 = (bf16[2,256,256]{2,1,0:T(8,128)(2,1)S(1)}, bf16[2,256,256]{2,1,0:T(8,128)(2,1)S(1)}, u32[]{:S(2)}, u32[]{:S(2)}) collective-permute-start(bf16[2,256,256]{2,1,0:T(8,128)(2,1)S(1)} %get-tuple-element.64), channel_id=1, source_target_pairs={{32,2},{33,3},{34,4},{35,5},{36,6},{37,7},{38,8},{39,9},{40,10},{4... | collective-permute-start | bytes 786440 | tf_op jit(solution)/shard_map/ppermute | solution.py:392
  40.9 2.8 %shard_map.84 = (f32[8,256,256]{2,1,0:T(8,128)S(1)}, f32[8,128]{1,0:T(8,128)S(1)}) custom-call(f32[2,4]{1,0:T(2,128)S(1)} %bitcast.189, bf16[4,4,256,256]{3,2,1,0:T(8,128)(2,1)S(1)} %copy-done.6, bf16[2,4,256,256]{3,2,1,0:T(8,128)(2,1)S(1)} %copy-done.8, bf16[4,2,256,256]{3,2,1,0:T(8,128)(2,1)S(1)} %copy-done.2, ...), custom_call_target="tpu_custom_call" | custom-call | flops 1879048192 | bytes 9543712 | tf_op jit(solution)/shard_map/pallas_call | solution.py:398
  43.6 0.0 collective-permute-done.23.refs_8_
  43.7 11.5 %collective-permute-done.24.refs_9_ = bf16[2,256,256]{2,1,0:T(8,128)(2,1)S(1)} collective-permute-done((bf16[2,256,256]{2,1,0:T(8,128)(2,1)S(1)}, bf16[2,256,256]{2,1,0:T(8,128)(2,1)S(1)}, u32[]{:S(2)}, u32[]{:S(2)}) %collective-permute-start.24) | collective-permute-done | bytes 262176 | tf_op jit(solution)/shard_map/ppermute | solution.py:392
  55.2 1.1 shard_map.85
  56.3 6.9 %collective-permute-start.25 = (bf16[2,256,256]{2,1,0:T(8,128)(2,1)S(1)}, bf16[2,256,256]{2,1,0:T(8,128)(2,1)S(1)}, u32[]{:S(2)}, u32[]{:S(2)}) collective-permute-start(bf16[2,256,256]{2,1,0:T(8,128)(2,1)S(1)} %get-tuple-element.68), channel_id=1, source_target_pairs={{0,62},{1,63},{2,32},{3,33},{4,34},{5,35},{6,36},{7,37},{8,38},{9,... | collective-permute-start | bytes 786440 | tf_op jit(solution)/shard_map/ppermute | solution.py:392
  63.2 1.3 %collective-permute-start.26 = (bf16[2,256,256]{2,1,0:T(8,128)(2,1)S(1)}, bf16[2,256,256]{2,1,0:T(8,128)(2,1)S(1)}, u32[]{:S(2)}, u32[]{:S(2)}) collective-permute-start(bf16[2,256,256]{2,1,0:T(8,128)(2,1)S(1)} %get-tuple-element.69), channel_id=1, source_target_pairs={{32,2},{33,3},{34,4},{35,5},{36,6},{37,7},{38,8},{39,9},{40,10},{4... | collective-permute-start | bytes 786440 | tf_op jit(solution)/shard_map/ppermute | solution.py:392
  64.5 2.8 %shard_map.86 = (f32[8,256,256]{2,1,0:T(8,128)S(1)}, f32[8,128]{1,0:T(8,128)S(1)}) custom-call(f32[2,4]{1,0:T(2,128)S(1)} %bitcast.191, bf16[4,4,256,256]{3,2,1,0:T(8,128)(2,1)S(1)} %copy-done.6, bf16[2,4,256,256]{3,2,1,0:T(8,128)(2,1)S(1)} %copy-done.8, bf16[4,2,256,256]{3,2,1,0:T(8,128)(2,1)S(1)} %copy-done.2, ...), custom_call_target="tpu_custom_call" | custom-call | flops 1879048192 | bytes 10592288 | tf_op jit(solution)/shard_map/pallas_call | solution.py:398
  67.3 2.2 %collective-permute-done.25.refs_10_ = bf16[2,256,256]{2,1,0:T(8,128)(2,1)S(1)} collective-permute-done((bf16[2,256,256]{2,1,0:T(8,128)(2,1)S(1)}, bf16[2,256,256]{2,1,0:T(8,128)(2,1)S(1)}, u32[]{:S(2)}, u32[]{:S(2)}) %collective-permute-start.25) | collective-permute-done | bytes 262176 | tf_op jit(solution)/shard_map/ppermute | solution.py:392
  69.5 6.1 %collective-permute-done.26.refs_11_ = bf16[2,256,256]{2,1,0:T(8,128)(2,1)S(1)} collective-permute-done((bf16[2,256,256]{2,1,0:T(8,128)(2,1)S(1)}, bf16[2,256,256]{2,1,0:T(8,128)(2,1)S(1)}, u32[]{:S(2)}, u32[]{:S(2)}) %collective-permute-start.26) | collective-permute-done | bytes 262176 | tf_op jit(solution)/shard_map/ppermute | solution.py:392
  75.6 0.0 copy-start.16
  75.6 0.0 copy-start.17
  75.6 3.0 %shard_map.87 = (bf16[8,256,256]{2,1,0:T(8,128)(2,1)S(1)}, bf16[9,256,256]{2,1,0:T(8,128)(2,1)}, bf16[3,256,256]{2,1,0:T(8,128)(2,1)}, f32[256,128]{1,0:T(8,128)}) custom-call(f32[2,4]{1,0:T(2,128)S(1)} %bitcast.192, bf16[4,4,256,256]{3,2,1,0:T(8,128)(2,1)S(1)} %copy-done.6, bf16[2,4,256,256]{3,2,1,0:T(8,128)(2,1)S(1)} %copy-done.8, ...), custom_call_target="tpu_custom_call" | custom-call | flops 268435456 | bytes 13864992 | tf_op jit(solution)/shard_map/pallas_call | solution.py:398
  78.6 0.0 copy-start
  78.6 1.0 copy-done
  79.6 1.5 %collective-permute-start.27 = (bf16[9,256,256]{2,1,0:T(8,128)(2,1)}, bf16[9,256,256]{2,1,0:T(8,128)(2,1)S(1)}, u32[]{:S(2)}, u32[]{:S(2)}) collective-permute-start(bf16[9,256,256]{2,1,0:T(8,128)(2,1)} %get-tuple-element.72), channel_id=1, source_target_pairs={{0,31},{1,0},{2,1},{3,2},{4,3},{5,4},{6,5},{7,6},{8,7},{9,8},{10,9... | collective-permute-start | bytes 3538952 | tf_op jit(solution)/shard_map/ppermute | solution.py:392
  81.1 0.2 collective-permute-start.28
  81.3 11.7 %all-to-all-start = ((f32[256,1,128]{2,1,0:T(1,128)}), f32[256,1,128]{2,1,0:T(1,128)S(1)}, u32[]{:S(2)}, u32[]{:S(2)}) async-start(f32[256,1,128]{2,1,0:T(1,128)} %bitcast.56), calls=%async_computation | async-start | bytes 262144 | tf_op jit(solution)/shard_map/all_to_all | solution.py:456
  93.0 12.9 %all-to-all-done = f32[256,1,128]{2,1,0:T(1,128)S(1)} async-done(((f32[256,1,128]{2,1,0:T(1,128)}), f32[256,1,128]{2,1,0:T(1,128)S(1)}, u32[]{:S(2)}, u32[]{:S(2)}) %all-to-all-start) | async-done | bytes 131104 | tf_op jit(solution)/shard_map/all_to_all | solution.py:456
  105.9 0.0 collective-permute-done.28.refs_8_
  105.9 0.0 collective-permute-done.27.refs_7_
  105.9 0.0 copy-done.16
  105.9 0.0 copy-done.17
  105.9 0.0 copy-start.1
  105.9 1.2 %copy-done.1 = bf16[8,256,256]{2,1,0:T(8,128)(2,1)S(1)} copy-done((bf16[8,256,256]{2,1,0:T(8,128)(2,1)S(1)}, bf16[8,256,256]{2,1,0:T(8,128)(2,1)}, u32[]{:S(2)}) %copy-start.1) | copy-done | bytes 1048600
  107.2 0.0 copy-start.3
  107.2 3.6 %shard_map.88 = (bf16[4,2,256,256]{3,2,1,0:T(8,128)(2,1)}, f32[1,128]{1,0:T(1,128)S(1)}) custom-call(s32[2]{0:T(128)S(1)} %copy-done.16, s32[2]{0:T(128)S(1)} %copy-done.17, f32[256,128]{1,0:T(8,128)S(1)} %bitcast.185, bf16[4,2,256,256]{3,2,1,0:T(8,128)(2,1)} %refs_3_.13, bf16[8,256,256]{2,1,0:T(8,128)(2,1)S(1)} %get-tuple-element.60.refs_7_.refs_8_.refs_4_, ...), custom_call_target="tpu_custom_call" | custom-call | bytes 6947344 | tf_op jit(solution)/shard_map/pallas_call | solution.py:398
  110.8 0.6 slice.131
  112.0 0.0 copy-done.3
  112.0 0.2 conditional.1
  112.3 0.0 copy-start.18
  112.3 0.5 copy-done.18
  (1 shorter events, 0.0 us)
Async XLA Ops:
  0.6 16.4 %copy-start.2 = (bf16[4,2,256,256]{3,2,1,0:T(8,128)(2,1)S(1)}, bf16[4,2,256,256]{3,2,1,0:T(8,128)(2,1)}, u32[]{:S(2)}) copy-start(bf16[4,2,256,256]{3,2,1,0:T(8,128)(2,1)} %refs_3_.13) | copy-start | bytes 3145732
  0.6 16.4 %copy-start.8 = (bf16[2,4,256,256]{3,2,1,0:T(8,128)(2,1)S(1)}, bf16[2,4,256,256]{3,2,1,0:T(8,128)(2,1)}, u32[]{:S(2)}) copy-start(bf16[2,4,256,256]{3,2,1,0:T(8,128)(2,1)} %refs_2_.11) | copy-start | bytes 3145732
  0.7 16.4 %copy-start.15 = (f32[4,2]{0,1:T(2,128)S(1)}, f32[4,2]{0,1:T(2,128)}, u32[]{:S(2)}) copy-start(f32[4,2]{0,1:T(2,128)} %param.11) | copy-start | bytes 100
  2.5 33.5 %collective-permute-start.18 = (bf16[2960,256]{1,0:T(8,128)(2,1)S(1)}, bf16[2960,256]{1,0:T(8,128)(2,1)S(1)}, u32[]{:S(2)}, u32[]{:S(2)}) collective-permute-start(bf16[2960,256]{1,0:T(8,128)(2,1)S(1)} %get-tuple-element.53), channel_id=1, source_target_pairs={{0,1},{1,2},{2,3},{3,4},{4,5},{5,6},{6,7},{7,8},{8,9},{9,10},{10,1... | collective-permute-start | bytes 4546568 | tf_op jit(solution)/shard_map/ppermute | solution.py:392
  5.3 30.7 %collective-permute-start.19 = (bf16[1328,256]{1,0:T(8,128)(2,1)S(1)}, bf16[1328,256]{1,0:T(8,128)(2,1)S(1)}, u32[]{:S(2)}, u32[]{:S(2)}) collective-permute-start(bf16[1328,256]{1,0:T(8,128)(2,1)S(1)} %get-tuple-element.54), channel_id=1, source_target_pairs={{0,31},{1,0},{2,1},{3,2},{4,3},{5,4},{6,5},{7,6},{8,7},{9,8},{10,9... | collective-permute-start | bytes 2039816 | tf_op jit(solution)/shard_map/ppermute | solution.py:392
  6.0 27.6 %collective-permute-start.20 = (bf16[2,256,256]{2,1,0:T(8,128)(2,1)S(1)}, bf16[2,256,256]{2,1,0:T(8,128)(2,1)S(1)}, u32[]{:S(2)}, u32[]{:S(2)}) collective-permute-start(bf16[2,256,256]{2,1,0:T(8,128)(2,1)S(1)} %get-tuple-element.57), channel_id=1, source_target_pairs={{0,63},{1,32},{2,33},{3,34},{4,35},{5,36},{6,37},{7,38},{8,39},{9,... | collective-permute-start | bytes 786440 | tf_op jit(solution)/shard_map/ppermute | solution.py:392
  14.9 4.9 %collective-permute-start.21 = (bf16[1,256,256]{2,1,0:T(8,128)(2,1)S(1)}, bf16[1,256,256]{2,1,0:T(8,128)(2,1)S(1)}, u32[]{:S(2)}, u32[]{:S(2)}) collective-permute-start(bf16[1,256,256]{2,1,0:T(8,128)(2,1)S(1)} %get-tuple-element.58), channel_id=1, source_target_pairs={{32,2},{33,3},{34,4},{35,5},{36,6},{37,7},{38,8},{39,9},{40,10},{4... | collective-permute-start | bytes 393224 | tf_op jit(solution)/shard_map/ppermute | solution.py:392
  15.6 20.4 %copy-start.6 = (bf16[4,4,256,256]{3,2,1,0:T(8,128)(2,1)S(1)}, bf16[4,4,256,256]{3,2,1,0:T(8,128)(2,1)}, u32[]{:S(2)}) copy-start(bf16[4,4,256,256]{3,2,1,0:T(8,128)(2,1)} %refs_1_.12) | copy-start | bytes 6291460
  15.6 9.7 %collective-permute-start.22 = (bf16[1,256,256]{2,1,0:T(8,128)(2,1)S(1)}, bf16[1,256,256]{2,1,0:T(8,128)(2,1)S(1)}, u32[]{:S(2)}, u32[]{:S(2)}) collective-permute-start(bf16[1,256,256]{2,1,0:T(8,128)(2,1)S(1)} %get-tuple-element.59), channel_id=1, source_target_pairs={{32,1},{33,2},{34,3},{35,4},{36,5},{37,6},{38,7},{39,8},{40,9},{41... | collective-permute-start | bytes 393224 | tf_op jit(solution)/shard_map/ppermute | solution.py:392
  38.3 5.4 %collective-permute-start.23 = (bf16[2,256,256]{2,1,0:T(8,128)(2,1)S(1)}, bf16[2,256,256]{2,1,0:T(8,128)(2,1)S(1)}, u32[]{:S(2)}, u32[]{:S(2)}) collective-permute-start(bf16[2,256,256]{2,1,0:T(8,128)(2,1)S(1)} %get-tuple-element.63), channel_id=1, source_target_pairs={{0,62},{1,63},{2,32},{3,33},{4,34},{5,35},{6,36},{7,37},{8,38},{9,... | collective-permute-start | bytes 786440 | tf_op jit(solution)/shard_map/ppermute | solution.py:392
  39.6 15.6 %collective-permute-start.24 = (bf16[2,256,256]{2,1,0:T(8,128)(2,1)S(1)}, bf16[2,256,256]{2,1,0:T(8,128)(2,1)S(1)}, u32[]{:S(2)}, u32[]{:S(2)}) collective-permute-start(bf16[2,256,256]{2,1,0:T(8,128)(2,1)S(1)} %get-tuple-element.64), channel_id=1, source_target_pairs={{32,2},{33,3},{34,4},{35,5},{36,6},{37,7},{38,8},{39,9},{40,10},{4... | collective-permute-start | bytes 786440 | tf_op jit(solution)/shard_map/ppermute | solution.py:392
  56.3 13.2 %collective-permute-start.25 = (bf16[2,256,256]{2,1,0:T(8,128)(2,1)S(1)}, bf16[2,256,256]{2,1,0:T(8,128)(2,1)S(1)}, u32[]{:S(2)}, u32[]{:S(2)}) collective-permute-start(bf16[2,256,256]{2,1,0:T(8,128)(2,1)S(1)} %get-tuple-element.68), channel_id=1, source_target_pairs={{0,62},{1,63},{2,32},{3,33},{4,34},{5,35},{6,36},{7,37},{8,38},{9,... | collective-permute-start | bytes 786440 | tf_op jit(solution)/shard_map/ppermute | solution.py:392
  63.2 12.4 %collective-permute-start.26 = (bf16[2,256,256]{2,1,0:T(8,128)(2,1)S(1)}, bf16[2,256,256]{2,1,0:T(8,128)(2,1)S(1)}, u32[]{:S(2)}, u32[]{:S(2)}) collective-permute-start(bf16[2,256,256]{2,1,0:T(8,128)(2,1)S(1)} %get-tuple-element.69), channel_id=1, source_target_pairs={{32,2},{33,3},{34,4},{35,5},{36,6},{37,7},{38,8},{39,9},{40,10},{4... | collective-permute-start | bytes 786440 | tf_op jit(solution)/shard_map/ppermute | solution.py:392
  75.6 30.4 %copy-start.16 = (s32[2]{0:T(128)S(1)}, s32[2]{0:T(128)}, u32[]{:S(2)}) copy-start(s32[2]{0:T(128)} %refs_0_.1) | copy-start | bytes 28
  75.6 30.4 %copy-start.17 = (s32[2]{0:T(128)S(1)}, s32[2]{0:T(128)}, u32[]{:S(2)}) copy-start(s32[2]{0:T(128)} %refs_1_.13) | copy-start | bytes 28
  78.6 1.0 copy-start
  79.6 26.3 %collective-permute-start.27 = (bf16[9,256,256]{2,1,0:T(8,128)(2,1)}, bf16[9,256,256]{2,1,0:T(8,128)(2,1)S(1)}, u32[]{:S(2)}, u32[]{:S(2)}) collective-permute-start(bf16[9,256,256]{2,1,0:T(8,128)(2,1)} %get-tuple-element.72), channel_id=1, source_target_pairs={{0,31},{1,0},{2,1},{3,2},{4,3},{5,4},{6,5},{7,6},{8,7},{9,8},{10,9... | collective-permute-start | bytes 3538952 | tf_op jit(solution)/shard_map/ppermute | solution.py:392
  81.1 24.8 %collective-permute-start.28 = (bf16[3,256,256]{2,1,0:T(8,128)(2,1)}, bf16[3,256,256]{2,1,0:T(8,128)(2,1)}, u32[]{:S(2)}, u32[]{:S(2)}) collective-permute-start(bf16[3,256,256]{2,1,0:T(8,128)(2,1)} %get-tuple-element.73), channel_id=1, source_target_pairs={{0,1},{1,2},{2,3},{3,4},{4,5},{5,6},{6,7},{7,8},{8,9},{9,10},{10,1... | collective-permute-start | bytes 1179656 | tf_op jit(solution)/shard_map/ppermute | solution.py:392
  81.3 24.6 %all-to-all-start = ((f32[256,1,128]{2,1,0:T(1,128)}), f32[256,1,128]{2,1,0:T(1,128)S(1)}, u32[]{:S(2)}, u32[]{:S(2)}) async-start(f32[256,1,128]{2,1,0:T(1,128)} %bitcast.56), calls=%async_computation | async-start | bytes 262144 | tf_op jit(solution)/shard_map/all_to_all | solution.py:456
  105.9 1.2 %copy-start.1 = (bf16[8,256,256]{2,1,0:T(8,128)(2,1)S(1)}, bf16[8,256,256]{2,1,0:T(8,128)(2,1)}, u32[]{:S(2)}) copy-start(bf16[8,256,256]{2,1,0:T(8,128)(2,1)} %copy-done) | copy-start | bytes 3145732
  107.2 4.9 %copy-start.3 = (bf16[4,2,256,256]{3,2,1,0:T(8,128)(2,1)S(1)}, bf16[4,2,256,256]{3,2,1,0:T(8,128)(2,1)}, u32[]{:S(2)}) copy-start(bf16[4,2,256,256]{3,2,1,0:T(8,128)(2,1)} %refs_3_.13) | copy-start | bytes 3145732
  112.3 0.5 copy-start.18

commit v5 on v4

--- a/solution.py
+++ b/solution.py
@@ -91,9 +91,10 @@
 
 ROWS, COLS, BLOCKS = 4, 2, 8
 SUMS = 10
+SIDE_TERMS = 2
 VMEM = pl.BlockSpec(memory_space=pltpu.VMEM)
 SMEM = pl.BlockSpec(memory_space=pltpu.SMEM)
-PARAMS = pltpu.CompilerParams(vmem_limit_bytes=40 * 1024 * 1024)
+PARAMS = pltpu.CompilerParams(vmem_limit_bytes=24 * 1024 * 1024)
 
 
 def dot(left, right):
@@ -124,17 +125,20 @@
         rest = rest - part.astype(jnp.float32)
 
 
-def pack_kernel(psi_ref, right_ref, energy_ref, right_out, left_out, top_out, low_out, corner_out):
+def pack_kernel(psi_ref, right_ref, energy_ref, side_out, right_out, left_out, top_out, low_out, corner_out):
     size = psi_ref.shape[-1]
     for place, (i, j) in enumerate(((2, 1), (3, 0), (3, 1))):
         right_out[place * size : (place + 1) * size] = psi_ref[i, j]
-        write_energy(right_out, 11 * size + 48 * place, energy_ref[j, i])
+        write_energy(right_out, 5 * size + 48 * place, energy_ref[j, i])
     left_out[:size] = psi_ref[0, 0]
     write_energy(left_out, 5 * size, energy_ref[0, 0])
     for term in range(4):
-        for col in range(COLS):
-            start = (3 + 4 * col + term) * size
-            right_out[start : start + size] = right_ref[col, term]
+        side_out[term] = right_ref[0, term]
+        if term < SIDE_TERMS:
+            side_out[4 + term] = right_ref[1, term]
+        else:
+            start = (3 + term - SIDE_TERMS) * size
+            right_out[start : start + size] = right_ref[1, term]
         left_out[(1 + term) * size : (2 + term) * size] = right_ref[0, term]
     top_out[0] = masked(psi_ref[3, 0], not_at(0))
     top_out[1] = psi_ref[3, 1]
@@ -149,13 +153,12 @@
 
 HELD = {0: (0, 1), 2: (1, 0), 3: (1, 1), 5: (2, 0)}
 PACKED = {4: 0, 6: 1, 7: 2}
-COLUMN = {4: 1, 6: 0, 7: 1}
 
 
 class Blocks:
     def __init__(self, step, psi_ref, packs, vec_ref, halo_refs, last):
         self.step, self.psi_ref, self.vec_ref, self.halo_refs = step, psi_ref, vec_ref, halo_refs
-        self.from_left, self.from_right = packs
+        self.side, self.from_left, self.from_right = packs
         self.size = psi_ref.shape[-1]
         first, last = not_at(0), not_at(last)
         self.cut = {(4, 2): first, (7, 5): first, (3, 1): last}
@@ -193,7 +196,11 @@
             return right_ref[HELD[k][1], term]
         if k == 1:
             return self.from_right[(1 + term) * self.size : (2 + term) * self.size]
-        start = (3 + 4 * COLUMN[k] + term) * self.size
+        if k == 6:
+            return self.side[term]
+        if term < SIDE_TERMS:
+            return self.side[4 + term]
+        start = (3 + term - SIDE_TERMS) * self.size
         return self.from_left[start : start + self.size]
 
     def term(self, k, term, left_ref, right_ref):
@@ -208,7 +215,7 @@
         if k in HELD:
             i, j = HELD[k]
             return energy_ref[j, i] - SHIFT
-        ref, start = (self.from_right, 5 * self.size) if k == 1 else (self.from_left, 11 * self.size + 48 * PACKED[k])
+        ref, start = (self.from_right, 5 * self.size) if k == 1 else (self.from_left, 5 * self.size + 48 * PACKED[k])
         parts = [ref[start + 16 * i : start + 16 * i + 16].astype(jnp.float32) for i in range(3)]
         return sum(parts)[:1] - SHIFT
 
@@ -235,9 +242,9 @@
 def near_kernel(step, last, *refs):
     energy_ref, left_ref, right_ref, psi_ref, *refs = refs
     if step == 0:
-        packs, vecs = (None, None), []
+        packs, vecs = (None, None, None), []
     else:
-        packs, sums_in, vecs, refs = refs[:2], refs[2], refs[3 : 3 + step], refs[3 + step :]
+        packs, sums_in, vecs, refs = refs[:3], refs[3], refs[4 : 4 + step], refs[4 + step :]
     total_ref, sums_ref = refs
     blocks = Blocks(step, psi_ref, packs, vecs[-1] if vecs else None, (), last)
     sums = Sums(step + 1, blocks.size)
@@ -265,7 +272,7 @@
 
 def far_kernel(step, last, *refs):
     energy_ref, left_ref, right_ref, psi_ref, *refs = refs
-    packs, total_ref, refs = refs[:2], refs[2], refs[3:]
+    packs, total_ref, refs = refs[:3], refs[3], refs[4:]
     final = step == ITERS - 1
     if final:
         sums_in, vecs, refs = refs[0], refs[1 : 1 + step], refs[1 + step :]
@@ -343,7 +350,7 @@
     return vec, thetas, fine
 
 
-def combine_kernel(count, num_ref, den_ref, sums_ref, psi_ref, one_ref, two_ref, three_ref, right_back, left_back, out_ref, row_ref):
+def combine_kernel(count, num_ref, den_ref, sums_ref, psi_ref, one_ref, two_ref, three_ref, right_back, left_back, out_ref, theta_ref, fine_ref):
     sums = jnp.sum(sums_ref[...], axis=0, keepdims=True) * count
     lanes = lax.broadcasted_iota(jnp.int32, sums.shape, 1)
     entries = [
@@ -361,10 +368,9 @@
         den = jnp.full(entries[0].shape, den_ref[step], jnp.int32).astype(jnp.float32)
         coefs.append(num / den)
     weights, thetas, fine = recursion(gram, coefs)
-    row = jnp.zeros((1, 128), jnp.float32)
-    for place, value in enumerate(thetas + [fine]):
-        row = place_in(row, place, value)
-    row_ref[...] = row
+    for place, value in enumerate(thetas):
+        theta_ref[place] = jnp.max(value)
+    fine_ref[0] = jnp.max(fine)
     held = {where: k for k, where in HELD.items()}
     back = {(0, 0): (left_back, 0), (2, 1): (right_back, 0), (3, 0): (right_back, 1), (3, 1): (right_back, 2)}
     for i in range(ROWS):
@@ -383,12 +389,12 @@
 
 def move(block, down, right, skipped=None):
     rows, cols = lax.axis_size("lsec"), lax.axis_size("rsec")
-    pairs = [
-        (row * cols + col, (row + down) * cols + (col + right) % cols)
-        for row in range(rows)
-        for col in range(cols)
-        if 0 <= row + down < rows and col != skipped
-    ]
+    pairs = []
+    for row in range(rows):
+        target = row ^ 1 if down == "twin" else row + down
+        for col in range(cols):
+            if 0 <= target < rows and col != skipped:
+                pairs.append((row * cols + col, target * cols + (col + right) % cols))
     return lax.ppermute(block, AXES, pairs)
 
 
@@ -398,7 +404,7 @@
     return pl.pallas_call(
         kernel,
         in_specs=in_specs,
-        out_specs=[VMEM] * len(out_shapes),
+        out_specs=[SMEM if len(shape.shape) == 1 else VMEM for shape in out_shapes],
         out_shape=out_shapes,
         compiler_params=PARAMS,
         cost_estimate=pl.CostEstimate(flops=flops, bytes_accessed=nbytes, transcendentals=0),
@@ -415,17 +421,18 @@
         return jax.ShapeDtypeStruct((number, size, size), jnp.bfloat16)
 
     levels = energies.T
-    to_right, to_left, top, low, corner = call(
+    side, to_right, to_left, top, low, corner = call(
         pack_kernel,
         [VMEM, VMEM, SMEM],
         [
-            jax.ShapeDtypeStruct((11 * size + 144, size), jnp.bfloat16),
+            blocks(4 + SIDE_TERMS),
+            jax.ShapeDtypeStruct((5 * size + 144, size), jnp.bfloat16),
             jax.ShapeDtypeStruct((5 * size + 48, size), jnp.bfloat16),
             blocks(2), blocks(1), blocks(1),
         ],
         0, psi, right_env, levels,
     )
-    packs = [move(to_right, 0, 1), move(to_left, 0, -1)]
+    packs = [move(side, "twin", 1), move(to_right, 0, 1), move(to_left, 0, -1)]
     halos = [move(top, 1, -1), move(low, -1, 2, last), move(corner, -1, 1)]
     fixed = [levels, left_env, right_env, psi]
     row = jax.ShapeDtypeStruct((8, 128), jnp.float32)
@@ -454,15 +461,18 @@
     right_back = move(result[1], 0, -1)
     left_back = move(result[2], 0, 1)
     gathered = lax.all_to_all(result[3].reshape(devices, 1, 128), AXES, 0, 0).reshape(devices, 128)
-    vec, row = call(
+    vec, thetas, fine = call(
         lambda *refs: combine_kernel(count, *refs),
         [SMEM, SMEM] + [VMEM] * 7,
-        [jax.ShapeDtypeStruct(psi.shape, jnp.bfloat16), jax.ShapeDtypeStruct((1, 128), jnp.float32)],
+        [
+            jax.ShapeDtypeStruct(psi.shape, jnp.bfloat16),
+            jax.ShapeDtypeStruct((ITERS,), jnp.float32),
+            jax.ShapeDtypeStruct((1,), jnp.float32),
+        ],
         0, coef_num, coef_den, gathered, psi, *vecs, right_back, left_back,
     )
-    thetas = row[0, :ITERS]
     return lax.cond(
-        row[0, ITERS] > 0.5,
+        fine[0] > 0.5,
         lambda: (vec, thetas),
         lambda: stepwise(psi, left_env, right_env, energies, coef_num, coef_den, count),
     )

time: 113 us -> 119 us (1.053)
  waiting for transfers between devices: 49 us -> 53 us
  starting transfers between devices: 38.7 us -> 40.8 us
    ppermute x11 -> x12, starting transfers between devices: 27 us -> 31.1 us  [move(): return lax.ppermute(block, AXES, pairs)]
    ppermute x11 -> x12, waiting for transfers between devices: 36 us -> 40.1 us  [move(): return lax.ppermute(block, AXES, pairs)]
    all_to_all x1, starting transfers between devices: 11.7 us -> 9.63 us  [per_device(): lax.all_to_all(result[3].reshape(devices, 1, 128), AXES, 0, 0)]
  transfers between devices with their start and end apart: 12 -> 13, of which waited for: 7 -> 7; matrix products, arithmetic and copies ran while one was open for 0% -> 0% of each run, Pallas kernels for 7% -> 7%
where the time goes in v5:
time: 119 us; the launch traced here: 118 us
  waiting for transfers between devices  53 us (45%)
  starting transfers between devices  40.8 us (34%)
  Pallas kernels  20.2 us (17%)
  local copies, waits for them, and re-layouts  2.73 us (2%)
  between operations  1.52 us (1%)
    ppermute x12, waiting for transfers between devices, move(): return lax.ppermute(block, AXES, pairs)  40.1 us
    ppermute x12, starting transfers between devices, move(): return lax.ppermute(block, AXES, pairs)  31.1 us
    pallas_call x8, Pallas kernels, call(): pl.pallas_call(kernel, in_specs=in_specs, out_specs=[SMEM if len(shape.sh...  20.2 us
    all_to_all x1, waiting for transfers between devices, per_device(): lax.all_to_all(result[3].reshape(devices, 1, 128), AXES, 0, 0)  12.9 us
    all_to_all x1, starting transfers between devices, per_device(): lax.all_to_all(result[3].reshape(devices, 1, 128), AXES, 0, 0)  9.63 us
    unnamed x20, local copies, waits for them, and re-layouts  2.73 us
  transfers between devices with their start and end apart: 13, of which 7 were waited for; matrix products, arithmetic and copies ran while one was open for 0% of the time, Pallas kernels for 7%

profile of v5, /device:TPU:1, one launch (start us, length us, event | category | flops | bytes accessed | tf_op | source)
XLA Modules:
  0.0 118.5 jit_solution(10268169401018170665)
XLA Ops:
  0.6 0.0 copy-start.2
  0.6 0.0 copy-start.8
  0.7 0.0 copy-start.15
  0.7 1.9 %shard_map.81 = (bf16[6,256,256]{2,1,0:T(8,128)(2,1)S(1)}, bf16[1424,256]{1,0:T(8,128)(2,1)S(1)}, bf16[1328,256]{1,0:T(8,128)(2,1)S(1)}, bf16[2,256,256]{2,1,0:T...) custom-call(bf16[4,2,256,256]{3,2,1,0:T(8,128)(2,1)} %refs_3_.13, ...), custom_call_target="tpu_custom_call" | custom-call | bytes 4816928 | tf_op jit(solution)/shard_map/pallas_call | solution.py:404
  2.5 4.2 %collective-permute-start.18 = (bf16[6,256,256]{2,1,0:T(8,128)(2,1)S(1)}, bf16[6,256,256]{2,1,0:T(8,128)(2,1)S(1)}, u32[]{:S(2)}, u32[]{:S(2)}) collective-permute-start(bf16[6,256,256]{2,1,0:T(8,128)(2,1)S(1)} %get-tuple-element.49), channel_id=1, source_target_pairs={{0,33},{1,34},{2,35},{3,36},{4,37},{5,38},{6,39},{7,40},{8,41},{9,... | collective-permute-start | bytes 2359304 | tf_op jit(solution)/shard_map/ppermute | solution.py:398
  6.7 0.3 collective-permute-start.19
  7.0 0.2 collective-permute-start.20
  7.3 0.7 collective-permute-start.22
  7.9 9.0 %collective-permute-start.21 = (bf16[2,256,256]{2,1,0:T(8,128)(2,1)S(1)}, bf16[2,256,256]{2,1,0:T(8,128)(2,1)S(1)}, u32[]{:S(2)}, u32[]{:S(2)}) collective-permute-start(bf16[2,256,256]{2,1,0:T(8,128)(2,1)S(1)} %get-tuple-element.54), channel_id=1, source_target_pairs={{0,63},{1,32},{2,33},{3,34},{4,35},{5,36},{6,37},{7,38},{8,39},{9,... | collective-permute-start | bytes 786440 | tf_op jit(solution)/shard_map/ppermute | solution.py:398
  17.0 0.0 collective-permute-done.22.refs_9_
  17.0 0.0 copy-start.6
  17.0 1.4 %collective-permute-start.23 = (bf16[1,256,256]{2,1,0:T(8,128)(2,1)S(1)}, bf16[1,256,256]{2,1,0:T(8,128)(2,1)S(1)}, u32[]{:S(2)}, u32[]{:S(2)}) collective-permute-start(bf16[1,256,256]{2,1,0:T(8,128)(2,1)S(1)} %get-tuple-element.56), channel_id=1, source_target_pairs={{32,1},{33,2},{34,3},{35,4},{36,5},{37,6},{38,7},{39,8},{40,9},{41... | collective-permute-start | bytes 393224 | tf_op jit(solution)/shard_map/ppermute | solution.py:398
  18.4 0.0 copy-done.2
  18.4 0.0 copy-done.8
  18.4 0.0 copy-done.15
  18.4 2.7 %shard_map.82 = (f32[8,256,256]{2,1,0:T(8,128)S(1)}, f32[8,128]{1,0:T(8,128)S(1)}) custom-call(f32[2,4]{1,0:T(2,128)S(1)} %bitcast.185, bf16[4,4,256,256]{3,2,1,0:T(8,128)(2,1)} %refs_1_.12, bf16[2,4,256,256]{3,2,1,0:T(8,128)(2,1)S(1)} %copy-done.8, bf16[4,2,256,256]{3,2,1,0:T(8,128)(2,1)S(1)} %copy-done.2), custom_call_target="tpu_custom_call" | custom-call | flops 805306368 | bytes 6295584 | tf_op jit(solution)/shard_map/pallas_call | solution.py:404
  21.2 12.6 %collective-permute-done.23.refs_10_ = bf16[1,256,256]{2,1,0:T(8,128)(2,1)S(1)} collective-permute-done((bf16[1,256,256]{2,1,0:T(8,128)(2,1)S(1)}, bf16[1,256,256]{2,1,0:T(8,128)(2,1)S(1)}, u32[]{:S(2)}, u32[]{:S(2)}) %collective-permute-start.23) | collective-permute-done | bytes 131104 | tf_op jit(solution)/shard_map/ppermute | solution.py:398
  33.8 1.4 %collective-permute-done.21.refs_8_ = bf16[2,256,256]{2,1,0:T(8,128)(2,1)S(1)} collective-permute-done((bf16[2,256,256]{2,1,0:T(8,128)(2,1)S(1)}, bf16[2,256,256]{2,1,0:T(8,128)(2,1)S(1)}, u32[]{:S(2)}, u32[]{:S(2)}) %collective-permute-start.21) | collective-permute-done | bytes 262176 | tf_op jit(solution)/shard_map/ppermute | solution.py:398
  35.2 3.7 %collective-permute-done.20.refs_6_ = bf16[1328,256]{1,0:T(8,128)(2,1)S(1)} collective-permute-done((bf16[1328,256]{1,0:T(8,128)(2,1)S(1)}, bf16[1328,256]{1,0:T(8,128)(2,1)S(1)}, u32[]{:S(2)}, u32[]{:S(2)}) %collective-permute-start.20) | collective-permute-done | bytes 679968 | tf_op jit(solution)/shard_map/ppermute | solution.py:398
  38.9 0.0 collective-permute-done.19.refs_5_
  38.9 0.0 collective-permute-done.18.refs_4_
  38.9 0.0 copy-done.6
  38.9 2.2 %shard_map.83 = (bf16[8,256,256]{2,1,0:T(8,128)(2,1)S(1)}, bf16[2,256,256]{2,1,0:T(8,128)(2,1)S(1)}, bf16[2,256,256]{2,1,0:T(8,128)(2,1)S(1)}) custom-call(f32[2,4]{1,0:T(2,128)S(1)} %bitcast.186, bf16[4,4,256,256]{3,2,1,0:T(8,128)(2,1)S(1)} %copy-done.6, bf16[2,4,256,256]{3,2,1,0:T(8,128)(2,1)S(1)} %copy-done.8, bf16[4,2,256,256]{3,2,1,0:T(8,128)(2,1)S(1)} %copy-done.2, ...), custom_call_target="tpu_custom_call" | custom-call | flops 1342177280 | bytes 10584096 | tf_op jit(solution)/shard_map/pallas_call | solution.py:404
  41.1 3.3 %collective-permute-start.24 = (bf16[2,256,256]{2,1,0:T(8,128)(2,1)S(1)}, bf16[2,256,256]{2,1,0:T(8,128)(2,1)S(1)}, u32[]{:S(2)}, u32[]{:S(2)}) collective-permute-start(bf16[2,256,256]{2,1,0:T(8,128)(2,1)S(1)} %get-tuple-element.60), channel_id=1, source_target_pairs={{0,62},{1,63},{2,32},{3,33},{4,34},{5,35},{6,36},{7,37},{8,38},{9,... | collective-permute-start | bytes 786440 | tf_op jit(solution)/shard_map/ppermute | solution.py:398
  44.5 1.3 %collective-permute-start.25 = (bf16[2,256,256]{2,1,0:T(8,128)(2,1)S(1)}, bf16[2,256,256]{2,1,0:T(8,128)(2,1)S(1)}, u32[]{:S(2)}, u32[]{:S(2)}) collective-permute-start(bf16[2,256,256]{2,1,0:T(8,128)(2,1)S(1)} %get-tuple-element.61), channel_id=1, source_target_pairs={{32,2},{33,3},{34,4},{35,5},{36,6},{37,7},{38,8},{39,9},{40,10},{4... | collective-permute-start | bytes 786440 | tf_op jit(solution)/shard_map/ppermute | solution.py:398
  45.8 2.8 %shard_map.84 = (f32[8,256,256]{2,1,0:T(8,128)S(1)}, f32[8,128]{1,0:T(8,128)S(1)}) custom-call(f32[2,4]{1,0:T(2,128)S(1)} %bitcast.187, bf16[4,4,256,256]{3,2,1,0:T(8,128)(2,1)S(1)} %copy-done.6, bf16[2,4,256,256]{3,2,1,0:T(8,128)(2,1)S(1)} %copy-done.8, bf16[4,2,256,256]{3,2,1,0:T(8,128)(2,1)S(1)} %copy-done.2, ...), custom_call_target="tpu_custom_call" | custom-call | flops 1879048192 | bytes 9543712 | tf_op jit(solution)/shard_map/pallas_call | solution.py:404
  48.5 0.0 collective-permute-done.24.refs_9_
  48.5 13.1 %collective-permute-done.25.refs_10_ = bf16[2,256,256]{2,1,0:T(8,128)(2,1)S(1)} collective-permute-done((bf16[2,256,256]{2,1,0:T(8,128)(2,1)S(1)}, bf16[2,256,256]{2,1,0:T(8,128)(2,1)S(1)}, u32[]{:S(2)}, u32[]{:S(2)}) %collective-permute-start.25) | collective-permute-done | bytes 262176 | tf_op jit(solution)/shard_map/ppermute | solution.py:398
  61.6 1.1 shard_map.85
  62.7 7.7 %collective-permute-start.26 = (bf16[2,256,256]{2,1,0:T(8,128)(2,1)S(1)}, bf16[2,256,256]{2,1,0:T(8,128)(2,1)S(1)}, u32[]{:S(2)}, u32[]{:S(2)}) collective-permute-start(bf16[2,256,256]{2,1,0:T(8,128)(2,1)S(1)} %get-tuple-element.65), channel_id=1, source_target_pairs={{0,62},{1,63},{2,32},{3,33},{4,34},{5,35},{6,36},{7,37},{8,38},{9,... | collective-permute-start | bytes 786440 | tf_op jit(solution)/shard_map/ppermute | solution.py:398
  70.4 1.3 %collective-permute-start.27 = (bf16[2,256,256]{2,1,0:T(8,128)(2,1)S(1)}, bf16[2,256,256]{2,1,0:T(8,128)(2,1)S(1)}, u32[]{:S(2)}, u32[]{:S(2)}) collective-permute-start(bf16[2,256,256]{2,1,0:T(8,128)(2,1)S(1)} %get-tuple-element.66), channel_id=1, source_target_pairs={{32,2},{33,3},{34,4},{35,5},{36,6},{37,7},{38,8},{39,9},{40,10},{4... | collective-permute-start | bytes 786440 | tf_op jit(solution)/shard_map/ppermute | solution.py:398
  71.7 2.8 %shard_map.86 = (f32[8,256,256]{2,1,0:T(8,128)S(1)}, f32[8,128]{1,0:T(8,128)S(1)}) custom-call(f32[2,4]{1,0:T(2,128)S(1)} %bitcast.189, bf16[4,4,256,256]{3,2,1,0:T(8,128)(2,1)S(1)} %copy-done.6, bf16[2,4,256,256]{3,2,1,0:T(8,128)(2,1)S(1)} %copy-done.8, bf16[4,2,256,256]{3,2,1,0:T(8,128)(2,1)S(1)} %copy-done.2, ...), custom_call_target="tpu_custom_call" | custom-call | flops 1879048192 | bytes 10592288 | tf_op jit(solution)/shard_map/pallas_call | solution.py:404
  74.5 2.9 %collective-permute-done.26.refs_11_ = bf16[2,256,256]{2,1,0:T(8,128)(2,1)S(1)} collective-permute-done((bf16[2,256,256]{2,1,0:T(8,128)(2,1)S(1)}, bf16[2,256,256]{2,1,0:T(8,128)(2,1)S(1)}, u32[]{:S(2)}, u32[]{:S(2)}) %collective-permute-start.26) | collective-permute-done | bytes 262176 | tf_op jit(solution)/shard_map/ppermute | solution.py:398
  77.4 6.4 %collective-permute-done.27.refs_12_ = bf16[2,256,256]{2,1,0:T(8,128)(2,1)S(1)} collective-permute-done((bf16[2,256,256]{2,1,0:T(8,128)(2,1)S(1)}, bf16[2,256,256]{2,1,0:T(8,128)(2,1)S(1)}, u32[]{:S(2)}, u32[]{:S(2)}) %collective-permute-start.27) | collective-permute-done | bytes 262176 | tf_op jit(solution)/shard_map/ppermute | solution.py:398
  83.8 0.0 copy-start.16
  83.8 0.0 copy-start.17
  83.8 3.1 %shard_map.87 = (bf16[8,256,256]{2,1,0:T(8,128)(2,1)S(1)}, bf16[9,256,256]{2,1,0:T(8,128)(2,1)}, bf16[3,256,256]{2,1,0:T(8,128)(2,1)}, f32[256,128]{1,0:T(8,128)}) custom-call(f32[2,4]{1,0:T(2,128)S(1)} %bitcast.190, bf16[4,4,256,256]{3,2,1,0:T(8,128)(2,1)S(1)} %copy-done.6, bf16[2,4,256,256]{3,2,1,0:T(8,128)(2,1)S(1)} %copy-done.8, ...), custom_call_target="tpu_custom_call" | custom-call | flops 268435456 | bytes 13864992 | tf_op jit(solution)/shard_map/pallas_call | solution.py:404
  86.8 0.0 copy-start
  86.8 1.0 copy-done
  87.8 0.6 collective-permute-start.28
  88.4 1.2 collective-permute-start.29
  89.6 9.6 %all-to-all-start = ((f32[256,1,128]{2,1,0:T(1,128)}), f32[256,1,128]{2,1,0:T(1,128)S(1)}, u32[]{:S(2)}, u32[]{:S(2)}) async-start(f32[256,1,128]{2,1,0:T(1,128)} %bitcast.55), calls=%async_computation | async-start | bytes 262144 | tf_op jit(solution)/shard_map/all_to_all | solution.py:463
  99.2 12.9 %all-to-all-done = f32[256,1,128]{2,1,0:T(1,128)S(1)} async-done(((f32[256,1,128]{2,1,0:T(1,128)}), f32[256,1,128]{2,1,0:T(1,128)S(1)}, u32[]{:S(2)}, u32[]{:S(2)}) %all-to-all-start) | async-done | bytes 131104 | tf_op jit(solution)/shard_map/all_to_all | solution.py:463
  112.1 0.0 collective-permute-done.29.refs_8_
  112.1 0.0 collective-permute-done.28.refs_7_
  112.1 0.0 copy-done.16
  112.1 0.0 copy-done.17
  112.1 0.0 copy-start.1
  112.1 1.2 %copy-done.1 = bf16[8,256,256]{2,1,0:T(8,128)(2,1)S(1)} copy-done((bf16[8,256,256]{2,1,0:T(8,128)(2,1)S(1)}, bf16[8,256,256]{2,1,0:T(8,128)(2,1)}, u32[]{:S(2)}) %copy-start.1) | copy-done | bytes 1048600
  113.4 0.0 copy-start.3
  113.4 3.7 %shard_map.88 = (bf16[4,2,256,256]{3,2,1,0:T(8,128)(2,1)}, f32[3]{0:T(128)S(1)}, f32[1]{0:T(128)}) custom-call(s32[2]{0:T(128)S(1)} %copy-done.16, s32[2]{0:T(128)S(1)} %copy-done.17, f32[256,128]{1,0:T(8,128)S(1)} %bitcast.183, bf16[4,2,256,256]{3,2,1,0:T(8,128)(2,1)} %refs_3_.13, bf16[8,256,256]{2,1,0:T(8,128)(2,1)S(1)} %get-tuple-element.57.refs_8_.refs_9_.refs_4_, ...), custom_call_target="tpu_custom_call" | custom-call | bytes 6946848 | tf_op jit(solution)/shard_map/pallas_call | solution.py:404
  117.7 0.0 copy-done.3
  117.7 0.3 conditional.1
  118.0 0.0 copy-start.18
  118.0 0.5 copy-done.18
Async XLA Ops:
  0.6 17.8 %copy-start.2 = (bf16[4,2,256,256]{3,2,1,0:T(8,128)(2,1)S(1)}, bf16[4,2,256,256]{3,2,1,0:T(8,128)(2,1)}, u32[]{:S(2)}) copy-start(bf16[4,2,256,256]{3,2,1,0:T(8,128)(2,1)} %refs_3_.13) | copy-start | bytes 3145732
  0.6 17.8 %copy-start.8 = (bf16[2,4,256,256]{3,2,1,0:T(8,128)(2,1)S(1)}, bf16[2,4,256,256]{3,2,1,0:T(8,128)(2,1)}, u32[]{:S(2)}) copy-start(bf16[2,4,256,256]{3,2,1,0:T(8,128)(2,1)} %refs_2_.11) | copy-start | bytes 3145732
  0.7 17.8 %copy-start.15 = (f32[4,2]{0,1:T(2,128)S(1)}, f32[4,2]{0,1:T(2,128)}, u32[]{:S(2)}) copy-start(f32[4,2]{0,1:T(2,128)} %param.11) | copy-start | bytes 100
  2.5 36.3 %collective-permute-start.18 = (bf16[6,256,256]{2,1,0:T(8,128)(2,1)S(1)}, bf16[6,256,256]{2,1,0:T(8,128)(2,1)S(1)}, u32[]{:S(2)}, u32[]{:S(2)}) collective-permute-start(bf16[6,256,256]{2,1,0:T(8,128)(2,1)S(1)} %get-tuple-element.49), channel_id=1, source_target_pairs={{0,33},{1,34},{2,35},{3,36},{4,37},{5,38},{6,39},{7,40},{8,41},{9,... | collective-permute-start | bytes 2359304 | tf_op jit(solution)/shard_map/ppermute | solution.py:398
  6.7 32.1 %collective-permute-start.19 = (bf16[1424,256]{1,0:T(8,128)(2,1)S(1)}, bf16[1424,256]{1,0:T(8,128)(2,1)S(1)}, u32[]{:S(2)}, u32[]{:S(2)}) collective-permute-start(bf16[1424,256]{1,0:T(8,128)(2,1)S(1)} %get-tuple-element.50), channel_id=1, source_target_pairs={{0,1},{1,2},{2,3},{3,4},{4,5},{5,6},{6,7},{7,8},{8,9},{9,10},{10,1... | collective-permute-start | bytes 2187272 | tf_op jit(solution)/shard_map/ppermute | solution.py:398
  7.0 31.8 %collective-permute-start.20 = (bf16[1328,256]{1,0:T(8,128)(2,1)S(1)}, bf16[1328,256]{1,0:T(8,128)(2,1)S(1)}, u32[]{:S(2)}, u32[]{:S(2)}) collective-permute-start(bf16[1328,256]{1,0:T(8,128)(2,1)S(1)} %get-tuple-element.51), channel_id=1, source_target_pairs={{0,31},{1,0},{2,1},{3,2},{4,3},{5,4},{6,5},{7,6},{8,7},{9,8},{10,9... | collective-permute-start | bytes 2039816 | tf_op jit(solution)/shard_map/ppermute | solution.py:398
  7.3 9.7 %collective-permute-start.22 = (bf16[1,256,256]{2,1,0:T(8,128)(2,1)S(1)}, bf16[1,256,256]{2,1,0:T(8,128)(2,1)S(1)}, u32[]{:S(2)}, u32[]{:S(2)}) collective-permute-start(bf16[1,256,256]{2,1,0:T(8,128)(2,1)S(1)} %get-tuple-element.55), channel_id=1, source_target_pairs={{32,2},{33,3},{34,4},{35,5},{36,6},{37,7},{38,8},{39,9},{40,10},{4... | collective-permute-start | bytes 393224 | tf_op jit(solution)/shard_map/ppermute | solution.py:398
  7.9 27.3 %collective-permute-start.21 = (bf16[2,256,256]{2,1,0:T(8,128)(2,1)S(1)}, bf16[2,256,256]{2,1,0:T(8,128)(2,1)S(1)}, u32[]{:S(2)}, u32[]{:S(2)}) collective-permute-start(bf16[2,256,256]{2,1,0:T(8,128)(2,1)S(1)} %get-tuple-element.54), channel_id=1, source_target_pairs={{0,63},{1,32},{2,33},{3,34},{4,35},{5,36},{6,37},{7,38},{8,39},{9,... | collective-permute-start | bytes 786440 | tf_op jit(solution)/shard_map/ppermute | solution.py:398
  17.0 21.9 %copy-start.6 = (bf16[4,4,256,256]{3,2,1,0:T(8,128)(2,1)S(1)}, bf16[4,4,256,256]{3,2,1,0:T(8,128)(2,1)}, u32[]{:S(2)}) copy-start(bf16[4,4,256,256]{3,2,1,0:T(8,128)(2,1)} %refs_1_.12) | copy-start | bytes 6291460
  17.0 16.8 %collective-permute-start.23 = (bf16[1,256,256]{2,1,0:T(8,128)(2,1)S(1)}, bf16[1,256,256]{2,1,0:T(8,128)(2,1)S(1)}, u32[]{:S(2)}, u32[]{:S(2)}) collective-permute-start(bf16[1,256,256]{2,1,0:T(8,128)(2,1)S(1)} %get-tuple-element.56), channel_id=1, source_target_pairs={{32,1},{33,2},{34,3},{35,4},{36,5},{37,6},{38,7},{39,8},{40,9},{41... | collective-permute-start | bytes 393224 | tf_op jit(solution)/shard_map/ppermute | solution.py:398
  41.1 7.4 %collective-permute-start.24 = (bf16[2,256,256]{2,1,0:T(8,128)(2,1)S(1)}, bf16[2,256,256]{2,1,0:T(8,128)(2,1)S(1)}, u32[]{:S(2)}, u32[]{:S(2)}) collective-permute-start(bf16[2,256,256]{2,1,0:T(8,128)(2,1)S(1)} %get-tuple-element.60), channel_id=1, source_target_pairs={{0,62},{1,63},{2,32},{3,33},{4,34},{5,35},{6,36},{7,37},{8,38},{9,... | collective-permute-start | bytes 786440 | tf_op jit(solution)/shard_map/ppermute | solution.py:398
  44.5 17.2 %collective-permute-start.25 = (bf16[2,256,256]{2,1,0:T(8,128)(2,1)S(1)}, bf16[2,256,256]{2,1,0:T(8,128)(2,1)S(1)}, u32[]{:S(2)}, u32[]{:S(2)}) collective-permute-start(bf16[2,256,256]{2,1,0:T(8,128)(2,1)S(1)} %get-tuple-element.61), channel_id=1, source_target_pairs={{32,2},{33,3},{34,4},{35,5},{36,6},{37,7},{38,8},{39,9},{40,10},{4... | collective-permute-start | bytes 786440 | tf_op jit(solution)/shard_map/ppermute | solution.py:398
  62.7 14.7 %collective-permute-start.26 = (bf16[2,256,256]{2,1,0:T(8,128)(2,1)S(1)}, bf16[2,256,256]{2,1,0:T(8,128)(2,1)S(1)}, u32[]{:S(2)}, u32[]{:S(2)}) collective-permute-start(bf16[2,256,256]{2,1,0:T(8,128)(2,1)S(1)} %get-tuple-element.65), channel_id=1, source_target_pairs={{0,62},{1,63},{2,32},{3,33},{4,34},{5,35},{6,36},{7,37},{8,38},{9,... | collective-permute-start | bytes 786440 | tf_op jit(solution)/shard_map/ppermute | solution.py:398
  70.4 13.4 %collective-permute-start.27 = (bf16[2,256,256]{2,1,0:T(8,128)(2,1)S(1)}, bf16[2,256,256]{2,1,0:T(8,128)(2,1)S(1)}, u32[]{:S(2)}, u32[]{:S(2)}) collective-permute-start(bf16[2,256,256]{2,1,0:T(8,128)(2,1)S(1)} %get-tuple-element.66), channel_id=1, source_target_pairs={{32,2},{33,3},{34,4},{35,5},{36,6},{37,7},{38,8},{39,9},{40,10},{4... | collective-permute-start | bytes 786440 | tf_op jit(solution)/shard_map/ppermute | solution.py:398
  83.8 28.3 %copy-start.16 = (s32[2]{0:T(128)S(1)}, s32[2]{0:T(128)}, u32[]{:S(2)}) copy-start(s32[2]{0:T(128)} %refs_0_.1) | copy-start | bytes 28
  83.8 28.4 %copy-start.17 = (s32[2]{0:T(128)S(1)}, s32[2]{0:T(128)}, u32[]{:S(2)}) copy-start(s32[2]{0:T(128)} %refs_1_.13) | copy-start | bytes 28
  86.8 1.0 copy-start
  87.8 24.3 %collective-permute-start.28 = (bf16[9,256,256]{2,1,0:T(8,128)(2,1)}, bf16[9,256,256]{2,1,0:T(8,128)(2,1)S(1)}, u32[]{:S(2)}, u32[]{:S(2)}) collective-permute-start(bf16[9,256,256]{2,1,0:T(8,128)(2,1)} %get-tuple-element.69), channel_id=1, source_target_pairs={{0,31},{1,0},{2,1},{3,2},{4,3},{5,4},{6,5},{7,6},{8,7},{9,8},{10,9... | collective-permute-start | bytes 3538952 | tf_op jit(solution)/shard_map/ppermute | solution.py:398
  88.4 23.7 %collective-permute-start.29 = (bf16[3,256,256]{2,1,0:T(8,128)(2,1)}, bf16[3,256,256]{2,1,0:T(8,128)(2,1)}, u32[]{:S(2)}, u32[]{:S(2)}) collective-permute-start(bf16[3,256,256]{2,1,0:T(8,128)(2,1)} %get-tuple-element.70), channel_id=1, source_target_pairs={{0,1},{1,2},{2,3},{3,4},{4,5},{5,6},{6,7},{7,8},{8,9},{9,10},{10,1... | collective-permute-start | bytes 1179656 | tf_op jit(solution)/shard_map/ppermute | solution.py:398
  89.6 22.6 %all-to-all-start = ((f32[256,1,128]{2,1,0:T(1,128)}), f32[256,1,128]{2,1,0:T(1,128)S(1)}, u32[]{:S(2)}, u32[]{:S(2)}) async-start(f32[256,1,128]{2,1,0:T(1,128)} %bitcast.55), calls=%async_computation | async-start | bytes 262144 | tf_op jit(solution)/shard_map/all_to_all | solution.py:463
  112.1 1.2 %copy-start.1 = (bf16[8,256,256]{2,1,0:T(8,128)(2,1)S(1)}, bf16[8,256,256]{2,1,0:T(8,128)(2,1)}, u32[]{:S(2)}) copy-start(bf16[8,256,256]{2,1,0:T(8,128)(2,1)} %copy-done) | copy-start | bytes 3145732
  113.4 4.3 %copy-start.3 = (bf16[4,2,256,256]{3,2,1,0:T(8,128)(2,1)S(1)}, bf16[4,2,256,256]{3,2,1,0:T(8,128)(2,1)}, u32[]{:S(2)}) copy-start(bf16[4,2,256,256]{3,2,1,0:T(8,128)(2,1)} %refs_3_.13) | copy-start | bytes 3145732
  118.0 0.5 copy-start.18

commit v6 on v3

--- a/solution.py
+++ b/solution.py
@@ -337,7 +337,7 @@
     return vec, thetas, fine
 
 
-def combine_kernel(count, num_ref, den_ref, sums_ref, psi_ref, one_ref, two_ref, three_ref, back_ref, out_ref, row_ref):
+def combine_kernel(count, num_ref, den_ref, sums_ref, psi_ref, one_ref, two_ref, three_ref, back_ref, out_ref, theta_ref, fine_ref):
     sums = jnp.sum(sums_ref[...], axis=0, keepdims=True) * count
     lanes = lax.broadcasted_iota(jnp.int32, sums.shape, 1)
     entries = [
@@ -355,10 +355,9 @@
         den = jnp.full(entries[0].shape, den_ref[step], jnp.int32).astype(jnp.float32)
         coefs.append(num / den)
     weights, thetas, fine = recursion(gram, coefs)
-    row = jnp.zeros((1, 128), jnp.float32)
-    for place, value in enumerate(thetas + [fine]):
-        row = place_in(row, place, value)
-    row_ref[...] = row
+    for place, value in enumerate(thetas):
+        theta_ref[place] = jnp.max(value)
+    fine_ref[0] = jnp.max(fine)
     for i in range(ROWS):
         for j in range(COLS):
             k = 2 * i + j + (i == 3)
@@ -390,7 +389,7 @@
     return pl.pallas_call(
         kernel,
         in_specs=in_specs,
-        out_specs=[VMEM] * len(out_shapes),
+        out_specs=[SMEM if len(shape.shape) == 1 else VMEM for shape in out_shapes],
         out_shape=out_shapes,
         compiler_params=PARAMS,
         cost_estimate=pl.CostEstimate(flops=flops, bytes_accessed=nbytes, transcendentals=0),
@@ -451,15 +450,18 @@
     sums = [result[-1]]
     back = move(result[1], 0, -1, True)
     gathered = lax.all_to_all(sums[0].reshape(devices, 1, 128), AXES, 0, 0).reshape(devices, 128)
-    vec, row = call(
+    vec, thetas, fine = call(
         lambda *refs: combine_kernel(count, *refs),
         [SMEM, SMEM] + [VMEM] * 6,
-        [jax.ShapeDtypeStruct(psi.shape, jnp.bfloat16), jax.ShapeDtypeStruct((1, 128), jnp.float32)],
+        [
+            jax.ShapeDtypeStruct(psi.shape, jnp.bfloat16),
+            jax.ShapeDtypeStruct((ITERS,), jnp.float32),
+            jax.ShapeDtypeStruct((1,), jnp.float32),
+        ],
         0, coef_num, coef_den, gathered, psi, *vecs, back,
     )
-    thetas = row[0, :ITERS]
     return lax.cond(
-        row[0, ITERS] > 0.5,
+        fine[0] > 0.5,
         lambda: (vec, thetas),
         lambda: stepwise(psi, left_env, right_env, energies, coef_num, coef_den, count),
     )

time: 110 us -> 110 us (level)
  no operation moved by 1% of the time
where the time goes in v6:
time: 110 us; the launch traced here: 109 us
  starting transfers between devices  59 us (54%)
  waiting for transfers between devices  28.5 us (26%)
  Pallas kernels  19.5 us (18%)
  between operations  1.54 us (1%)
    ppermute x14, starting transfers between devices, move(): return lax.ppermute(block, AXES, pairs)  39.3 us
    all_to_all x1, starting transfers between devices, per_device(): lax.all_to_all(sums[0].reshape(devices, 1, 128), AXES, 0, 0)  19.7 us
    pallas_call x8, Pallas kernels, call(): pl.pallas_call(kernel, in_specs=in_specs, out_specs=[SMEM if len(shape.sh...  19.5 us
    ppermute x14, waiting for transfers between devices, move(): return lax.ppermute(block, AXES, pairs)  15.5 us
    all_to_all x1, waiting for transfers between devices, per_device(): lax.all_to_all(sums[0].reshape(devices, 1, 128), AXES, 0, 0)  12.9 us
  transfers between devices with their start and end apart: 15, of which 8 were waited for; matrix products, arithmetic and copies ran while one was open for 0% of the time, Pallas kernels for 8%

profile of v6, /device:TPU:1, one launch (start us, length us, event | category | flops | bytes accessed | tf_op | source)
XLA Modules:
  0.0 109.0 jit_solution(5176407438390319908)
XLA Ops:
  0.6 0.0 copy-start
  0.6 0.0 copy-start.6
  0.7 0.0 copy-start.13
  0.7 1.8 %shard_map.81 = (bf16[1840,256]{1,0:T(8,128)(2,1)S(1)}, bf16[2,256,256]{2,1,0:T(8,128)(2,1)S(1)}, bf16[1,256,256]{2,1,0:T(8,128)(2,1)S(1)}, bf16[1,256,256]{2,1,0:T(8,128)(2,1)S(1)}, bf16[2,256,256]{2,1,0:T(8,128)(2,1)S(1)}) custom-call(bf16[4,2,256,256]{3,2,1,0:T(8,128)(2,1)} %refs_3_.13, bf16[2,4,256,256]{3,2,1,0:T(8,128)(2,1)} %refs_2_.11, f32[2,4]{1,0:T(2,128)} %bitcast.184), custom_call_target="tpu_custom_call" | custom-call | bytes 3825696 | tf_op jit(solution)/shard_map/pallas_call | solution.py:389
  2.5 2.8 %collective-permute-start.18 = (bf16[1840,256]{1,0:T(8,128)(2,1)S(1)}, bf16[1840,256]{1,0:T(8,128)(2,1)S(1)}, u32[]{:S(2)}, u32[]{:S(2)}) collective-permute-start(bf16[1840,256]{1,0:T(8,128)(2,1)S(1)} %get-tuple-element.51), channel_id=1, source_target_pairs={{0,1},{1,2},{2,3},{3,4},{4,5},{5,6},{6,7},{7,8},{8,9},{9,10},{10,1... | collective-permute-start | bytes 2826248 | tf_op jit(solution)/shard_map/ppermute | solution.py:383
  5.3 1.3 %collective-permute-start.20 = (bf16[2,256,256]{2,1,0:T(8,128)(2,1)S(1)}, bf16[2,256,256]{2,1,0:T(8,128)(2,1)S(1)}, u32[]{:S(2)}, u32[]{:S(2)}) collective-permute-start(bf16[2,256,256]{2,1,0:T(8,128)(2,1)S(1)} %get-tuple-element.55), channel_id=1, source_target_pairs={{32,1},{33,2},{34,3},{35,4},{36,5},{37,6},{38,7},{39,8},{40,9},{41... | collective-permute-start | bytes 786440 | tf_op jit(solution)/shard_map/ppermute | solution.py:383
  6.5 2.5 %collective-permute-start.21 = (bf16[2,256,256]{2,1,0:T(8,128)(2,1)S(1)}, bf16[2,256,256]{2,1,0:T(8,128)(2,1)S(1)}, u32[]{:S(2)}, u32[]{:S(2)}) collective-permute-start(bf16[2,256,256]{2,1,0:T(8,128)(2,1)S(1)} %get-tuple-element.56), channel_id=1, source_target_pairs={{1,0},{2,1},{3,2},{4,3},{5,4},{6,5},{7,6},{8,7},{9,8},{10,9},{11,1... | collective-permute-start | bytes 786440 | tf_op jit(solution)/shard_map/ppermute | solution.py:383
  9.0 5.3 %collective-permute-start.19 = (bf16[1,256,256]{2,1,0:T(8,128)(2,1)S(1)}, bf16[1,256,256]{2,1,0:T(8,128)(2,1)S(1)}, u32[]{:S(2)}, u32[]{:S(2)}) collective-permute-start(bf16[1,256,256]{2,1,0:T(8,128)(2,1)S(1)} %get-tuple-element.54), channel_id=1, source_target_pairs={{0,32},{1,33},{2,34},{3,35},{4,36},{5,37},{6,38},{7,39},{8,40},{9,... | collective-permute-start | bytes 393224 | tf_op jit(solution)/shard_map/ppermute | solution.py:383
  14.4 0.0 copy-start.4
  14.4 5.1 %collective-permute-start.22 = (bf16[1,256,256]{2,1,0:T(8,128)(2,1)S(1)}, bf16[1,256,256]{2,1,0:T(8,128)(2,1)S(1)}, u32[]{:S(2)}, u32[]{:S(2)}) collective-permute-start(bf16[1,256,256]{2,1,0:T(8,128)(2,1)S(1)} %get-tuple-element.57), channel_id=1, source_target_pairs={{1,32},{2,33},{3,34},{4,35},{5,36},{6,37},{7,38},{8,39},{9,40},{10... | collective-permute-start | bytes 393224 | tf_op jit(solution)/shard_map/ppermute | solution.py:383
  19.5 0.0 copy-done
  19.5 0.0 copy-done.6
  19.5 0.0 copy-done.13
  19.5 3.3 %shard_map.82 = (f32[8,256,256]{2,1,0:T(8,128)S(1)}, f32[8,128]{1,0:T(8,128)S(1)}) custom-call(f32[2,4]{1,0:T(2,128)S(1)} %bitcast.185, bf16[4,4,256,256]{3,2,1,0:T(8,128)(2,1)} %refs_1_.14, bf16[2,4,256,256]{3,2,1,0:T(8,128)(2,1)S(1)} %copy-done.6, bf16[4,2,256,256]{3,2,1,0:T(8,128)(2,1)S(1)} %copy-done), custom_call_target="tpu_custom_call" | custom-call | flops 1342177280 | bytes 6295584 | tf_op jit(solution)/shard_map/pallas_call | solution.py:389
  22.8 1.5 %collective-permute-done.19.refs_6_ = bf16[1,256,256]{2,1,0:T(8,128)(2,1)S(1)} collective-permute-done((bf16[1,256,256]{2,1,0:T(8,128)(2,1)S(1)}, bf16[1,256,256]{2,1,0:T(8,128)(2,1)S(1)}, u32[]{:S(2)}, u32[]{:S(2)}) %collective-permute-start.19) | collective-permute-done | bytes 131104 | tf_op jit(solution)/shard_map/ppermute | solution.py:383
  24.3 3.1 %collective-permute-done.22.refs_9_ = bf16[1,256,256]{2,1,0:T(8,128)(2,1)S(1)} collective-permute-done((bf16[1,256,256]{2,1,0:T(8,128)(2,1)S(1)}, bf16[1,256,256]{2,1,0:T(8,128)(2,1)S(1)}, u32[]{:S(2)}, u32[]{:S(2)}) %collective-permute-start.22) | collective-permute-done | bytes 131104 | tf_op jit(solution)/shard_map/ppermute | solution.py:383
  27.3 0.0 collective-permute-done.20.refs_7_
  27.3 2.0 %collective-permute-done.21.refs_8_ = bf16[2,256,256]{2,1,0:T(8,128)(2,1)S(1)} collective-permute-done((bf16[2,256,256]{2,1,0:T(8,128)(2,1)S(1)}, bf16[2,256,256]{2,1,0:T(8,128)(2,1)S(1)}, u32[]{:S(2)}, u32[]{:S(2)}) %collective-permute-start.21) | collective-permute-done | bytes 262176 | tf_op jit(solution)/shard_map/ppermute | solution.py:383
  29.4 0.0 collective-permute-done.18.refs_4_
  29.4 0.0 copy-done.4
  29.4 1.6 %shard_map.83 = (bf16[8,256,256]{2,1,0:T(8,128)(2,1)S(1)}, bf16[2,256,256]{2,1,0:T(8,128)(2,1)S(1)}, bf16[2,256,256]{2,1,0:T(8,128)(2,1)S(1)}, bf16[2,256,256]{2,1,0:T(8,128)(2,1)S(1)}, bf16[2,256,256]{2,1,0:T(8,128)(2,1)S(1)}) custom-call(f32[2,4]{1,0:T(2,128)S(1)} %bitcast.186, bf16[4,4,256,256]{3,2,1,0:T(8,128)(2,1)S(1)} %copy-done.4, ...), custom_call_target="tpu_custom_call" | custom-call | flops 805306368 | bytes 10117152 | tf_op jit(solution)/shard_map/pallas_call | solution.py:389
  31.0 5.1 %collective-permute-start.23 = (bf16[2,256,256]{2,1,0:T(8,128)(2,1)S(1)}, bf16[2,256,256]{2,1,0:T(8,128)(2,1)S(1)}, u32[]{:S(2)}, u32[]{:S(2)}) collective-permute-start(bf16[2,256,256]{2,1,0:T(8,128)(2,1)S(1)} %get-tuple-element.61), channel_id=1, source_target_pairs={{0,63},{1,32},{2,33},{3,34},{4,35},{5,36},{6,37},{7,38},{8,39},{9,... | collective-permute-start | bytes 786440 | tf_op jit(solution)/shard_map/ppermute | solution.py:383
  36.1 1.3 %collective-permute-start.24 = (bf16[2,256,256]{2,1,0:T(8,128)(2,1)S(1)}, bf16[2,256,256]{2,1,0:T(8,128)(2,1)S(1)}, u32[]{:S(2)}, u32[]{:S(2)}) collective-permute-start(bf16[2,256,256]{2,1,0:T(8,128)(2,1)S(1)} %get-tuple-element.62), channel_id=1, source_target_pairs={{32,1},{33,2},{34,3},{35,4},{36,5},{37,6},{38,7},{39,8},{40,9},{41... | collective-permute-start | bytes 786440 | tf_op jit(solution)/shard_map/ppermute | solution.py:383
  37.4 1.9 %collective-permute-start.25 = (bf16[2,256,256]{2,1,0:T(8,128)(2,1)S(1)}, bf16[2,256,256]{2,1,0:T(8,128)(2,1)S(1)}, u32[]{:S(2)}, u32[]{:S(2)}) collective-permute-start(bf16[2,256,256]{2,1,0:T(8,128)(2,1)S(1)} %get-tuple-element.63), channel_id=1, source_target_pairs={{0,1},{1,2},{2,3},{3,4},{4,5},{5,6},{6,7},{7,8},{8,9},{9,10},{10,1... | collective-permute-start | bytes 786440 | tf_op jit(solution)/shard_map/ppermute | solution.py:383
  39.3 2.4 %collective-permute-start.26 = (bf16[2,256,256]{2,1,0:T(8,128)(2,1)S(1)}, bf16[2,256,256]{2,1,0:T(8,128)(2,1)S(1)}, u32[]{:S(2)}, u32[]{:S(2)}) collective-permute-start(bf16[2,256,256]{2,1,0:T(8,128)(2,1)S(1)} %get-tuple-element.64), channel_id=1, source_target_pairs={{1,0},{2,1},{3,2},{4,3},{5,4},{6,5},{7,6},{8,7},{9,8},{10,9},{11,1... | collective-permute-start | bytes 786440 | tf_op jit(solution)/shard_map/ppermute | solution.py:383
  41.7 2.5 %shard_map.84 = (f32[8,256,256]{2,1,0:T(8,128)S(1)}, f32[8,128]{1,0:T(8,128)S(1)}) custom-call(f32[2,4]{1,0:T(2,128)S(1)} %bitcast.187, bf16[4,4,256,256]{3,2,1,0:T(8,128)(2,1)S(1)} %copy-done.4, bf16[2,4,256,256]{3,2,1,0:T(8,128)(2,1)S(1)} %copy-done.6, bf16[4,2,256,256]{3,2,1,0:T(8,128)(2,1)S(1)} %copy-done, ...), custom_call_target="tpu_custom_call" | custom-call | flops 1610612736 | bytes 8290336 | tf_op jit(solution)/shard_map/pallas_call | solution.py:389
  44.2 0.0 collective-permute-done.23.refs_7_
  44.2 3.8 %collective-permute-done.24.refs_8_ = bf16[2,256,256]{2,1,0:T(8,128)(2,1)S(1)} collective-permute-done((bf16[2,256,256]{2,1,0:T(8,128)(2,1)S(1)}, bf16[2,256,256]{2,1,0:T(8,128)(2,1)S(1)}, u32[]{:S(2)}, u32[]{:S(2)}) %collective-permute-start.24) | collective-permute-done | bytes 262176 | tf_op jit(solution)/shard_map/ppermute | solution.py:383
  48.1 0.0 collective-permute-done.25.refs_9_
  48.1 0.6 collective-permute-done.26.refs_10_
  48.7 1.4 %shard_map.85 = (bf16[8,256,256]{2,1,0:T(8,128)(2,1)S(1)}, bf16[2,256,256]{2,1,0:T(8,128)(2,1)S(1)}, bf16[2,256,256]{2,1,0:T(8,128)(2,1)S(1)}, bf16[2,256,256]{2,1,0:T(8,128)(2,1)S(1)}, bf16[2,256,256]{2,1,0:T(8,128)(2,1)S(1)}) custom-call(f32[2,4]{1,0:T(2,128)S(1)} %bitcast.188, bf16[4,4,256,256]{3,2,1,0:T(8,128)(2,1)S(1)} %copy-done.4, ...), custom_call_target="tpu_custom_call" | custom-call | flops 536870912 | bytes 11427872 | tf_op jit(solution)/shard_map/pallas_call | solution.py:389
  50.1 2.8 %collective-permute-start.27 = (bf16[2,256,256]{2,1,0:T(8,128)(2,1)S(1)}, bf16[2,256,256]{2,1,0:T(8,128)(2,1)S(1)}, u32[]{:S(2)}, u32[]{:S(2)}) collective-permute-start(bf16[2,256,256]{2,1,0:T(8,128)(2,1)S(1)} %get-tuple-element.68), channel_id=1, source_target_pairs={{0,63},{1,32},{2,33},{3,34},{4,35},{5,36},{6,37},{7,38},{8,39},{9,... | collective-permute-start | bytes 786440 | tf_op jit(solution)/shard_map/ppermute | solution.py:383
  52.9 1.3 %collective-permute-start.28 = (bf16[2,256,256]{2,1,0:T(8,128)(2,1)S(1)}, bf16[2,256,256]{2,1,0:T(8,128)(2,1)S(1)}, u32[]{:S(2)}, u32[]{:S(2)}) collective-permute-start(bf16[2,256,256]{2,1,0:T(8,128)(2,1)S(1)} %get-tuple-element.69), channel_id=1, source_target_pairs={{32,1},{33,2},{34,3},{35,4},{36,5},{37,6},{38,7},{39,8},{40,9},{41... | collective-permute-start | bytes 786440 | tf_op jit(solution)/shard_map/ppermute | solution.py:383
  54.2 5.7 %collective-permute-start.29 = (bf16[2,256,256]{2,1,0:T(8,128)(2,1)S(1)}, bf16[2,256,256]{2,1,0:T(8,128)(2,1)S(1)}, u32[]{:S(2)}, u32[]{:S(2)}) collective-permute-start(bf16[2,256,256]{2,1,0:T(8,128)(2,1)S(1)} %get-tuple-element.70), channel_id=1, source_target_pairs={{0,1},{1,2},{2,3},{3,4},{4,5},{5,6},{6,7},{7,8},{8,9},{9,10},{10,1... | collective-permute-start | bytes 786440 | tf_op jit(solution)/shard_map/ppermute | solution.py:383
  59.9 1.9 %collective-permute-start.30 = (bf16[2,256,256]{2,1,0:T(8,128)(2,1)S(1)}, bf16[2,256,256]{2,1,0:T(8,128)(2,1)S(1)}, u32[]{:S(2)}, u32[]{:S(2)}) collective-permute-start(bf16[2,256,256]{2,1,0:T(8,128)(2,1)S(1)} %get-tuple-element.71), channel_id=1, source_target_pairs={{1,0},{2,1},{3,2},{4,3},{5,4},{6,5},{7,6},{8,7},{9,8},{10,9},{11,1... | collective-permute-start | bytes 786440 | tf_op jit(solution)/shard_map/ppermute | solution.py:383
  61.8 2.5 %shard_map.86 = (f32[8,256,256]{2,1,0:T(8,128)S(1)}, f32[8,128]{1,0:T(8,128)S(1)}) custom-call(f32[2,4]{1,0:T(2,128)S(1)} %bitcast.189, bf16[4,4,256,256]{3,2,1,0:T(8,128)(2,1)S(1)} %copy-done.4, bf16[2,4,256,256]{3,2,1,0:T(8,128)(2,1)S(1)} %copy-done.6, bf16[4,2,256,256]{3,2,1,0:T(8,128)(2,1)S(1)} %copy-done, ...), custom_call_target="tpu_custom_call" | custom-call | flops 1610612736 | bytes 9338912 | tf_op jit(solution)/shard_map/pallas_call | solution.py:389
  64.3 0.0 collective-permute-done.27.refs_9_
  64.4 1.3 %collective-permute-done.28.refs_10_ = bf16[2,256,256]{2,1,0:T(8,128)(2,1)S(1)} collective-permute-done((bf16[2,256,256]{2,1,0:T(8,128)(2,1)S(1)}, bf16[2,256,256]{2,1,0:T(8,128)(2,1)S(1)}, u32[]{:S(2)}, u32[]{:S(2)}) %collective-permute-start.28) | collective-permute-done | bytes 262176 | tf_op jit(solution)/shard_map/ppermute | solution.py:383
  65.7 3.1 %collective-permute-done.29.refs_11_ = bf16[2,256,256]{2,1,0:T(8,128)(2,1)S(1)} collective-permute-done((bf16[2,256,256]{2,1,0:T(8,128)(2,1)S(1)}, bf16[2,256,256]{2,1,0:T(8,128)(2,1)S(1)}, u32[]{:S(2)}, u32[]{:S(2)}) %collective-permute-start.29) | collective-permute-done | bytes 262176 | tf_op jit(solution)/shard_map/ppermute | solution.py:383
  68.8 0.0 collective-permute-done.30.refs_12_
  68.8 0.0 copy-start.14
  68.8 0.0 copy-start.15
  68.8 2.7 %shard_map.87 = (bf16[8,256,256]{2,1,0:T(8,128)(2,1)S(1)}, bf16[3,256,256]{2,1,0:T(8,128)(2,1)}, f32[256,128]{1,0:T(8,128)}) custom-call(f32[2,4]{1,0:T(2,128)S(1)} %bitcast.190, bf16[4,4,256,256]{3,2,1,0:T(8,128)(2,1)S(1)} %copy-done.4, bf16[2,4,256,256]{3,2,1,0:T(8,128)(2,1)S(1)} %copy-done.6, bf16[4,2,256,256]{3,2,1,0:T(8,128)(2,1)S(1)} %copy-done, ...), custom_call_target="tpu_custom_call" | custom-call | flops 536870912 | bytes 11956256 | tf_op jit(solution)/shard_map/pallas_call | solution.py:389
  71.5 0.0 collective-permute-start.31
  71.5 19.7 %all-to-all-start = ((f32[256,1,128]{2,1,0:T(1,128)}), f32[256,1,128]{2,1,0:T(1,128)S(1)}, u32[]{:S(2)}, u32[]{:S(2)}) async-start(f32[256,1,128]{2,1,0:T(1,128)} %bitcast.55), calls=%async_computation | async-start | bytes 262144 | tf_op jit(solution)/shard_map/all_to_all | solution.py:452
  91.2 12.9 %all-to-all-done = f32[256,1,128]{2,1,0:T(1,128)S(1)} async-done(((f32[256,1,128]{2,1,0:T(1,128)}), f32[256,1,128]{2,1,0:T(1,128)S(1)}, u32[]{:S(2)}, u32[]{:S(2)}) %all-to-all-start) | async-done | bytes 131104 | tf_op jit(solution)/shard_map/all_to_all | solution.py:452
  104.1 0.0 collective-permute-done.31.refs_7_
  104.1 0.0 copy-done.14
  104.1 0.0 copy-done.15
  104.1 0.0 copy-start.1
  104.2 3.7 %shard_map.88 = (bf16[4,2,256,256]{3,2,1,0:T(8,128)(2,1)}, f32[3]{0:T(128)S(1)}, f32[1]{0:T(128)}) custom-call(s32[2]{0:T(128)S(1)} %copy-done.14, s32[2]{0:T(128)S(1)} %copy-done.15, f32[256,128]{1,0:T(8,128)S(1)} %bitcast.183, bf16[4,2,256,256]{3,2,1,0:T(8,128)(2,1)} %refs_3_.13, bf16[8,256,256]{2,1,0:T(8,128)(2,1)S(1)} %get-tuple-element.58.refs_6_.refs_7_.refs_4_, ...), custom_call_target="tpu_custom_call" | custom-call | bytes 5767200 | tf_op jit(solution)/shard_map/pallas_call | solution.py:389
  108.5 0.0 copy-done.1
  108.5 0.0 copy-start.16
  108.5 0.5 copy-done.16
  (1 shorter events, 0.0 us)
Async XLA Ops:
  0.6 18.9 %copy-start = (bf16[4,2,256,256]{3,2,1,0:T(8,128)(2,1)S(1)}, bf16[4,2,256,256]{3,2,1,0:T(8,128)(2,1)}, u32[]{:S(2)}) copy-start(bf16[4,2,256,256]{3,2,1,0:T(8,128)(2,1)} %refs_3_.13) | copy-start | bytes 3145732
  0.6 18.9 %copy-start.6 = (bf16[2,4,256,256]{3,2,1,0:T(8,128)(2,1)S(1)}, bf16[2,4,256,256]{3,2,1,0:T(8,128)(2,1)}, u32[]{:S(2)}) copy-start(bf16[2,4,256,256]{3,2,1,0:T(8,128)(2,1)} %refs_2_.11) | copy-start | bytes 3145732
  0.7 18.9 %copy-start.13 = (f32[4,2]{0,1:T(2,128)S(1)}, f32[4,2]{0,1:T(2,128)}, u32[]{:S(2)}) copy-start(f32[4,2]{0,1:T(2,128)} %param.11) | copy-start | bytes 100
  2.5 26.9 %collective-permute-start.18 = (bf16[1840,256]{1,0:T(8,128)(2,1)S(1)}, bf16[1840,256]{1,0:T(8,128)(2,1)S(1)}, u32[]{:S(2)}, u32[]{:S(2)}) collective-permute-start(bf16[1840,256]{1,0:T(8,128)(2,1)S(1)} %get-tuple-element.51), channel_id=1, source_target_pairs={{0,1},{1,2},{2,3},{3,4},{4,5},{5,6},{6,7},{7,8},{8,9},{9,10},{10,1... | collective-permute-start | bytes 2826248 | tf_op jit(solution)/shard_map/ppermute | solution.py:383
  5.3 22.1 %collective-permute-start.20 = (bf16[2,256,256]{2,1,0:T(8,128)(2,1)S(1)}, bf16[2,256,256]{2,1,0:T(8,128)(2,1)S(1)}, u32[]{:S(2)}, u32[]{:S(2)}) collective-permute-start(bf16[2,256,256]{2,1,0:T(8,128)(2,1)S(1)} %get-tuple-element.55), channel_id=1, source_target_pairs={{32,1},{33,2},{34,3},{35,4},{36,5},{37,6},{38,7},{39,8},{40,9},{41... | collective-permute-start | bytes 786440 | tf_op jit(solution)/shard_map/ppermute | solution.py:383
  6.5 22.8 %collective-permute-start.21 = (bf16[2,256,256]{2,1,0:T(8,128)(2,1)S(1)}, bf16[2,256,256]{2,1,0:T(8,128)(2,1)S(1)}, u32[]{:S(2)}, u32[]{:S(2)}) collective-permute-start(bf16[2,256,256]{2,1,0:T(8,128)(2,1)S(1)} %get-tuple-element.56), channel_id=1, source_target_pairs={{1,0},{2,1},{3,2},{4,3},{5,4},{6,5},{7,6},{8,7},{9,8},{10,9},{11,1... | collective-permute-start | bytes 786440 | tf_op jit(solution)/shard_map/ppermute | solution.py:383
  9.0 15.2 %collective-permute-start.19 = (bf16[1,256,256]{2,1,0:T(8,128)(2,1)S(1)}, bf16[1,256,256]{2,1,0:T(8,128)(2,1)S(1)}, u32[]{:S(2)}, u32[]{:S(2)}) collective-permute-start(bf16[1,256,256]{2,1,0:T(8,128)(2,1)S(1)} %get-tuple-element.54), channel_id=1, source_target_pairs={{0,32},{1,33},{2,34},{3,35},{4,36},{5,37},{6,38},{7,39},{8,40},{9,... | collective-permute-start | bytes 393224 | tf_op jit(solution)/shard_map/ppermute | solution.py:383
  14.4 15.0 %copy-start.4 = (bf16[4,4,256,256]{3,2,1,0:T(8,128)(2,1)S(1)}, bf16[4,4,256,256]{3,2,1,0:T(8,128)(2,1)}, u32[]{:S(2)}) copy-start(bf16[4,4,256,256]{3,2,1,0:T(8,128)(2,1)} %refs_1_.14) | copy-start | bytes 6291460
  14.4 13.0 %collective-permute-start.22 = (bf16[1,256,256]{2,1,0:T(8,128)(2,1)S(1)}, bf16[1,256,256]{2,1,0:T(8,128)(2,1)S(1)}, u32[]{:S(2)}, u32[]{:S(2)}) collective-permute-start(bf16[1,256,256]{2,1,0:T(8,128)(2,1)S(1)} %get-tuple-element.57), channel_id=1, source_target_pairs={{1,32},{2,33},{3,34},{4,35},{5,36},{6,37},{7,38},{8,39},{9,40},{10... | collective-permute-start | bytes 393224 | tf_op jit(solution)/shard_map/ppermute | solution.py:383
  31.0 13.2 %collective-permute-start.23 = (bf16[2,256,256]{2,1,0:T(8,128)(2,1)S(1)}, bf16[2,256,256]{2,1,0:T(8,128)(2,1)S(1)}, u32[]{:S(2)}, u32[]{:S(2)}) collective-permute-start(bf16[2,256,256]{2,1,0:T(8,128)(2,1)S(1)} %get-tuple-element.61), channel_id=1, source_target_pairs={{0,63},{1,32},{2,33},{3,34},{4,35},{5,36},{6,37},{7,38},{8,39},{9,... | collective-permute-start | bytes 786440 | tf_op jit(solution)/shard_map/ppermute | solution.py:383
  36.1 12.0 %collective-permute-start.24 = (bf16[2,256,256]{2,1,0:T(8,128)(2,1)S(1)}, bf16[2,256,256]{2,1,0:T(8,128)(2,1)S(1)}, u32[]{:S(2)}, u32[]{:S(2)}) collective-permute-start(bf16[2,256,256]{2,1,0:T(8,128)(2,1)S(1)} %get-tuple-element.62), channel_id=1, source_target_pairs={{32,1},{33,2},{34,3},{35,4},{36,5},{37,6},{38,7},{39,8},{40,9},{41... | collective-permute-start | bytes 786440 | tf_op jit(solution)/shard_map/ppermute | solution.py:383
  37.4 10.7 %collective-permute-start.25 = (bf16[2,256,256]{2,1,0:T(8,128)(2,1)S(1)}, bf16[2,256,256]{2,1,0:T(8,128)(2,1)S(1)}, u32[]{:S(2)}, u32[]{:S(2)}) collective-permute-start(bf16[2,256,256]{2,1,0:T(8,128)(2,1)S(1)} %get-tuple-element.63), channel_id=1, source_target_pairs={{0,1},{1,2},{2,3},{3,4},{4,5},{5,6},{6,7},{7,8},{8,9},{9,10},{10,1... | collective-permute-start | bytes 786440 | tf_op jit(solution)/shard_map/ppermute | solution.py:383
  39.3 9.4 %collective-permute-start.26 = (bf16[2,256,256]{2,1,0:T(8,128)(2,1)S(1)}, bf16[2,256,256]{2,1,0:T(8,128)(2,1)S(1)}, u32[]{:S(2)}, u32[]{:S(2)}) collective-permute-start(bf16[2,256,256]{2,1,0:T(8,128)(2,1)S(1)} %get-tuple-element.64), channel_id=1, source_target_pairs={{1,0},{2,1},{3,2},{4,3},{5,4},{6,5},{7,6},{8,7},{9,8},{10,9},{11,1... | collective-permute-start | bytes 786440 | tf_op jit(solution)/shard_map/ppermute | solution.py:383
  50.1 14.2 %collective-permute-start.27 = (bf16[2,256,256]{2,1,0:T(8,128)(2,1)S(1)}, bf16[2,256,256]{2,1,0:T(8,128)(2,1)S(1)}, u32[]{:S(2)}, u32[]{:S(2)}) collective-permute-start(bf16[2,256,256]{2,1,0:T(8,128)(2,1)S(1)} %get-tuple-element.68), channel_id=1, source_target_pairs={{0,63},{1,32},{2,33},{3,34},{4,35},{5,36},{6,37},{7,38},{8,39},{9,... | collective-permute-start | bytes 786440 | tf_op jit(solution)/shard_map/ppermute | solution.py:383
  52.9 12.8 %collective-permute-start.28 = (bf16[2,256,256]{2,1,0:T(8,128)(2,1)S(1)}, bf16[2,256,256]{2,1,0:T(8,128)(2,1)S(1)}, u32[]{:S(2)}, u32[]{:S(2)}) collective-permute-start(bf16[2,256,256]{2,1,0:T(8,128)(2,1)S(1)} %get-tuple-element.69), channel_id=1, source_target_pairs={{32,1},{33,2},{34,3},{35,4},{36,5},{37,6},{38,7},{39,8},{40,9},{41... | collective-permute-start | bytes 786440 | tf_op jit(solution)/shard_map/ppermute | solution.py:383
  54.2 14.6 %collective-permute-start.29 = (bf16[2,256,256]{2,1,0:T(8,128)(2,1)S(1)}, bf16[2,256,256]{2,1,0:T(8,128)(2,1)S(1)}, u32[]{:S(2)}, u32[]{:S(2)}) collective-permute-start(bf16[2,256,256]{2,1,0:T(8,128)(2,1)S(1)} %get-tuple-element.70), channel_id=1, source_target_pairs={{0,1},{1,2},{2,3},{3,4},{4,5},{5,6},{6,7},{7,8},{8,9},{9,10},{10,1... | collective-permute-start | bytes 786440 | tf_op jit(solution)/shard_map/ppermute | solution.py:383
  59.9 8.9 %collective-permute-start.30 = (bf16[2,256,256]{2,1,0:T(8,128)(2,1)S(1)}, bf16[2,256,256]{2,1,0:T(8,128)(2,1)S(1)}, u32[]{:S(2)}, u32[]{:S(2)}) collective-permute-start(bf16[2,256,256]{2,1,0:T(8,128)(2,1)S(1)} %get-tuple-element.71), channel_id=1, source_target_pairs={{1,0},{2,1},{3,2},{4,3},{5,4},{6,5},{7,6},{8,7},{9,8},{10,9},{11,1... | collective-permute-start | bytes 786440 | tf_op jit(solution)/shard_map/ppermute | solution.py:383
  68.8 35.3 %copy-start.14 = (s32[2]{0:T(128)S(1)}, s32[2]{0:T(128)}, u32[]{:S(2)}) copy-start(s32[2]{0:T(128)} %refs_0_.3) | copy-start | bytes 28
  68.8 35.3 %copy-start.15 = (s32[2]{0:T(128)S(1)}, s32[2]{0:T(128)}, u32[]{:S(2)}) copy-start(s32[2]{0:T(128)} %refs_1_.15) | copy-start | bytes 28
  71.5 32.6 %collective-permute-start.31 = (bf16[3,256,256]{2,1,0:T(8,128)(2,1)}, bf16[3,256,256]{2,1,0:T(8,128)(2,1)}, u32[]{:S(2)}, u32[]{:S(2)}) collective-permute-start(bf16[3,256,256]{2,1,0:T(8,128)(2,1)} %get-tuple-element.74), channel_id=1, source_target_pairs={{0,31},{1,0},{2,1},{3,2},{4,3},{5,4},{6,5},{7,6},{8,7},{9,8},{10,9... | collective-permute-start | bytes 1179656 | tf_op jit(solution)/shard_map/ppermute | solution.py:383
  71.5 32.6 %all-to-all-start = ((f32[256,1,128]{2,1,0:T(1,128)}), f32[256,1,128]{2,1,0:T(1,128)S(1)}, u32[]{:S(2)}, u32[]{:S(2)}) async-start(f32[256,1,128]{2,1,0:T(1,128)} %bitcast.55), calls=%async_computation | async-start | bytes 262144 | tf_op jit(solution)/shard_map/all_to_all | solution.py:452
  104.1 4.3 %copy-start.1 = (bf16[4,2,256,256]{3,2,1,0:T(8,128)(2,1)S(1)}, bf16[4,2,256,256]{3,2,1,0:T(8,128)(2,1)}, u32[]{:S(2)}) copy-start(bf16[4,2,256,256]{3,2,1,0:T(8,128)(2,1)} %refs_3_.13) | copy-start | bytes 3145732
  108.5 0.5 copy-start.16

commit v7 on v6

--- a/solution.py
+++ b/solution.py
@@ -11,7 +11,7 @@
 AXES = ("lsec", "rsec")
 eps = 1e-06
 SHIFT = 1.75
-SHRINK = 8.0
+SHRINK = 4.0
 
 
 def shift_blocks(block, down, right):
@@ -110,6 +110,14 @@
 
 def not_at(place):
     return (lax.axis_index("rsec") != place).astype(jnp.float32)
+
+
+def on_first_core():
+    return (lax.axis_index("rsec") % 2 == 0).astype(jnp.float32)
+
+
+def mixed(one, other, share):
+    return (one.astype(jnp.float32) * share + other.astype(jnp.float32) * (1.0 - share)).astype(jnp.bfloat16)
 
 
 def masked(block, keep):
@@ -175,6 +183,9 @@
             return self.halo_refs[(0, 4)[place]][0]
         if self.step == 0 and group == 2:
             return self.packed(place)
+        if self.step > 0 and group > 1:
+            near, far = (ref[place] for ref in self.halo_refs[2:])
+            return mixed(far, near, on_first_core()) if group == 2 else mixed(near, far, on_first_core())
         return self.halo_refs[group][place]
 
     def near(self, k, term):
@@ -274,7 +285,7 @@
         new_ref, back_ref, sums_ref = refs
         sums = Sums(step + 2, blocks.size)
     else:
-        new_ref, to_top, to_low, to_left, to_right = refs
+        new_ref, to_top, to_low, to_near, to_far = refs
     for k in (0, 1, 6, 7, 2, 3, 4, 5):
         far = [term for term in range(4) if not blocks.near(k, term)]
         if len(far) == 4:
@@ -297,11 +308,14 @@
                 back_ref[step] = image
             continue
         for place, out, slot, keep in (
-            (0, to_left, 0, None), (2, to_left, 1, None), (3, to_right, 0, None), (5, to_right, 1, None),
             (6, to_top, 0, None), (7, to_top, 1, first_keep), (0, to_low, 0, None), (1, to_low, 1, last_keep),
         ):
             if place == k:
                 out[slot] = image if keep is None else masked(image, keep)
+    if not final:
+        for slot, (left, right) in enumerate(((0, 3), (2, 5))):
+            to_near[slot] = mixed(new_ref[right], new_ref[left], on_first_core())
+            to_far[slot] = mixed(new_ref[left], new_ref[right], on_first_core())
     if final:
         row = sums.write(sums_in[0:1], FIRST_SUM[ITERS])
         sums_ref[...] = jnp.broadcast_to(row, sums_ref.shape)
@@ -383,6 +397,16 @@
     return lax.ppermute(block, AXES, pairs)
 
 
+def swap(block, offset):
+    rows, cols = lax.axis_size("lsec"), lax.axis_size("rsec")
+    pairs = []
+    for row in range(rows):
+        for col in range(offset, cols - 1, 2):
+            first = row * cols + col
+            pairs += [(first, first + 1), (first + 1, first)]
+    return lax.ppermute(block, AXES, pairs)
+
+
 def call(kernel, in_specs, out_shapes, flops, *args):
     nbytes = sum(a.size * a.dtype.itemsize for a in args)
     nbytes += sum(s.size * s.dtype.itemsize for s in out_shapes)
@@ -441,12 +465,10 @@
         )
         vecs.append(result[0])
         if not final:
-            to_top, to_low, to_left, to_right = result[1:5]
+            to_top, to_low, to_near, to_far = result[1:5]
             to_top = move(to_top, 1, -1, True)
             to_low = move(to_low, -1, 1, True)
-            to_left = move(to_left, 0, -1, False)
-            to_right = move(to_right, 0, 1, False)
-            halos = [to_top, to_low, to_right, to_left]
+            halos = [to_top, to_low, swap(to_near, 0), swap(to_far, 1)]
     sums = [result[-1]]
     back = move(result[1], 0, -1, True)
     gathered = lax.all_to_all(sums[0].reshape(devices, 1, 128), AXES, 0, 0).reshape(devices, 128)

time: 110 us -> 109 us (level)
    ppermute x14 -> x10, starting transfers between devices: 39.3 us -> 28.1 us  [move(): return lax.ppermute(block, AXES, pairs)]
    ppermute x0 -> x4, starting transfers between devices: none -> 11 us  [swap(): return lax.ppermute(block, AXES, pairs)]
    ppermute x14 -> x10, waiting for transfers between devices: 15.5 us -> 10.5 us  [move(): return lax.ppermute(block, AXES, pairs)]
    ppermute x0 -> x4, waiting for transfers between devices: none -> 4.77 us  [swap(): return lax.ppermute(block, AXES, pairs)]
  transfers between devices with their start and end apart: 15 -> 15, of which waited for: 8 -> 7; matrix products, arithmetic and copies ran while one was open for 0% -> 0% of each run, Pallas kernels for 8% -> 8%
where the time goes in v7:
time: 109 us
  starting transfers between devices  58.4 us (54%)
  waiting for transfers between devices  28.2 us (26%)
  Pallas kernels  19.6 us (18%)
  between operations  1.56 us (1%)
    ppermute x10, starting transfers between devices, move(): return lax.ppermute(block, AXES, pairs)  28.1 us
    pallas_call x8, Pallas kernels, call(): pl.pallas_call(kernel, in_specs=in_specs, out_specs=[SMEM if len(shape.sh...  19.6 us
    all_to_all x1, starting transfers between devices, per_device(): lax.all_to_all(sums[0].reshape(devices, 1, 128), AXES, 0, 0)  19.3 us
    all_to_all x1, waiting for transfers between devices, per_device(): lax.all_to_all(sums[0].reshape(devices, 1, 128), AXES, 0, 0)  12.9 us
    ppermute x4, starting transfers between devices, swap(): return lax.ppermute(block, AXES, pairs)  11 us
    ppermute x10, waiting for transfers between devices, move(): return lax.ppermute(block, AXES, pairs)  10.5 us
    ppermute x4, waiting for transfers between devices, swap(): return lax.ppermute(block, AXES, pairs)  4.77 us
  transfers between devices with their start and end apart: 15, of which 7 were waited for; matrix products, arithmetic and copies ran while one was open for 0% of the time, Pallas kernels for 8%

profile of v7, /device:TPU:1, one launch (start us, length us, event | category | flops | bytes accessed | tf_op | source)
XLA Modules:
  0.0 108.5 jit_solution(4986701436685877508)
XLA Ops:
  0.6 0.0 copy-start
  0.6 0.0 copy-start.6
  0.7 0.0 copy-start.13
  0.7 1.8 %shard_map.81 = (bf16[1840,256]{1,0:T(8,128)(2,1)S(1)}, bf16[2,256,256]{2,1,0:T(8,128)(2,1)S(1)}, bf16[1,256,256]{2,1,0:T(8,128)(2,1)S(1)}, bf16[1,256,256]{2,1,0:T(8,128)(2,1)S(1)}, bf16[2,256,256]{2,1,0:T(8,128)(2,1)S(1)}) custom-call(bf16[4,2,256,256]{3,2,1,0:T(8,128)(2,1)} %refs_3_.13, bf16[2,4,256,256]{3,2,1,0:T(8,128)(2,1)} %refs_2_.11, f32[2,4]{1,0:T(2,128)} %bitcast.184), custom_call_target="tpu_custom_call" | custom-call | bytes 3825696 | tf_op jit(solution)/shard_map/pallas_call | solution.py:413
  2.5 2.8 %collective-permute-start.18 = (bf16[1840,256]{1,0:T(8,128)(2,1)S(1)}, bf16[1840,256]{1,0:T(8,128)(2,1)S(1)}, u32[]{:S(2)}, u32[]{:S(2)}) collective-permute-start(bf16[1840,256]{1,0:T(8,128)(2,1)S(1)} %get-tuple-element.51), channel_id=1, source_target_pairs={{0,1},{1,2},{2,3},{3,4},{4,5},{5,6},{6,7},{7,8},{8,9},{9,10},{10,1... | collective-permute-start | bytes 2826248 | tf_op jit(solution)/shard_map/ppermute | solution.py:397
  5.3 1.3 %collective-permute-start.20 = (bf16[2,256,256]{2,1,0:T(8,128)(2,1)S(1)}, bf16[2,256,256]{2,1,0:T(8,128)(2,1)S(1)}, u32[]{:S(2)}, u32[]{:S(2)}) collective-permute-start(bf16[2,256,256]{2,1,0:T(8,128)(2,1)S(1)} %get-tuple-element.55), channel_id=1, source_target_pairs={{32,1},{33,2},{34,3},{35,4},{36,5},{37,6},{38,7},{39,8},{40,9},{41... | collective-permute-start | bytes 786440 | tf_op jit(solution)/shard_map/ppermute | solution.py:397
  6.5 2.5 %collective-permute-start.21 = (bf16[2,256,256]{2,1,0:T(8,128)(2,1)S(1)}, bf16[2,256,256]{2,1,0:T(8,128)(2,1)S(1)}, u32[]{:S(2)}, u32[]{:S(2)}) collective-permute-start(bf16[2,256,256]{2,1,0:T(8,128)(2,1)S(1)} %get-tuple-element.56), channel_id=1, source_target_pairs={{1,0},{2,1},{3,2},{4,3},{5,4},{6,5},{7,6},{8,7},{9,8},{10,9},{11,1... | collective-permute-start | bytes 786440 | tf_op jit(solution)/shard_map/ppermute | solution.py:397
  9.0 5.3 %collective-permute-start.19 = (bf16[1,256,256]{2,1,0:T(8,128)(2,1)S(1)}, bf16[1,256,256]{2,1,0:T(8,128)(2,1)S(1)}, u32[]{:S(2)}, u32[]{:S(2)}) collective-permute-start(bf16[1,256,256]{2,1,0:T(8,128)(2,1)S(1)} %get-tuple-element.54), channel_id=1, source_target_pairs={{0,32},{1,33},{2,34},{3,35},{4,36},{5,37},{6,38},{7,39},{8,40},{9,... | collective-permute-start | bytes 393224 | tf_op jit(solution)/shard_map/ppermute | solution.py:397
  14.4 0.0 copy-start.4
  14.4 5.1 %collective-permute-start.22 = (bf16[1,256,256]{2,1,0:T(8,128)(2,1)S(1)}, bf16[1,256,256]{2,1,0:T(8,128)(2,1)S(1)}, u32[]{:S(2)}, u32[]{:S(2)}) collective-permute-start(bf16[1,256,256]{2,1,0:T(8,128)(2,1)S(1)} %get-tuple-element.57), channel_id=1, source_target_pairs={{1,32},{2,33},{3,34},{4,35},{5,36},{6,37},{7,38},{8,39},{9,40},{10... | collective-permute-start | bytes 393224 | tf_op jit(solution)/shard_map/ppermute | solution.py:397
  19.5 0.0 copy-done
  19.5 0.0 copy-done.6
  19.5 0.0 copy-done.13
  19.5 3.3 %shard_map.82 = (f32[8,256,256]{2,1,0:T(8,128)S(1)}, f32[8,128]{1,0:T(8,128)S(1)}) custom-call(f32[2,4]{1,0:T(2,128)S(1)} %bitcast.185, bf16[4,4,256,256]{3,2,1,0:T(8,128)(2,1)} %refs_1_.14, bf16[2,4,256,256]{3,2,1,0:T(8,128)(2,1)S(1)} %copy-done.6, bf16[4,2,256,256]{3,2,1,0:T(8,128)(2,1)S(1)} %copy-done), custom_call_target="tpu_custom_call" | custom-call | flops 1342177280 | bytes 6295584 | tf_op jit(solution)/shard_map/pallas_call | solution.py:413
  22.8 1.5 %collective-permute-done.19.refs_6_ = bf16[1,256,256]{2,1,0:T(8,128)(2,1)S(1)} collective-permute-done((bf16[1,256,256]{2,1,0:T(8,128)(2,1)S(1)}, bf16[1,256,256]{2,1,0:T(8,128)(2,1)S(1)}, u32[]{:S(2)}, u32[]{:S(2)}) %collective-permute-start.19) | collective-permute-done | bytes 131104 | tf_op jit(solution)/shard_map/ppermute | solution.py:397
  24.3 3.1 %collective-permute-done.22.refs_9_ = bf16[1,256,256]{2,1,0:T(8,128)(2,1)S(1)} collective-permute-done((bf16[1,256,256]{2,1,0:T(8,128)(2,1)S(1)}, bf16[1,256,256]{2,1,0:T(8,128)(2,1)S(1)}, u32[]{:S(2)}, u32[]{:S(2)}) %collective-permute-start.22) | collective-permute-done | bytes 131104 | tf_op jit(solution)/shard_map/ppermute | solution.py:397
  27.3 0.0 collective-permute-done.20.refs_7_
  27.3 2.0 %collective-permute-done.21.refs_8_ = bf16[2,256,256]{2,1,0:T(8,128)(2,1)S(1)} collective-permute-done((bf16[2,256,256]{2,1,0:T(8,128)(2,1)S(1)}, bf16[2,256,256]{2,1,0:T(8,128)(2,1)S(1)}, u32[]{:S(2)}, u32[]{:S(2)}) %collective-permute-start.21) | collective-permute-done | bytes 262176 | tf_op jit(solution)/shard_map/ppermute | solution.py:397
  29.4 0.0 collective-permute-done.18.refs_4_
  29.4 0.0 copy-done.4
  29.4 1.7 %shard_map.83 = (bf16[8,256,256]{2,1,0:T(8,128)(2,1)S(1)}, bf16[2,256,256]{2,1,0:T(8,128)(2,1)S(1)}, bf16[2,256,256]{2,1,0:T(8,128)(2,1)S(1)}, bf16[2,256,256]{2,1,0:T(8,128)(2,1)S(1)}, bf16[2,256,256]{2,1,0:T(8,128)(2,1)S(1)}) custom-call(f32[2,4]{1,0:T(2,128)S(1)} %bitcast.186, bf16[4,4,256,256]{3,2,1,0:T(8,128)(2,1)S(1)} %copy-done.4, ...), custom_call_target="tpu_custom_call" | custom-call | flops 805306368 | bytes 10117152 | tf_op jit(solution)/shard_map/pallas_call | solution.py:413
  31.0 5.1 %collective-permute-start.23 = (bf16[2,256,256]{2,1,0:T(8,128)(2,1)S(1)}, bf16[2,256,256]{2,1,0:T(8,128)(2,1)S(1)}, u32[]{:S(2)}, u32[]{:S(2)}) collective-permute-start(bf16[2,256,256]{2,1,0:T(8,128)(2,1)S(1)} %get-tuple-element.61), channel_id=1, source_target_pairs={{0,63},{1,32},{2,33},{3,34},{4,35},{5,36},{6,37},{7,38},{8,39},{9,... | collective-permute-start | bytes 786440 | tf_op jit(solution)/shard_map/ppermute | solution.py:397
  36.1 1.3 %collective-permute-start.24 = (bf16[2,256,256]{2,1,0:T(8,128)(2,1)S(1)}, bf16[2,256,256]{2,1,0:T(8,128)(2,1)S(1)}, u32[]{:S(2)}, u32[]{:S(2)}) collective-permute-start(bf16[2,256,256]{2,1,0:T(8,128)(2,1)S(1)} %get-tuple-element.62), channel_id=1, source_target_pairs={{32,1},{33,2},{34,3},{35,4},{36,5},{37,6},{38,7},{39,8},{40,9},{41... | collective-permute-start | bytes 786440 | tf_op jit(solution)/shard_map/ppermute | solution.py:397
  37.4 0.1 collective-permute-start.25
  37.5 4.2 %collective-permute-start.26 = (bf16[2,256,256]{2,1,0:T(8,128)(2,1)S(1)}, bf16[2,256,256]{2,1,0:T(8,128)(2,1)S(1)}, u32[]{:S(2)}, u32[]{:S(2)}) collective-permute-start(bf16[2,256,256]{2,1,0:T(8,128)(2,1)S(1)} %get-tuple-element.64), channel_id=1, source_target_pairs={{1,2},{2,1},{3,4},{4,3},{5,6},{6,5},{7,8},{8,7},{9,10},{10,9},{11,... | collective-permute-start | bytes 786440 | tf_op jit(solution)/shard_map/ppermute | solution.py:407
  41.7 2.5 %shard_map.84 = (f32[8,256,256]{2,1,0:T(8,128)S(1)}, f32[8,128]{1,0:T(8,128)S(1)}) custom-call(f32[2,4]{1,0:T(2,128)S(1)} %bitcast.187, bf16[4,4,256,256]{3,2,1,0:T(8,128)(2,1)S(1)} %copy-done.4, bf16[2,4,256,256]{3,2,1,0:T(8,128)(2,1)S(1)} %copy-done.6, bf16[4,2,256,256]{3,2,1,0:T(8,128)(2,1)S(1)} %copy-done, ...), custom_call_target="tpu_custom_call" | custom-call | flops 1610612736 | bytes 8290336 | tf_op jit(solution)/shard_map/pallas_call | solution.py:413
  44.2 0.0 collective-permute-done.23.refs_7_
  44.2 3.9 %collective-permute-done.24.refs_8_ = bf16[2,256,256]{2,1,0:T(8,128)(2,1)S(1)} collective-permute-done((bf16[2,256,256]{2,1,0:T(8,128)(2,1)S(1)}, bf16[2,256,256]{2,1,0:T(8,128)(2,1)S(1)}, u32[]{:S(2)}, u32[]{:S(2)}) %collective-permute-start.24) | collective-permute-done | bytes 262176 | tf_op jit(solution)/shard_map/ppermute | solution.py:397
  48.1 0.0 collective-permute-done.25.refs_9_
  48.1 0.1 collective-permute-done.26.refs_10_
  48.2 1.4 %shard_map.85 = (bf16[8,256,256]{2,1,0:T(8,128)(2,1)S(1)}, bf16[2,256,256]{2,1,0:T(8,128)(2,1)S(1)}, bf16[2,256,256]{2,1,0:T(8,128)(2,1)S(1)}, bf16[2,256,256]{2,1,0:T(8,128)(2,1)S(1)}, bf16[2,256,256]{2,1,0:T(8,128)(2,1)S(1)}) custom-call(f32[2,4]{1,0:T(2,128)S(1)} %bitcast.188, bf16[4,4,256,256]{3,2,1,0:T(8,128)(2,1)S(1)} %copy-done.4, ...), custom_call_target="tpu_custom_call" | custom-call | flops 536870912 | bytes 11427872 | tf_op jit(solution)/shard_map/pallas_call | solution.py:413
  49.7 3.3 %collective-permute-start.27 = (bf16[2,256,256]{2,1,0:T(8,128)(2,1)S(1)}, bf16[2,256,256]{2,1,0:T(8,128)(2,1)S(1)}, u32[]{:S(2)}, u32[]{:S(2)}) collective-permute-start(bf16[2,256,256]{2,1,0:T(8,128)(2,1)S(1)} %get-tuple-element.68), channel_id=1, source_target_pairs={{0,63},{1,32},{2,33},{3,34},{4,35},{5,36},{6,37},{7,38},{8,39},{9,... | collective-permute-start | bytes 786440 | tf_op jit(solution)/shard_map/ppermute | solution.py:397
  53.0 1.3 %collective-permute-start.28 = (bf16[2,256,256]{2,1,0:T(8,128)(2,1)S(1)}, bf16[2,256,256]{2,1,0:T(8,128)(2,1)S(1)}, u32[]{:S(2)}, u32[]{:S(2)}) collective-permute-start(bf16[2,256,256]{2,1,0:T(8,128)(2,1)S(1)} %get-tuple-element.69), channel_id=1, source_target_pairs={{32,1},{33,2},{34,3},{35,4},{36,5},{37,6},{38,7},{39,8},{40,9},{41... | collective-permute-start | bytes 786440 | tf_op jit(solution)/shard_map/ppermute | solution.py:397
  54.3 4.4 %collective-permute-start.29 = (bf16[2,256,256]{2,1,0:T(8,128)(2,1)S(1)}, bf16[2,256,256]{2,1,0:T(8,128)(2,1)S(1)}, u32[]{:S(2)}, u32[]{:S(2)}) collective-permute-start(bf16[2,256,256]{2,1,0:T(8,128)(2,1)S(1)} %get-tuple-element.70), channel_id=1, source_target_pairs={{0,1},{1,0},{2,3},{3,2},{4,5},{5,4},{6,7},{7,6},{8,9},{9,8},{10,11... | collective-permute-start | bytes 786440 | tf_op jit(solution)/shard_map/ppermute | solution.py:407
  58.7 2.2 %collective-permute-start.30 = (bf16[2,256,256]{2,1,0:T(8,128)(2,1)S(1)}, bf16[2,256,256]{2,1,0:T(8,128)(2,1)S(1)}, u32[]{:S(2)}, u32[]{:S(2)}) collective-permute-start(bf16[2,256,256]{2,1,0:T(8,128)(2,1)S(1)} %get-tuple-element.71), channel_id=1, source_target_pairs={{1,2},{2,1},{3,4},{4,3},{5,6},{6,5},{7,8},{8,7},{9,10},{10,9},{11,... | collective-permute-start | bytes 786440 | tf_op jit(solution)/shard_map/ppermute | solution.py:407
  60.9 2.5 %shard_map.86 = (f32[8,256,256]{2,1,0:T(8,128)S(1)}, f32[8,128]{1,0:T(8,128)S(1)}) custom-call(f32[2,4]{1,0:T(2,128)S(1)} %bitcast.189, bf16[4,4,256,256]{3,2,1,0:T(8,128)(2,1)S(1)} %copy-done.4, bf16[2,4,256,256]{3,2,1,0:T(8,128)(2,1)S(1)} %copy-done.6, bf16[4,2,256,256]{3,2,1,0:T(8,128)(2,1)S(1)} %copy-done, ...), custom_call_target="tpu_custom_call" | custom-call | flops 1610612736 | bytes 9338912 | tf_op jit(solution)/shard_map/pallas_call | solution.py:413
  63.4 0.0 collective-permute-done.27.refs_9_
  63.5 0.0 collective-permute-done.28.refs_10_
  63.5 0.0 collective-permute-done.29.refs_11_
  63.5 4.6 %collective-permute-done.30.refs_12_ = bf16[2,256,256]{2,1,0:T(8,128)(2,1)S(1)} collective-permute-done((bf16[2,256,256]{2,1,0:T(8,128)(2,1)S(1)}, bf16[2,256,256]{2,1,0:T(8,128)(2,1)S(1)}, u32[]{:S(2)}, u32[]{:S(2)}) %collective-permute-start.30) | collective-permute-done | bytes 262176 | tf_op jit(solution)/shard_map/ppermute | solution.py:407
  68.1 0.0 copy-start.14
  68.1 0.0 copy-start.15
  68.1 2.8 %shard_map.87 = (bf16[8,256,256]{2,1,0:T(8,128)(2,1)S(1)}, bf16[3,256,256]{2,1,0:T(8,128)(2,1)}, f32[256,128]{1,0:T(8,128)}) custom-call(f32[2,4]{1,0:T(2,128)S(1)} %bitcast.190, bf16[4,4,256,256]{3,2,1,0:T(8,128)(2,1)S(1)} %copy-done.4, bf16[2,4,256,256]{3,2,1,0:T(8,128)(2,1)S(1)} %copy-done.6, bf16[4,2,256,256]{3,2,1,0:T(8,128)(2,1)S(1)} %copy-done, ...), custom_call_target="tpu_custom_call" | custom-call | flops 536870912 | bytes 11956256 | tf_op jit(solution)/shard_map/pallas_call | solution.py:413
  70.9 0.2 collective-permute-start.31
  71.2 19.3 %all-to-all-start = ((f32[256,1,128]{2,1,0:T(1,128)}), f32[256,1,128]{2,1,0:T(1,128)S(1)}, u32[]{:S(2)}, u32[]{:S(2)}) async-start(f32[256,1,128]{2,1,0:T(1,128)} %bitcast.55), calls=%async_computation | async-start | bytes 262144 | tf_op jit(solution)/shard_map/all_to_all | solution.py:474
  90.5 12.9 %all-to-all-done = f32[256,1,128]{2,1,0:T(1,128)S(1)} async-done(((f32[256,1,128]{2,1,0:T(1,128)}), f32[256,1,128]{2,1,0:T(1,128)S(1)}, u32[]{:S(2)}, u32[]{:S(2)}) %all-to-all-start) | async-done | bytes 131104 | tf_op jit(solution)/shard_map/all_to_all | solution.py:474
  103.4 0.0 collective-permute-done.31.refs_7_
  103.4 0.0 copy-done.14
  103.4 0.0 copy-done.15
  103.4 0.0 copy-start.1
  103.4 3.7 %shard_map.88 = (bf16[4,2,256,256]{3,2,1,0:T(8,128)(2,1)}, f32[3]{0:T(128)S(1)}, f32[1]{0:T(128)}) custom-call(s32[2]{0:T(128)S(1)} %copy-done.14, s32[2]{0:T(128)S(1)} %copy-done.15, f32[256,128]{1,0:T(8,128)S(1)} %bitcast.183, bf16[4,2,256,256]{3,2,1,0:T(8,128)(2,1)} %refs_3_.13, bf16[8,256,256]{2,1,0:T(8,128)(2,1)S(1)} %get-tuple-element.58.refs_6_.refs_7_.refs_4_, ...), custom_call_target="tpu_custom_call" | custom-call | bytes 5767200 | tf_op jit(solution)/shard_map/pallas_call | solution.py:413
  107.7 0.0 copy-done.1
  107.8 0.2 conditional.1
  108.0 0.0 copy-start.16
  108.0 0.5 copy-done.16
Async XLA Ops:
  0.6 18.9 %copy-start = (bf16[4,2,256,256]{3,2,1,0:T(8,128)(2,1)S(1)}, bf16[4,2,256,256]{3,2,1,0:T(8,128)(2,1)}, u32[]{:S(2)}) copy-start(bf16[4,2,256,256]{3,2,1,0:T(8,128)(2,1)} %refs_3_.13) | copy-start | bytes 3145732
  0.6 18.9 %copy-start.6 = (bf16[2,4,256,256]{3,2,1,0:T(8,128)(2,1)S(1)}, bf16[2,4,256,256]{3,2,1,0:T(8,128)(2,1)}, u32[]{:S(2)}) copy-start(bf16[2,4,256,256]{3,2,1,0:T(8,128)(2,1)} %refs_2_.11) | copy-start | bytes 3145732
  0.7 18.9 %copy-start.13 = (f32[4,2]{0,1:T(2,128)S(1)}, f32[4,2]{0,1:T(2,128)}, u32[]{:S(2)}) copy-start(f32[4,2]{0,1:T(2,128)} %param.11) | copy-start | bytes 100
  2.5 26.9 %collective-permute-start.18 = (bf16[1840,256]{1,0:T(8,128)(2,1)S(1)}, bf16[1840,256]{1,0:T(8,128)(2,1)S(1)}, u32[]{:S(2)}, u32[]{:S(2)}) collective-permute-start(bf16[1840,256]{1,0:T(8,128)(2,1)S(1)} %get-tuple-element.51), channel_id=1, source_target_pairs={{0,1},{1,2},{2,3},{3,4},{4,5},{5,6},{6,7},{7,8},{8,9},{9,10},{10,1... | collective-permute-start | bytes 2826248 | tf_op jit(solution)/shard_map/ppermute | solution.py:397
  5.3 22.1 %collective-permute-start.20 = (bf16[2,256,256]{2,1,0:T(8,128)(2,1)S(1)}, bf16[2,256,256]{2,1,0:T(8,128)(2,1)S(1)}, u32[]{:S(2)}, u32[]{:S(2)}) collective-permute-start(bf16[2,256,256]{2,1,0:T(8,128)(2,1)S(1)} %get-tuple-element.55), channel_id=1, source_target_pairs={{32,1},{33,2},{34,3},{35,4},{36,5},{37,6},{38,7},{39,8},{40,9},{41... | collective-permute-start | bytes 786440 | tf_op jit(solution)/shard_map/ppermute | solution.py:397
  6.5 22.8 %collective-permute-start.21 = (bf16[2,256,256]{2,1,0:T(8,128)(2,1)S(1)}, bf16[2,256,256]{2,1,0:T(8,128)(2,1)S(1)}, u32[]{:S(2)}, u32[]{:S(2)}) collective-permute-start(bf16[2,256,256]{2,1,0:T(8,128)(2,1)S(1)} %get-tuple-element.56), channel_id=1, source_target_pairs={{1,0},{2,1},{3,2},{4,3},{5,4},{6,5},{7,6},{8,7},{9,8},{10,9},{11,1... | collective-permute-start | bytes 786440 | tf_op jit(solution)/shard_map/ppermute | solution.py:397
  9.0 15.2 %collective-permute-start.19 = (bf16[1,256,256]{2,1,0:T(8,128)(2,1)S(1)}, bf16[1,256,256]{2,1,0:T(8,128)(2,1)S(1)}, u32[]{:S(2)}, u32[]{:S(2)}) collective-permute-start(bf16[1,256,256]{2,1,0:T(8,128)(2,1)S(1)} %get-tuple-element.54), channel_id=1, source_target_pairs={{0,32},{1,33},{2,34},{3,35},{4,36},{5,37},{6,38},{7,39},{8,40},{9,... | collective-permute-start | bytes 393224 | tf_op jit(solution)/shard_map/ppermute | solution.py:397
  14.4 15.0 %copy-start.4 = (bf16[4,4,256,256]{3,2,1,0:T(8,128)(2,1)S(1)}, bf16[4,4,256,256]{3,2,1,0:T(8,128)(2,1)}, u32[]{:S(2)}) copy-start(bf16[4,4,256,256]{3,2,1,0:T(8,128)(2,1)} %refs_1_.14) | copy-start | bytes 6291460
  14.4 13.0 %collective-permute-start.22 = (bf16[1,256,256]{2,1,0:T(8,128)(2,1)S(1)}, bf16[1,256,256]{2,1,0:T(8,128)(2,1)S(1)}, u32[]{:S(2)}, u32[]{:S(2)}) collective-permute-start(bf16[1,256,256]{2,1,0:T(8,128)(2,1)S(1)} %get-tuple-element.57), channel_id=1, source_target_pairs={{1,32},{2,33},{3,34},{4,35},{5,36},{6,37},{7,38},{8,39},{9,40},{10... | collective-permute-start | bytes 393224 | tf_op jit(solution)/shard_map/ppermute | solution.py:397
  31.0 13.2 %collective-permute-start.23 = (bf16[2,256,256]{2,1,0:T(8,128)(2,1)S(1)}, bf16[2,256,256]{2,1,0:T(8,128)(2,1)S(1)}, u32[]{:S(2)}, u32[]{:S(2)}) collective-permute-start(bf16[2,256,256]{2,1,0:T(8,128)(2,1)S(1)} %get-tuple-element.61), channel_id=1, source_target_pairs={{0,63},{1,32},{2,33},{3,34},{4,35},{5,36},{6,37},{7,38},{8,39},{9,... | collective-permute-start | bytes 786440 | tf_op jit(solution)/shard_map/ppermute | solution.py:397
  36.1 12.0 %collective-permute-start.24 = (bf16[2,256,256]{2,1,0:T(8,128)(2,1)S(1)}, bf16[2,256,256]{2,1,0:T(8,128)(2,1)S(1)}, u32[]{:S(2)}, u32[]{:S(2)}) collective-permute-start(bf16[2,256,256]{2,1,0:T(8,128)(2,1)S(1)} %get-tuple-element.62), channel_id=1, source_target_pairs={{32,1},{33,2},{34,3},{35,4},{36,5},{37,6},{38,7},{39,8},{40,9},{41... | collective-permute-start | bytes 786440 | tf_op jit(solution)/shard_map/ppermute | solution.py:397
  37.4 10.7 %collective-permute-start.25 = (bf16[2,256,256]{2,1,0:T(8,128)(2,1)S(1)}, bf16[2,256,256]{2,1,0:T(8,128)(2,1)S(1)}, u32[]{:S(2)}, u32[]{:S(2)}) collective-permute-start(bf16[2,256,256]{2,1,0:T(8,128)(2,1)S(1)} %get-tuple-element.63), channel_id=1, source_target_pairs={{0,1},{1,0},{2,3},{3,2},{4,5},{5,4},{6,7},{7,6},{8,9},{9,8},{10,11... | collective-permute-start | bytes 786440 | tf_op jit(solution)/shard_map/ppermute | solution.py:407
  37.5 10.7 %collective-permute-start.26 = (bf16[2,256,256]{2,1,0:T(8,128)(2,1)S(1)}, bf16[2,256,256]{2,1,0:T(8,128)(2,1)S(1)}, u32[]{:S(2)}, u32[]{:S(2)}) collective-permute-start(bf16[2,256,256]{2,1,0:T(8,128)(2,1)S(1)} %get-tuple-element.64), channel_id=1, source_target_pairs={{1,2},{2,1},{3,4},{4,3},{5,6},{6,5},{7,8},{8,7},{9,10},{10,9},{11,... | collective-permute-start | bytes 786440 | tf_op jit(solution)/shard_map/ppermute | solution.py:407
  49.7 13.8 %collective-permute-start.27 = (bf16[2,256,256]{2,1,0:T(8,128)(2,1)S(1)}, bf16[2,256,256]{2,1,0:T(8,128)(2,1)S(1)}, u32[]{:S(2)}, u32[]{:S(2)}) collective-permute-start(bf16[2,256,256]{2,1,0:T(8,128)(2,1)S(1)} %get-tuple-element.68), channel_id=1, source_target_pairs={{0,63},{1,32},{2,33},{3,34},{4,35},{5,36},{6,37},{7,38},{8,39},{9,... | collective-permute-start | bytes 786440 | tf_op jit(solution)/shard_map/ppermute | solution.py:397
  53.0 10.5 %collective-permute-start.28 = (bf16[2,256,256]{2,1,0:T(8,128)(2,1)S(1)}, bf16[2,256,256]{2,1,0:T(8,128)(2,1)S(1)}, u32[]{:S(2)}, u32[]{:S(2)}) collective-permute-start(bf16[2,256,256]{2,1,0:T(8,128)(2,1)S(1)} %get-tuple-element.69), channel_id=1, source_target_pairs={{32,1},{33,2},{34,3},{35,4},{36,5},{37,6},{38,7},{39,8},{40,9},{41... | collective-permute-start | bytes 786440 | tf_op jit(solution)/shard_map/ppermute | solution.py:397
  54.3 9.2 %collective-permute-start.29 = (bf16[2,256,256]{2,1,0:T(8,128)(2,1)S(1)}, bf16[2,256,256]{2,1,0:T(8,128)(2,1)S(1)}, u32[]{:S(2)}, u32[]{:S(2)}) collective-permute-start(bf16[2,256,256]{2,1,0:T(8,128)(2,1)S(1)} %get-tuple-element.70), channel_id=1, source_target_pairs={{0,1},{1,0},{2,3},{3,2},{4,5},{5,4},{6,7},{7,6},{8,9},{9,8},{10,11... | collective-permute-start | bytes 786440 | tf_op jit(solution)/shard_map/ppermute | solution.py:407
  58.7 9.4 %collective-permute-start.30 = (bf16[2,256,256]{2,1,0:T(8,128)(2,1)S(1)}, bf16[2,256,256]{2,1,0:T(8,128)(2,1)S(1)}, u32[]{:S(2)}, u32[]{:S(2)}) collective-permute-start(bf16[2,256,256]{2,1,0:T(8,128)(2,1)S(1)} %get-tuple-element.71), channel_id=1, source_target_pairs={{1,2},{2,1},{3,4},{4,3},{5,6},{6,5},{7,8},{8,7},{9,10},{10,9},{11,... | collective-permute-start | bytes 786440 | tf_op jit(solution)/shard_map/ppermute | solution.py:407
  68.1 35.3 %copy-start.14 = (s32[2]{0:T(128)S(1)}, s32[2]{0:T(128)}, u32[]{:S(2)}) copy-start(s32[2]{0:T(128)} %refs_0_.3) | copy-start | bytes 28
  68.1 35.3 %copy-start.15 = (s32[2]{0:T(128)S(1)}, s32[2]{0:T(128)}, u32[]{:S(2)}) copy-start(s32[2]{0:T(128)} %refs_1_.15) | copy-start | bytes 28
  70.9 32.5 %collective-permute-start.31 = (bf16[3,256,256]{2,1,0:T(8,128)(2,1)}, bf16[3,256,256]{2,1,0:T(8,128)(2,1)}, u32[]{:S(2)}, u32[]{:S(2)}) collective-permute-start(bf16[3,256,256]{2,1,0:T(8,128)(2,1)} %get-tuple-element.74), channel_id=1, source_target_pairs={{0,31},{1,0},{2,1},{3,2},{4,3},{5,4},{6,5},{7,6},{8,7},{9,8},{10,9... | collective-permute-start | bytes 1179656 | tf_op jit(solution)/shard_map/ppermute | solution.py:397
  71.2 32.2 %all-to-all-start = ((f32[256,1,128]{2,1,0:T(1,128)}), f32[256,1,128]{2,1,0:T(1,128)S(1)}, u32[]{:S(2)}, u32[]{:S(2)}) async-start(f32[256,1,128]{2,1,0:T(1,128)} %bitcast.55), calls=%async_computation | async-start | bytes 262144 | tf_op jit(solution)/shard_map/all_to_all | solution.py:474
  103.4 4.3 %copy-start.1 = (bf16[4,2,256,256]{3,2,1,0:T(8,128)(2,1)S(1)}, bf16[4,2,256,256]{3,2,1,0:T(8,128)(2,1)}, u32[]{:S(2)}) copy-start(bf16[4,2,256,256]{3,2,1,0:T(8,128)(2,1)} %refs_3_.13) | copy-start | bytes 3145732
  108.0 0.5 copy-start.16

commit v8 on v7

--- a/solution.py
+++ b/solution.py
@@ -124,25 +124,33 @@
     return (block.astype(jnp.float32) * keep).astype(jnp.bfloat16)
 
 
-def pack_kernel(last, psi_ref, right_ref, energy_ref, pack_ref, left_out, up_out, corner_out, low_out):
+def pack_kernel(last, psi_ref, right_ref, energy_ref, pack_ref, left_out, up_out, corner_out, low_out, sems):
     size = psi_ref.shape[-1]
-    inner = not_at(last)
-    for place in range(2):
-        pack_ref[place * size : (place + 1) * size] = masked(psi_ref[place + 1, 1], inner)
-        left_out[place] = psi_ref[place, 0]
-    pack_ref[2 * size : 3 * size] = psi_ref[3, 1]
-    for term in range(4):
-        pack_ref[(3 + term) * size : (4 + term) * size] = right_ref[1, term]
+
+    def packed(place):
+        return pack_ref.at[place * size : (place + 1) * size]
+
+    pairs = [(psi_ref.at[place + 1, 1], packed(place)) for place in range(3)]
+    pairs += [(right_ref.at[1, term], packed(3 + term)) for term in range(4)]
+    pairs += [(psi_ref.at[place, 0], left_out.at[place]) for place in range(2)]
+    pairs += [(psi_ref.at[3, 1], up_out.at[0]), (psi_ref.at[3, 0], corner_out.at[0])]
+    pairs += [(psi_ref.at[0, place], low_out.at[place]) for place in range(2)]
+    copies = [pltpu.make_async_copy(source, target, sems.at[i]) for i, (source, target) in enumerate(pairs)]
+    for copy in copies:
+        copy.start()
     rest = jnp.full((16, size), energy_ref[1, 3], jnp.float32)
     for place in range(3):
         part = rest.astype(jnp.bfloat16)
         start = 7 * size + 16 * place
         pack_ref[start : start + 16] = part
         rest = rest - part.astype(jnp.float32)
-    up_out[0] = psi_ref[3, 1]
-    corner_out[0] = psi_ref[3, 0]
-    low_out[0] = psi_ref[0, 0]
-    low_out[1] = masked(psi_ref[0, 1], inner)
+    for copy in copies:
+        copy.wait()
+
+    @pl.when(lax.axis_index("rsec") == last)
+    def _():
+        pack_ref[: 2 * size] = jnp.zeros((2 * size, size), jnp.bfloat16)
+        low_out[1] = jnp.zeros((size, size), jnp.bfloat16)
 
 
 def place_in(row, lane, value):
@@ -407,7 +415,7 @@
     return lax.ppermute(block, AXES, pairs)
 
 
-def call(kernel, in_specs, out_shapes, flops, *args):
+def call(kernel, in_specs, out_shapes, flops, *args, scratch=()):
     nbytes = sum(a.size * a.dtype.itemsize for a in args)
     nbytes += sum(s.size * s.dtype.itemsize for s in out_shapes)
     return pl.pallas_call(
@@ -415,6 +423,7 @@
         in_specs=in_specs,
         out_specs=[SMEM if len(shape.shape) == 1 else VMEM for shape in out_shapes],
         out_shape=out_shapes,
+        scratch_shapes=list(scratch),
         compiler_params=PARAMS,
         cost_estimate=pl.CostEstimate(flops=flops, bytes_accessed=nbytes, transcendentals=0),
     )(*args)
@@ -432,9 +441,9 @@
     levels = energies.T
     pack, to_left, to_up, to_corner, to_low = call(
         lambda *refs: pack_kernel(last, *refs),
-        [VMEM, VMEM, SMEM],
+        [pl.BlockSpec(memory_space=pl.ANY)] * 2 + [SMEM],
         [jax.ShapeDtypeStruct((7 * size + 48, size), jnp.bfloat16), blocks(2), blocks(1), blocks(1), blocks(2)],
-        0, psi, right_env, levels,
+        0, psi, right_env, levels, scratch=[pltpu.SemaphoreType.DMA((13,))],
     )
     pack = move(pack, 0, 1, True)
     to_low = move(to_low, -1, 1, True)

time: 109 us -> 110 us (level)
  no operation moved by 1% of the time
where the time goes in v8:
time: 110 us; the launch traced here: 109 us
  starting transfers between devices  58.3 us (53%)
  waiting for transfers between devices  28.2 us (26%)
  Pallas kernels  20.2 us (18%)
  between operations  1.56 us (1%)
    ppermute x10, starting transfers between devices, move(): return lax.ppermute(block, AXES, pairs)  28 us
    pallas_call x8, Pallas kernels, call(): pl.pallas_call(kernel, in_specs=in_specs, out_specs=[SMEM if len(shape.sh...  20.2 us
    all_to_all x1, starting transfers between devices, per_device(): lax.all_to_all(sums[0].reshape(devices, 1, 128), AXES, 0, 0)  19.3 us
    all_to_all x1, waiting for transfers between devices, per_device(): lax.all_to_all(sums[0].reshape(devices, 1, 128), AXES, 0, 0)  12.9 us
    ppermute x4, starting transfers between devices, swap(): return lax.ppermute(block, AXES, pairs)  10.9 us
    ppermute x10, waiting for transfers between devices, move(): return lax.ppermute(block, AXES, pairs)  10.5 us
    ppermute x4, waiting for transfers between devices, swap(): return lax.ppermute(block, AXES, pairs)  4.83 us
  transfers between devices with their start and end apart: 15, of which 7 were waited for; matrix products, arithmetic and copies ran while one was open for 0% of the time, Pallas kernels for 8%

profile of v8, /device:TPU:1, one launch (start us, length us, event | category | flops | bytes accessed | tf_op | source)
XLA Modules:
  0.0 109.1 jit_solution(7380442018617395401)
XLA Ops:
  0.6 0.0 copy-start
  0.6 0.0 copy-start.6
  0.7 0.0 copy-start.13
  0.7 2.4 %shard_map.81 = (bf16[1840,256]{1,0:T(8,128)(2,1)S(1)}, bf16[2,256,256]{2,1,0:T(8,128)(2,1)S(1)}, bf16[1,256,256]{2,1,0:T(8,128)(2,1)S(1)}, bf16[1,256,256]{2,1,0:T(8,128)(2,1)S(1)}, bf16[2,256,256]{2,1,0:T(8,128)(2,1)S(1)}) custom-call(bf16[4,2,256,256]{3,2,1,0:T(8,128)(2,1)} %refs_3_.13, bf16[2,4,256,256]{3,2,1,0:T(8,128)(2,1)} %refs_2_.11, f32[2,4]{1,0:T(2,128)} %bitcast.184), custom_call_target="tpu_custom_call" | custom-call | bytes 3825696 | tf_op jit(solution)/shard_map/pallas_call | solution.py:421
  3.1 2.8 %collective-permute-start.18 = (bf16[1840,256]{1,0:T(8,128)(2,1)S(1)}, bf16[1840,256]{1,0:T(8,128)(2,1)S(1)}, u32[]{:S(2)}, u32[]{:S(2)}) collective-permute-start(bf16[1840,256]{1,0:T(8,128)(2,1)S(1)} %get-tuple-element.51), channel_id=1, source_target_pairs={{0,1},{1,2},{2,3},{3,4},{4,5},{5,6},{6,7},{7,8},{8,9},{9,10},{10,1... | collective-permute-start | bytes 2826248 | tf_op jit(solution)/shard_map/ppermute | solution.py:405
  5.8 1.3 %collective-permute-start.20 = (bf16[2,256,256]{2,1,0:T(8,128)(2,1)S(1)}, bf16[2,256,256]{2,1,0:T(8,128)(2,1)S(1)}, u32[]{:S(2)}, u32[]{:S(2)}) collective-permute-start(bf16[2,256,256]{2,1,0:T(8,128)(2,1)S(1)} %get-tuple-element.55), channel_id=1, source_target_pairs={{32,1},{33,2},{34,3},{35,4},{36,5},{37,6},{38,7},{39,8},{40,9},{41... | collective-permute-start | bytes 786440 | tf_op jit(solution)/shard_map/ppermute | solution.py:405
  7.1 2.5 %collective-permute-start.21 = (bf16[2,256,256]{2,1,0:T(8,128)(2,1)S(1)}, bf16[2,256,256]{2,1,0:T(8,128)(2,1)S(1)}, u32[]{:S(2)}, u32[]{:S(2)}) collective-permute-start(bf16[2,256,256]{2,1,0:T(8,128)(2,1)S(1)} %get-tuple-element.56), channel_id=1, source_target_pairs={{1,0},{2,1},{3,2},{4,3},{5,4},{6,5},{7,6},{8,7},{9,8},{10,9},{11,1... | collective-permute-start | bytes 786440 | tf_op jit(solution)/shard_map/ppermute | solution.py:405
  9.6 5.3 %collective-permute-start.19 = (bf16[1,256,256]{2,1,0:T(8,128)(2,1)S(1)}, bf16[1,256,256]{2,1,0:T(8,128)(2,1)S(1)}, u32[]{:S(2)}, u32[]{:S(2)}) collective-permute-start(bf16[1,256,256]{2,1,0:T(8,128)(2,1)S(1)} %get-tuple-element.54), channel_id=1, source_target_pairs={{0,32},{1,33},{2,34},{3,35},{4,36},{5,37},{6,38},{7,39},{8,40},{9,... | collective-permute-start | bytes 393224 | tf_op jit(solution)/shard_map/ppermute | solution.py:405
  14.9 0.0 copy-start.4
  15.0 5.1 %collective-permute-start.22 = (bf16[1,256,256]{2,1,0:T(8,128)(2,1)S(1)}, bf16[1,256,256]{2,1,0:T(8,128)(2,1)S(1)}, u32[]{:S(2)}, u32[]{:S(2)}) collective-permute-start(bf16[1,256,256]{2,1,0:T(8,128)(2,1)S(1)} %get-tuple-element.57), channel_id=1, source_target_pairs={{1,32},{2,33},{3,34},{4,35},{5,36},{6,37},{7,38},{8,39},{9,40},{10... | collective-permute-start | bytes 393224 | tf_op jit(solution)/shard_map/ppermute | solution.py:405
  20.1 0.0 copy-done
  20.1 0.0 copy-done.6
  20.1 0.0 copy-done.13
  20.1 3.3 %shard_map.82 = (f32[8,256,256]{2,1,0:T(8,128)S(1)}, f32[8,128]{1,0:T(8,128)S(1)}) custom-call(f32[2,4]{1,0:T(2,128)S(1)} %bitcast.185, bf16[4,4,256,256]{3,2,1,0:T(8,128)(2,1)} %refs_1_.14, bf16[2,4,256,256]{3,2,1,0:T(8,128)(2,1)S(1)} %copy-done.6, bf16[4,2,256,256]{3,2,1,0:T(8,128)(2,1)S(1)} %copy-done), custom_call_target="tpu_custom_call" | custom-call | flops 1342177280 | bytes 6295584 | tf_op jit(solution)/shard_map/pallas_call | solution.py:421
  23.4 1.5 %collective-permute-done.19.refs_6_ = bf16[1,256,256]{2,1,0:T(8,128)(2,1)S(1)} collective-permute-done((bf16[1,256,256]{2,1,0:T(8,128)(2,1)S(1)}, bf16[1,256,256]{2,1,0:T(8,128)(2,1)S(1)}, u32[]{:S(2)}, u32[]{:S(2)}) %collective-permute-start.19) | collective-permute-done | bytes 131104 | tf_op jit(solution)/shard_map/ppermute | solution.py:405
  24.9 3.0 %collective-permute-done.22.refs_9_ = bf16[1,256,256]{2,1,0:T(8,128)(2,1)S(1)} collective-permute-done((bf16[1,256,256]{2,1,0:T(8,128)(2,1)S(1)}, bf16[1,256,256]{2,1,0:T(8,128)(2,1)S(1)}, u32[]{:S(2)}, u32[]{:S(2)}) %collective-permute-start.22) | collective-permute-done | bytes 131104 | tf_op jit(solution)/shard_map/ppermute | solution.py:405
  27.9 0.0 collective-permute-done.20.refs_7_
  27.9 2.1 %collective-permute-done.21.refs_8_ = bf16[2,256,256]{2,1,0:T(8,128)(2,1)S(1)} collective-permute-done((bf16[2,256,256]{2,1,0:T(8,128)(2,1)S(1)}, bf16[2,256,256]{2,1,0:T(8,128)(2,1)S(1)}, u32[]{:S(2)}, u32[]{:S(2)}) %collective-permute-start.21) | collective-permute-done | bytes 262176 | tf_op jit(solution)/shard_map/ppermute | solution.py:405
  30.0 0.0 collective-permute-done.18.refs_4_
  30.0 0.0 copy-done.4
  30.0 1.7 %shard_map.83 = (bf16[8,256,256]{2,1,0:T(8,128)(2,1)S(1)}, bf16[2,256,256]{2,1,0:T(8,128)(2,1)S(1)}, bf16[2,256,256]{2,1,0:T(8,128)(2,1)S(1)}, bf16[2,256,256]{2,1,0:T(8,128)(2,1)S(1)}, bf16[2,256,256]{2,1,0:T(8,128)(2,1)S(1)}) custom-call(f32[2,4]{1,0:T(2,128)S(1)} %bitcast.186, bf16[4,4,256,256]{3,2,1,0:T(8,128)(2,1)S(1)} %copy-done.4, ...), custom_call_target="tpu_custom_call" | custom-call | flops 805306368 | bytes 10117152 | tf_op jit(solution)/shard_map/pallas_call | solution.py:421
  31.7 5.0 %collective-permute-start.23 = (bf16[2,256,256]{2,1,0:T(8,128)(2,1)S(1)}, bf16[2,256,256]{2,1,0:T(8,128)(2,1)S(1)}, u32[]{:S(2)}, u32[]{:S(2)}) collective-permute-start(bf16[2,256,256]{2,1,0:T(8,128)(2,1)S(1)} %get-tuple-element.61), channel_id=1, source_target_pairs={{0,63},{1,32},{2,33},{3,34},{4,35},{5,36},{6,37},{7,38},{8,39},{9,... | collective-permute-start | bytes 786440 | tf_op jit(solution)/shard_map/ppermute | solution.py:405
  36.7 1.3 %collective-permute-start.24 = (bf16[2,256,256]{2,1,0:T(8,128)(2,1)S(1)}, bf16[2,256,256]{2,1,0:T(8,128)(2,1)S(1)}, u32[]{:S(2)}, u32[]{:S(2)}) collective-permute-start(bf16[2,256,256]{2,1,0:T(8,128)(2,1)S(1)} %get-tuple-element.62), channel_id=1, source_target_pairs={{32,1},{33,2},{34,3},{35,4},{36,5},{37,6},{38,7},{39,8},{40,9},{41... | collective-permute-start | bytes 786440 | tf_op jit(solution)/shard_map/ppermute | solution.py:405
  38.0 0.1 collective-permute-start.25
  38.1 4.2 %collective-permute-start.26 = (bf16[2,256,256]{2,1,0:T(8,128)(2,1)S(1)}, bf16[2,256,256]{2,1,0:T(8,128)(2,1)S(1)}, u32[]{:S(2)}, u32[]{:S(2)}) collective-permute-start(bf16[2,256,256]{2,1,0:T(8,128)(2,1)S(1)} %get-tuple-element.64), channel_id=1, source_target_pairs={{1,2},{2,1},{3,4},{4,3},{5,6},{6,5},{7,8},{8,7},{9,10},{10,9},{11,... | collective-permute-start | bytes 786440 | tf_op jit(solution)/shard_map/ppermute | solution.py:415
  42.3 2.5 %shard_map.84 = (f32[8,256,256]{2,1,0:T(8,128)S(1)}, f32[8,128]{1,0:T(8,128)S(1)}) custom-call(f32[2,4]{1,0:T(2,128)S(1)} %bitcast.187, bf16[4,4,256,256]{3,2,1,0:T(8,128)(2,1)S(1)} %copy-done.4, bf16[2,4,256,256]{3,2,1,0:T(8,128)(2,1)S(1)} %copy-done.6, bf16[4,2,256,256]{3,2,1,0:T(8,128)(2,1)S(1)} %copy-done, ...), custom_call_target="tpu_custom_call" | custom-call | flops 1610612736 | bytes 8290336 | tf_op jit(solution)/shard_map/pallas_call | solution.py:421
  44.8 0.0 collective-permute-done.23.refs_7_
  44.8 3.9 %collective-permute-done.24.refs_8_ = bf16[2,256,256]{2,1,0:T(8,128)(2,1)S(1)} collective-permute-done((bf16[2,256,256]{2,1,0:T(8,128)(2,1)S(1)}, bf16[2,256,256]{2,1,0:T(8,128)(2,1)S(1)}, u32[]{:S(2)}, u32[]{:S(2)}) %collective-permute-start.24) | collective-permute-done | bytes 262176 | tf_op jit(solution)/shard_map/ppermute | solution.py:405
  48.7 0.0 collective-permute-done.25.refs_9_
  48.7 0.2 collective-permute-done.26.refs_10_
  48.9 1.4 %shard_map.85 = (bf16[8,256,256]{2,1,0:T(8,128)(2,1)S(1)}, bf16[2,256,256]{2,1,0:T(8,128)(2,1)S(1)}, bf16[2,256,256]{2,1,0:T(8,128)(2,1)S(1)}, bf16[2,256,256]{2,1,0:T(8,128)(2,1)S(1)}, bf16[2,256,256]{2,1,0:T(8,128)(2,1)S(1)}) custom-call(f32[2,4]{1,0:T(2,128)S(1)} %bitcast.188, bf16[4,4,256,256]{3,2,1,0:T(8,128)(2,1)S(1)} %copy-done.4, ...), custom_call_target="tpu_custom_call" | custom-call | flops 536870912 | bytes 11427872 | tf_op jit(solution)/shard_map/pallas_call | solution.py:421
  50.3 3.3 %collective-permute-start.27 = (bf16[2,256,256]{2,1,0:T(8,128)(2,1)S(1)}, bf16[2,256,256]{2,1,0:T(8,128)(2,1)S(1)}, u32[]{:S(2)}, u32[]{:S(2)}) collective-permute-start(bf16[2,256,256]{2,1,0:T(8,128)(2,1)S(1)} %get-tuple-element.68), channel_id=1, source_target_pairs={{0,63},{1,32},{2,33},{3,34},{4,35},{5,36},{6,37},{7,38},{8,39},{9,... | collective-permute-start | bytes 786440 | tf_op jit(solution)/shard_map/ppermute | solution.py:405
  53.6 1.3 %collective-permute-start.28 = (bf16[2,256,256]{2,1,0:T(8,128)(2,1)S(1)}, bf16[2,256,256]{2,1,0:T(8,128)(2,1)S(1)}, u32[]{:S(2)}, u32[]{:S(2)}) collective-permute-start(bf16[2,256,256]{2,1,0:T(8,128)(2,1)S(1)} %get-tuple-element.69), channel_id=1, source_target_pairs={{32,1},{33,2},{34,3},{35,4},{36,5},{37,6},{38,7},{39,8},{40,9},{41... | collective-permute-start | bytes 786440 | tf_op jit(solution)/shard_map/ppermute | solution.py:405
  54.9 4.4 %collective-permute-start.29 = (bf16[2,256,256]{2,1,0:T(8,128)(2,1)S(1)}, bf16[2,256,256]{2,1,0:T(8,128)(2,1)S(1)}, u32[]{:S(2)}, u32[]{:S(2)}) collective-permute-start(bf16[2,256,256]{2,1,0:T(8,128)(2,1)S(1)} %get-tuple-element.70), channel_id=1, source_target_pairs={{0,1},{1,0},{2,3},{3,2},{4,5},{5,4},{6,7},{7,6},{8,9},{9,8},{10,11... | collective-permute-start | bytes 786440 | tf_op jit(solution)/shard_map/ppermute | solution.py:415
  59.3 2.2 %collective-permute-start.30 = (bf16[2,256,256]{2,1,0:T(8,128)(2,1)S(1)}, bf16[2,256,256]{2,1,0:T(8,128)(2,1)S(1)}, u32[]{:S(2)}, u32[]{:S(2)}) collective-permute-start(bf16[2,256,256]{2,1,0:T(8,128)(2,1)S(1)} %get-tuple-element.71), channel_id=1, source_target_pairs={{1,2},{2,1},{3,4},{4,3},{5,6},{6,5},{7,8},{8,7},{9,10},{10,9},{11,... | collective-permute-start | bytes 786440 | tf_op jit(solution)/shard_map/ppermute | solution.py:415
  61.5 2.5 %shard_map.86 = (f32[8,256,256]{2,1,0:T(8,128)S(1)}, f32[8,128]{1,0:T(8,128)S(1)}) custom-call(f32[2,4]{1,0:T(2,128)S(1)} %bitcast.189, bf16[4,4,256,256]{3,2,1,0:T(8,128)(2,1)S(1)} %copy-done.4, bf16[2,4,256,256]{3,2,1,0:T(8,128)(2,1)S(1)} %copy-done.6, bf16[4,2,256,256]{3,2,1,0:T(8,128)(2,1)S(1)} %copy-done, ...), custom_call_target="tpu_custom_call" | custom-call | flops 1610612736 | bytes 9338912 | tf_op jit(solution)/shard_map/pallas_call | solution.py:421
  64.0 0.0 collective-permute-done.27.refs_9_
  64.0 0.0 collective-permute-done.28.refs_10_
  64.1 0.0 collective-permute-done.29.refs_11_
  64.1 4.7 %collective-permute-done.30.refs_12_ = bf16[2,256,256]{2,1,0:T(8,128)(2,1)S(1)} collective-permute-done((bf16[2,256,256]{2,1,0:T(8,128)(2,1)S(1)}, bf16[2,256,256]{2,1,0:T(8,128)(2,1)S(1)}, u32[]{:S(2)}, u32[]{:S(2)}) %collective-permute-start.30) | collective-permute-done | bytes 262176 | tf_op jit(solution)/shard_map/ppermute | solution.py:415
  68.7 0.0 copy-start.14
  68.7 0.0 copy-start.15
  68.7 2.8 %shard_map.87 = (bf16[8,256,256]{2,1,0:T(8,128)(2,1)S(1)}, bf16[3,256,256]{2,1,0:T(8,128)(2,1)}, f32[256,128]{1,0:T(8,128)}) custom-call(f32[2,4]{1,0:T(2,128)S(1)} %bitcast.190, bf16[4,4,256,256]{3,2,1,0:T(8,128)(2,1)S(1)} %copy-done.4, bf16[2,4,256,256]{3,2,1,0:T(8,128)(2,1)S(1)} %copy-done.6, bf16[4,2,256,256]{3,2,1,0:T(8,128)(2,1)S(1)} %copy-done, ...), custom_call_target="tpu_custom_call" | custom-call | flops 536870912 | bytes 11956256 | tf_op jit(solution)/shard_map/pallas_call | solution.py:421
  71.6 0.2 collective-permute-start.31
  71.8 19.3 %all-to-all-start = ((f32[256,1,128]{2,1,0:T(1,128)}), f32[256,1,128]{2,1,0:T(1,128)S(1)}, u32[]{:S(2)}, u32[]{:S(2)}) async-start(f32[256,1,128]{2,1,0:T(1,128)} %bitcast.55), calls=%async_computation | async-start | bytes 262144 | tf_op jit(solution)/shard_map/all_to_all | solution.py:483
  91.1 12.9 %all-to-all-done = f32[256,1,128]{2,1,0:T(1,128)S(1)} async-done(((f32[256,1,128]{2,1,0:T(1,128)}), f32[256,1,128]{2,1,0:T(1,128)S(1)}, u32[]{:S(2)}, u32[]{:S(2)}) %all-to-all-start) | async-done | bytes 131104 | tf_op jit(solution)/shard_map/all_to_all | solution.py:483
  104.0 0.0 collective-permute-done.31.refs_7_
  104.0 0.0 copy-done.14
  104.0 0.0 copy-done.15
  104.0 0.0 copy-start.1
  104.0 3.7 %shard_map.88 = (bf16[4,2,256,256]{3,2,1,0:T(8,128)(2,1)}, f32[3]{0:T(128)S(1)}, f32[1]{0:T(128)}) custom-call(s32[2]{0:T(128)S(1)} %copy-done.14, s32[2]{0:T(128)S(1)} %copy-done.15, f32[256,128]{1,0:T(8,128)S(1)} %bitcast.183, bf16[4,2,256,256]{3,2,1,0:T(8,128)(2,1)} %refs_3_.13, bf16[8,256,256]{2,1,0:T(8,128)(2,1)S(1)} %get-tuple-element.58.refs_6_.refs_7_.refs_4_, ...), custom_call_target="tpu_custom_call" | custom-call | bytes 5767200 | tf_op jit(solution)/shard_map/pallas_call | solution.py:421
  108.3 0.0 copy-done.1
  108.3 0.2 conditional.1
  108.6 0.0 copy-start.16
  108.6 0.5 copy-done.16
Async XLA Ops:
  0.6 19.5 %copy-start = (bf16[4,2,256,256]{3,2,1,0:T(8,128)(2,1)S(1)}, bf16[4,2,256,256]{3,2,1,0:T(8,128)(2,1)}, u32[]{:S(2)}) copy-start(bf16[4,2,256,256]{3,2,1,0:T(8,128)(2,1)} %refs_3_.13) | copy-start | bytes 3145732
  0.6 19.4 %copy-start.6 = (bf16[2,4,256,256]{3,2,1,0:T(8,128)(2,1)S(1)}, bf16[2,4,256,256]{3,2,1,0:T(8,128)(2,1)}, u32[]{:S(2)}) copy-start(bf16[2,4,256,256]{3,2,1,0:T(8,128)(2,1)} %refs_2_.11) | copy-start | bytes 3145732
  0.7 19.4 %copy-start.13 = (f32[4,2]{0,1:T(2,128)S(1)}, f32[4,2]{0,1:T(2,128)}, u32[]{:S(2)}) copy-start(f32[4,2]{0,1:T(2,128)} %param.11) | copy-start | bytes 100
  3.1 26.9 %collective-permute-start.18 = (bf16[1840,256]{1,0:T(8,128)(2,1)S(1)}, bf16[1840,256]{1,0:T(8,128)(2,1)S(1)}, u32[]{:S(2)}, u32[]{:S(2)}) collective-permute-start(bf16[1840,256]{1,0:T(8,128)(2,1)S(1)} %get-tuple-element.51), channel_id=1, source_target_pairs={{0,1},{1,2},{2,3},{3,4},{4,5},{5,6},{6,7},{7,8},{8,9},{9,10},{10,1... | collective-permute-start | bytes 2826248 | tf_op jit(solution)/shard_map/ppermute | solution.py:405
  5.8 22.1 %collective-permute-start.20 = (bf16[2,256,256]{2,1,0:T(8,128)(2,1)S(1)}, bf16[2,256,256]{2,1,0:T(8,128)(2,1)S(1)}, u32[]{:S(2)}, u32[]{:S(2)}) collective-permute-start(bf16[2,256,256]{2,1,0:T(8,128)(2,1)S(1)} %get-tuple-element.55), channel_id=1, source_target_pairs={{32,1},{33,2},{34,3},{35,4},{36,5},{37,6},{38,7},{39,8},{40,9},{41... | collective-permute-start | bytes 786440 | tf_op jit(solution)/shard_map/ppermute | solution.py:405
  7.1 22.8 %collective-permute-start.21 = (bf16[2,256,256]{2,1,0:T(8,128)(2,1)S(1)}, bf16[2,256,256]{2,1,0:T(8,128)(2,1)S(1)}, u32[]{:S(2)}, u32[]{:S(2)}) collective-permute-start(bf16[2,256,256]{2,1,0:T(8,128)(2,1)S(1)} %get-tuple-element.56), channel_id=1, source_target_pairs={{1,0},{2,1},{3,2},{4,3},{5,4},{6,5},{7,6},{8,7},{9,8},{10,9},{11,1... | collective-permute-start | bytes 786440 | tf_op jit(solution)/shard_map/ppermute | solution.py:405
  9.6 15.2 %collective-permute-start.19 = (bf16[1,256,256]{2,1,0:T(8,128)(2,1)S(1)}, bf16[1,256,256]{2,1,0:T(8,128)(2,1)S(1)}, u32[]{:S(2)}, u32[]{:S(2)}) collective-permute-start(bf16[1,256,256]{2,1,0:T(8,128)(2,1)S(1)} %get-tuple-element.54), channel_id=1, source_target_pairs={{0,32},{1,33},{2,34},{3,35},{4,36},{5,37},{6,38},{7,39},{8,40},{9,... | collective-permute-start | bytes 393224 | tf_op jit(solution)/shard_map/ppermute | solution.py:405
  14.9 15.0 %copy-start.4 = (bf16[4,4,256,256]{3,2,1,0:T(8,128)(2,1)S(1)}, bf16[4,4,256,256]{3,2,1,0:T(8,128)(2,1)}, u32[]{:S(2)}) copy-start(bf16[4,4,256,256]{3,2,1,0:T(8,128)(2,1)} %refs_1_.14) | copy-start | bytes 6291460
  15.0 12.9 %collective-permute-start.22 = (bf16[1,256,256]{2,1,0:T(8,128)(2,1)S(1)}, bf16[1,256,256]{2,1,0:T(8,128)(2,1)S(1)}, u32[]{:S(2)}, u32[]{:S(2)}) collective-permute-start(bf16[1,256,256]{2,1,0:T(8,128)(2,1)S(1)} %get-tuple-element.57), channel_id=1, source_target_pairs={{1,32},{2,33},{3,34},{4,35},{5,36},{6,37},{7,38},{8,39},{9,40},{10... | collective-permute-start | bytes 393224 | tf_op jit(solution)/shard_map/ppermute | solution.py:405
  31.7 13.2 %collective-permute-start.23 = (bf16[2,256,256]{2,1,0:T(8,128)(2,1)S(1)}, bf16[2,256,256]{2,1,0:T(8,128)(2,1)S(1)}, u32[]{:S(2)}, u32[]{:S(2)}) collective-permute-start(bf16[2,256,256]{2,1,0:T(8,128)(2,1)S(1)} %get-tuple-element.61), channel_id=1, source_target_pairs={{0,63},{1,32},{2,33},{3,34},{4,35},{5,36},{6,37},{7,38},{8,39},{9,... | collective-permute-start | bytes 786440 | tf_op jit(solution)/shard_map/ppermute | solution.py:405
  36.7 12.0 %collective-permute-start.24 = (bf16[2,256,256]{2,1,0:T(8,128)(2,1)S(1)}, bf16[2,256,256]{2,1,0:T(8,128)(2,1)S(1)}, u32[]{:S(2)}, u32[]{:S(2)}) collective-permute-start(bf16[2,256,256]{2,1,0:T(8,128)(2,1)S(1)} %get-tuple-element.62), channel_id=1, source_target_pairs={{32,1},{33,2},{34,3},{35,4},{36,5},{37,6},{38,7},{39,8},{40,9},{41... | collective-permute-start | bytes 786440 | tf_op jit(solution)/shard_map/ppermute | solution.py:405
  38.0 10.7 %collective-permute-start.25 = (bf16[2,256,256]{2,1,0:T(8,128)(2,1)S(1)}, bf16[2,256,256]{2,1,0:T(8,128)(2,1)S(1)}, u32[]{:S(2)}, u32[]{:S(2)}) collective-permute-start(bf16[2,256,256]{2,1,0:T(8,128)(2,1)S(1)} %get-tuple-element.63), channel_id=1, source_target_pairs={{0,1},{1,0},{2,3},{3,2},{4,5},{5,4},{6,7},{7,6},{8,9},{9,8},{10,11... | collective-permute-start | bytes 786440 | tf_op jit(solution)/shard_map/ppermute | solution.py:415
  38.1 10.8 %collective-permute-start.26 = (bf16[2,256,256]{2,1,0:T(8,128)(2,1)S(1)}, bf16[2,256,256]{2,1,0:T(8,128)(2,1)S(1)}, u32[]{:S(2)}, u32[]{:S(2)}) collective-permute-start(bf16[2,256,256]{2,1,0:T(8,128)(2,1)S(1)} %get-tuple-element.64), channel_id=1, source_target_pairs={{1,2},{2,1},{3,4},{4,3},{5,6},{6,5},{7,8},{8,7},{9,10},{10,9},{11,... | collective-permute-start | bytes 786440 | tf_op jit(solution)/shard_map/ppermute | solution.py:415
  50.3 13.7 %collective-permute-start.27 = (bf16[2,256,256]{2,1,0:T(8,128)(2,1)S(1)}, bf16[2,256,256]{2,1,0:T(8,128)(2,1)S(1)}, u32[]{:S(2)}, u32[]{:S(2)}) collective-permute-start(bf16[2,256,256]{2,1,0:T(8,128)(2,1)S(1)} %get-tuple-element.68), channel_id=1, source_target_pairs={{0,63},{1,32},{2,33},{3,34},{4,35},{5,36},{6,37},{7,38},{8,39},{9,... | collective-permute-start | bytes 786440 | tf_op jit(solution)/shard_map/ppermute | solution.py:405
  53.6 10.5 %collective-permute-start.28 = (bf16[2,256,256]{2,1,0:T(8,128)(2,1)S(1)}, bf16[2,256,256]{2,1,0:T(8,128)(2,1)S(1)}, u32[]{:S(2)}, u32[]{:S(2)}) collective-permute-start(bf16[2,256,256]{2,1,0:T(8,128)(2,1)S(1)} %get-tuple-element.69), channel_id=1, source_target_pairs={{32,1},{33,2},{34,3},{35,4},{36,5},{37,6},{38,7},{39,8},{40,9},{41... | collective-permute-start | bytes 786440 | tf_op jit(solution)/shard_map/ppermute | solution.py:405
  54.9 9.2 %collective-permute-start.29 = (bf16[2,256,256]{2,1,0:T(8,128)(2,1)S(1)}, bf16[2,256,256]{2,1,0:T(8,128)(2,1)S(1)}, u32[]{:S(2)}, u32[]{:S(2)}) collective-permute-start(bf16[2,256,256]{2,1,0:T(8,128)(2,1)S(1)} %get-tuple-element.70), channel_id=1, source_target_pairs={{0,1},{1,0},{2,3},{3,2},{4,5},{5,4},{6,7},{7,6},{8,9},{9,8},{10,11... | collective-permute-start | bytes 786440 | tf_op jit(solution)/shard_map/ppermute | solution.py:415
  59.3 9.4 %collective-permute-start.30 = (bf16[2,256,256]{2,1,0:T(8,128)(2,1)S(1)}, bf16[2,256,256]{2,1,0:T(8,128)(2,1)S(1)}, u32[]{:S(2)}, u32[]{:S(2)}) collective-permute-start(bf16[2,256,256]{2,1,0:T(8,128)(2,1)S(1)} %get-tuple-element.71), channel_id=1, source_target_pairs={{1,2},{2,1},{3,4},{4,3},{5,6},{6,5},{7,8},{8,7},{9,10},{10,9},{11,... | collective-permute-start | bytes 786440 | tf_op jit(solution)/shard_map/ppermute | solution.py:415
  68.7 35.3 %copy-start.14 = (s32[2]{0:T(128)S(1)}, s32[2]{0:T(128)}, u32[]{:S(2)}) copy-start(s32[2]{0:T(128)} %refs_0_.3) | copy-start | bytes 28
  68.7 35.3 %copy-start.15 = (s32[2]{0:T(128)S(1)}, s32[2]{0:T(128)}, u32[]{:S(2)}) copy-start(s32[2]{0:T(128)} %refs_1_.15) | copy-start | bytes 28
  71.6 32.5 %collective-permute-start.31 = (bf16[3,256,256]{2,1,0:T(8,128)(2,1)}, bf16[3,256,256]{2,1,0:T(8,128)(2,1)}, u32[]{:S(2)}, u32[]{:S(2)}) collective-permute-start(bf16[3,256,256]{2,1,0:T(8,128)(2,1)} %get-tuple-element.74), channel_id=1, source_target_pairs={{0,31},{1,0},{2,1},{3,2},{4,3},{5,4},{6,5},{7,6},{8,7},{9,8},{10,9... | collective-permute-start | bytes 1179656 | tf_op jit(solution)/shard_map/ppermute | solution.py:405
  71.8 32.2 %all-to-all-start = ((f32[256,1,128]{2,1,0:T(1,128)}), f32[256,1,128]{2,1,0:T(1,128)S(1)}, u32[]{:S(2)}, u32[]{:S(2)}) async-start(f32[256,1,128]{2,1,0:T(1,128)} %bitcast.55), calls=%async_computation | async-start | bytes 262144 | tf_op jit(solution)/shard_map/all_to_all | solution.py:483
  104.0 4.3 %copy-start.1 = (bf16[4,2,256,256]{3,2,1,0:T(8,128)(2,1)S(1)}, bf16[4,2,256,256]{3,2,1,0:T(8,128)(2,1)}, u32[]{:S(2)}) copy-start(bf16[4,2,256,256]{3,2,1,0:T(8,128)(2,1)} %refs_3_.13) | copy-start | bytes 3145732
  108.6 0.5 copy-start.16
